TPU v7x, 512 devices: a whole 4x8x8 slice. The times are simulated.
512 devices in a mesh: ep: 16 (over y_hi, x, core), blk: 32 (over z, y_lo).
Axes of the slice: x: 4, y: 8 (y_hi: 2, y_lo: 4; y = y_hi * 4 + y_lo), z: 8, core: 2. Of those that a mesh axis runs over, the one named last changes fastest.
Arguments:
- vertex: float32 [524288, 128], P(('ep', 'blk')), parts along dimension 0, may hold values from -2.4 to 2.4
- context: float32 [524288, 128], P(('ep', 'blk')), parts along dimension 0, may hold values from -2.4 to 2.4
- tile_ids: int32 [512, 8, 2], P(('ep', 'blk')), parts along dimension 0, may hold values from 0 to 63, as said below
- live_tiles: int32 [512, 8], P(('ep', 'blk')), parts along dimension 0, may hold values from 1 to 2, as said below
- pos_counts: int32 [512, 8, 2, 128, 128], P(('ep', 'blk')), parts along dimension 0, may hold values from 0 to 3, as said below
- neg_counts: int32 [512, 8, 2, 128, 128], P(('ep', 'blk')), parts along dimension 0, may hold values from 0 to 5, as said below
Outputs:
- new_vertex: float32 [524288, 128], P(('ep', 'blk')), parts along dimension 0
- new_context: float32 [524288, 128], P(('ep', 'blk')), parts along dimension 0
There are 16 independent parts, one for each index of `ep`. A program takes and returns all parts, laid end to end along the dimension named above; each array names one. Nothing has to cross between parts.
Inputs may be any that keep to these rules, and one draw needn't show every extreme that they name: `tile_ids`: for each slice and offset the 2 entries are distinct tile pairs of 0 to 63. `live_tiles`: at every offset some slice has all 2 slots live. `pos_counts`: slots at or above live_tiles hold zeros. `neg_counts`: slots at or above live_tiles hold zeros.
All inputs are finite; a program needn't handle non-finite values.
Results may differ from a plain program's by a relative error of at most 0.0003.
Values sent between devices are 32-bit elements; how exact they have to be, the bound alone decides.
No kernel may reach another device: no remote copies, remote signals or barrier semaphores. Data moves between devices by JAX's collectives and lax.ppermute only.
A program may use at most 64 MiB of HBM per device.

v0:
```python
import jax
import jax.numpy as jnp
from jax import lax
from jax.sharding import PartitionSpec as P

RATES = (0.02, 0.01)


def shifted(block, axis, distance):
    devices = range(lax.axis_size(axis))
    route = [((i - distance) % len(devices), i) for i in devices]
    return lax.ppermute(block, axis, route)


def device_terms(vert, ctx, ids, live, pos, neg):
    tile = pos.shape[-1]
    width = vert.shape[1]
    row_tiles = vert.shape[0] // tile
    slots = ids.shape[0]
    vert_tiles = vert.reshape(row_tiles, tile, width)
    ctx_tiles = ctx.reshape(row_tiles, tile, width)
    which = jnp.arange(row_tiles, dtype=jnp.int32)
    rows_pick = (ids[:, None] // row_tiles == which[None, :]).astype(jnp.float32)
    cols_pick = (ids[:, None] % row_tiles == which[None, :]).astype(jnp.float32)
    high = lax.Precision.HIGHEST
    left = jnp.einsum("sr,rad->sad", rows_pick, vert_tiles, precision=high)
    right = jnp.einsum("sr,rad->sad", cols_pick, ctx_tiles, precision=high)
    score = jnp.einsum("sad,sbd->sab", left, right, precision=high)
    sig = jax.nn.sigmoid(score)
    mask = (jnp.arange(slots, dtype=jnp.int32) < live).astype(jnp.float32)
    grad = neg.astype(jnp.float32) * sig - pos.astype(jnp.float32) * (1.0 - sig)
    grad = grad * mask[:, None, None]
    grad_left = jnp.einsum("sab,sbd->sad", grad, right, precision=high)
    grad_right = jnp.einsum("sab,sad->sbd", grad, left, precision=high)
    vert_grad = jnp.einsum("sr,sad->rad", rows_pick, grad_left, precision=high)
    ctx_grad = jnp.einsum("sr,sad->rad", cols_pick, grad_right, precision=high)
    return (vert_grad.reshape(vert.shape), ctx_grad.reshape(ctx.shape))


def offset_terms(vert, ctx, ids, live, pos, neg):
    return device_terms(vert, ctx, ids, live, pos, neg)


def per_device(vertex, context, tile_ids, live_tiles, pos_counts, neg_counts):
    sub_steps = lax.axis_size("blk") // 8
    vert = vertex
    owned = context
    carried = context
    for epoch in range(2):
        vert_acc = jnp.zeros_like(vert)
        ctx_acc = jnp.zeros_like(carried)
        for inner in range(sub_steps):
            offset = epoch * sub_steps + inner
            vert_grad, ctx_grad = offset_terms(
                vert,
                carried,
                tile_ids[0, offset],
                live_tiles[0, offset],
                pos_counts[0, offset],
                neg_counts[0, offset],
            )
            vert_acc = vert_acc + vert_grad
            ctx_acc = ctx_acc + ctx_grad
            carried, ctx_acc = shifted((carried, ctx_acc), "blk", 1)
        vert = vert - RATES[epoch] * vert_acc
        returned = shifted(ctx_acc, "blk", -(epoch + 1) * sub_steps)
        owned = owned - RATES[epoch] * returned
        if epoch == 0:
            carried = shifted(owned, "blk", sub_steps)
    return (vert, owned)


def solution(mesh):
    placed = (
        P(("ep", "blk"), None),
        P(("ep", "blk"), None),
        P(("ep", "blk"), None, None),
        P(("ep", "blk"), None),
        P(("ep", "blk"), None, None, None, None),
        P(("ep", "blk"), None, None, None, None),
    )
    return jax.shard_map(
        per_device,
        mesh=mesh,
        in_specs=placed,
        out_specs=(P(("ep", "blk"), None), P(("ep", "blk"), None)),
        check_vma=False,
    )
```

profile of v0, /device:TPU:66, one launch (start us, length us, event | category | flops | bytes accessed | tf_op | source)
XLA Modules:
  0.0 236.7 jit_solution(4186293236676729481)
XLA Ops:
  0.6 3.6 %collective-permute-start = (f32[1024,128]{1,0:T(8,128)}, f32[1024,128]{1,0:T(8,128)S(1)}, u32[]{:S(2)}, u32[]{:S(2)}) collective-permute-start(f32[1024,128]{1,0:T(8,128)} %param.7), channel_id=1, source_target_pairs={{31,0},{0,1},{1,2},{2,3},{3,4},{4,5},{5,6},{6,7},{7,8},{8,9},{9,10... | collective-permute-start | bytes 1572872 | tf_op jit(solution)/shard_map/ppermute | solution.py:12
  12.6 3.5 %collective-permute-start.3 = (f32[1024,128]{1,0:T(8,128)S(1)}, f32[1024,128]{1,0:T(8,128)S(1)}, u32[]{:S(2)}, u32[]{:S(2)}) collective-permute-start(f32[1024,128]{1,0:T(8,128)S(1)} %bitcast.222), channel_id=1, source_target_pairs={{31,0},{0,1},{1,2},{2,3},{3,4},{4,5},{5,6},{6,7},{7,8},{8,9},{9,10... | collective-permute-start | bytes 1572872 | tf_op jit(solution)/shard_map/ppermute | solution.py:12
  25.9 3.5 %collective-permute-start.1 = (f32[1024,128]{1,0:T(8,128)S(1)}, f32[1024,128]{1,0:T(8,128)S(1)}, u32[]{:S(2)}, u32[]{:S(2)}) collective-permute-start(f32[1024,128]{1,0:T(8,128)S(1)} %collective-permute-done), channel_id=1, source_target_pairs={{31,0},{0,1},{1,2},{2,3},{3,4},{4,5},{5,6},{6,7},{7,8},{8,9},{9,10... | collective-permute-start | bytes 1572872 | tf_op jit(solution)/shard_map/ppermute | solution.py:12
  30.7 2.7 %collective-permute-start.4 = (f32[1024,128]{1,0:T(8,128)S(1)}, f32[1024,128]{1,0:T(8,128)S(1)}, u32[]{:S(2)}, u32[]{:S(2)}) collective-permute-start(f32[1024,128]{1,0:T(8,128)S(1)} %bitcast_add_fusion.5), channel_id=1, source_target_pairs={{31,0},{0,1},{1,2},{2,3},{3,4},{4,5},{5,6},{6,7},{7,8},{8,9},{9,10... | collective-permute-start | bytes 1572872 | tf_op jit(solution)/shard_map/ppermute | solution.py:12
  34.2 11.1 %collective-permute-done.1 = f32[1024,128]{1,0:T(8,128)S(1)} collective-permute-done((f32[1024,128]{1,0:T(8,128)S(1)}, f32[1024,128]{1,0:T(8,128)S(1)}, u32[]{:S(2)}, u32[]{:S(2)}) %collective-permute-start.1) | collective-permute-done | bytes 524320 | tf_op jit(solution)/shard_map/ppermute | solution.py:12
  46.4 1.9 collective-permute-start.2
  49.4 7.2 %collective-permute-done.4 = f32[1024,128]{1,0:T(8,128)S(1)} collective-permute-done((f32[1024,128]{1,0:T(8,128)S(1)}, f32[1024,128]{1,0:T(8,128)S(1)}, u32[]{:S(2)}, u32[]{:S(2)}) %collective-permute-start.4) | collective-permute-done | bytes 524320 | tf_op jit(solution)/shard_map/ppermute | solution.py:12
  56.6 2.1 collective-permute-start.5
  58.7 9.1 %collective-permute-done.2 = f32[1024,128]{1,0:T(8,128)S(1)} collective-permute-done((f32[1024,128]{1,0:T(8,128)S(1)}, f32[1024,128]{1,0:T(8,128)S(1)}, u32[]{:S(2)}, u32[]{:S(2)}) %collective-permute-start.2) | collective-permute-done | bytes 524320 | tf_op jit(solution)/shard_map/ppermute | solution.py:12
  69.9 7.3 %collective-permute-done.5 = f32[1024,128]{1,0:T(8,128)S(1)} collective-permute-done((f32[1024,128]{1,0:T(8,128)S(1)}, f32[1024,128]{1,0:T(8,128)S(1)}, u32[]{:S(2)}, u32[]{:S(2)}) %collective-permute-start.5) | collective-permute-done | bytes 524320 | tf_op jit(solution)/shard_map/ppermute | solution.py:12
  77.3 1.9 collective-permute-start.6
  80.3 13.8 %collective-permute-done.6 = f32[1024,128]{1,0:T(8,128)S(1)} collective-permute-done((f32[1024,128]{1,0:T(8,128)S(1)}, f32[1024,128]{1,0:T(8,128)S(1)}, u32[]{:S(2)}, u32[]{:S(2)}) %collective-permute-start.6) | collective-permute-done | bytes 524320 | tf_op jit(solution)/shard_map/ppermute | solution.py:12
  94.1 9.2 %collective-permute-start.7 = (f32[1024,128]{1,0:T(8,128)S(1)}, f32[1024,128]{1,0:T(8,128)S(1)}, u32[]{:S(2)}, u32[]{:S(2)}) collective-permute-start(f32[1024,128]{1,0:T(8,128)S(1)} %collective-permute-done.6), channel_id=1, source_target_pairs={{4,0},{5,1},{6,2},{7,3},{8,4},{9,5},{10,6},{11,7},{12,8},{13,9},{1... | collective-permute-start | bytes 1572872 | tf_op jit(solution)/shard_map/ppermute | solution.py:12
  104.6 7.9 %collective-permute-done.7 = f32[1024,128]{1,0:T(8,128)S(1)} collective-permute-done((f32[1024,128]{1,0:T(8,128)S(1)}, f32[1024,128]{1,0:T(8,128)S(1)}, u32[]{:S(2)}, u32[]{:S(2)}) %collective-permute-start.7) | collective-permute-done | bytes 524320 | tf_op jit(solution)/shard_map/ppermute | solution.py:12
  112.7 1.9 collective-permute-start.8
  116.6 9.6 %collective-permute-done.8 = f32[1024,128]{1,0:T(8,128)S(1)} collective-permute-done((f32[1024,128]{1,0:T(8,128)S(1)}, f32[1024,128]{1,0:T(8,128)S(1)}, u32[]{:S(2)}, u32[]{:S(2)}) %collective-permute-start.8) | collective-permute-done | bytes 524320 | tf_op jit(solution)/shard_map/ppermute | solution.py:12
  127.7 1.9 collective-permute-start.9
  130.3 1.9 collective-permute-start.12
  133.0 14.1 %collective-permute-done.9 = f32[1024,128]{1,0:T(8,128)S(1)} collective-permute-done((f32[1024,128]{1,0:T(8,128)S(1)}, f32[1024,128]{1,0:T(8,128)S(1)}, u32[]{:S(2)}, u32[]{:S(2)}) %collective-permute-start.9) | collective-permute-done | bytes 524320 | tf_op jit(solution)/shard_map/ppermute | solution.py:12
  148.3 1.9 collective-permute-start.10
  151.2 7.2 %collective-permute-done.12 = f32[1024,128]{1,0:T(8,128)S(1)} collective-permute-done((f32[1024,128]{1,0:T(8,128)S(1)}, f32[1024,128]{1,0:T(8,128)S(1)}, u32[]{:S(2)}, u32[]{:S(2)}) %collective-permute-start.12) | collective-permute-done | bytes 524320 | tf_op jit(solution)/shard_map/ppermute | solution.py:12
  158.5 2.1 collective-permute-start.13
  160.9 8.8 %collective-permute-done.10 = f32[1024,128]{1,0:T(8,128)S(1)} collective-permute-done((f32[1024,128]{1,0:T(8,128)S(1)}, f32[1024,128]{1,0:T(8,128)S(1)}, u32[]{:S(2)}, u32[]{:S(2)}) %collective-permute-start.10) | collective-permute-done | bytes 524320 | tf_op jit(solution)/shard_map/ppermute | solution.py:12
  170.8 1.9 collective-permute-start.11
  173.7 7.2 %collective-permute-done.13 = f32[1024,128]{1,0:T(8,128)S(1)} collective-permute-done((f32[1024,128]{1,0:T(8,128)S(1)}, f32[1024,128]{1,0:T(8,128)S(1)}, u32[]{:S(2)}, u32[]{:S(2)}) %collective-permute-start.13) | collective-permute-done | bytes 524320 | tf_op jit(solution)/shard_map/ppermute | solution.py:12
  180.9 1.9 collective-permute-start.14
  182.9 9.2 %collective-permute-done.11 = f32[1024,128]{1,0:T(8,128)S(1)} collective-permute-done((f32[1024,128]{1,0:T(8,128)S(1)}, f32[1024,128]{1,0:T(8,128)S(1)}, u32[]{:S(2)}, u32[]{:S(2)}) %collective-permute-start.11) | collective-permute-done | bytes 524320 | tf_op jit(solution)/shard_map/ppermute | solution.py:12
  194.3 4.5 %collective-permute-done.14 = f32[1024,128]{1,0:T(8,128)S(1)} collective-permute-done((f32[1024,128]{1,0:T(8,128)S(1)}, f32[1024,128]{1,0:T(8,128)S(1)}, u32[]{:S(2)}, u32[]{:S(2)}) %collective-permute-start.14) | collective-permute-done | bytes 524320 | tf_op jit(solution)/shard_map/ppermute | solution.py:12
  198.8 1.9 collective-permute-start.15
  202.1 10.7 %collective-permute-done.15 = f32[1024,128]{1,0:T(8,128)S(1)} collective-permute-done((f32[1024,128]{1,0:T(8,128)S(1)}, f32[1024,128]{1,0:T(8,128)S(1)}, u32[]{:S(2)}, u32[]{:S(2)}) %collective-permute-start.15) | collective-permute-done | bytes 524320 | tf_op jit(solution)/shard_map/ppermute | solution.py:12
  212.8 3.6 %collective-permute-start.16 = (f32[1024,128]{1,0:T(8,128)S(1)}, f32[1024,128]{1,0:T(8,128)S(1)}, u32[]{:S(2)}, u32[]{:S(2)}) collective-permute-start(f32[1024,128]{1,0:T(8,128)S(1)} %collective-permute-done.15), channel_id=1, source_target_pairs={{8,0},{9,1},{10,2},{11,3},{12,4},{13,5},{14,6},{15,7},{16,8},{17,9... | collective-permute-start | bytes 1572872 | tf_op jit(solution)/shard_map/ppermute | solution.py:12
  218.1 17.7 %collective-permute-done.16 = f32[1024,128]{1,0:T(8,128)S(1)} collective-permute-done((f32[1024,128]{1,0:T(8,128)S(1)}, f32[1024,128]{1,0:T(8,128)S(1)}, u32[]{:S(2)}, u32[]{:S(2)}) %collective-permute-start.16) | collective-permute-done | bytes 524320 | tf_op jit(solution)/shard_map/ppermute | solution.py:12
  (104 shorter events, 42.3 us)
Async XLA Ops:
  0.6 8.9 %copy-start = (f32[1024,128]{1,0:T(8,128)S(1)}, f32[1024,128]{1,0:T(8,128)}, u32[]{:S(2)}) copy-start(f32[1024,128]{1,0:T(8,128)} %param.6) | copy-start | bytes 1572868
  0.6 23.0 %collective-permute-start = (f32[1024,128]{1,0:T(8,128)}, f32[1024,128]{1,0:T(8,128)S(1)}, u32[]{:S(2)}, u32[]{:S(2)}) collective-permute-start(f32[1024,128]{1,0:T(8,128)} %param.7), channel_id=1, source_target_pairs={{31,0},{0,1},{1,2},{2,3},{3,4},{4,5},{5,6},{6,7},{7,8},{8,9},{9,10... | collective-permute-start | bytes 1572872 | tf_op jit(solution)/shard_map/ppermute | solution.py:12
  12.6 18.0 %collective-permute-start.3 = (f32[1024,128]{1,0:T(8,128)S(1)}, f32[1024,128]{1,0:T(8,128)S(1)}, u32[]{:S(2)}, u32[]{:S(2)}) collective-permute-start(f32[1024,128]{1,0:T(8,128)S(1)} %bitcast.222), channel_id=1, source_target_pairs={{31,0},{0,1},{1,2},{2,3},{3,4},{4,5},{5,6},{6,7},{7,8},{8,9},{9,10... | collective-permute-start | bytes 1572872 | tf_op jit(solution)/shard_map/ppermute | solution.py:12
  16.9 7.4 %copy-start.3 = (s32[1,8,2,128,128]{4,3,2,1,0:T(8,128)S(1)}, s32[1,8,2,128,128]{4,3,2,1,0:T(8,128)}, u32[]{:S(2)}) copy-start(s32[1,8,2,128,128]{4,3,2,1,0:T(8,128)} %param.11) | copy-start | bytes 3145732
  17.6 6.7 %copy-start.2 = (s32[1,8,2,128,128]{4,3,2,1,0:T(8,128)S(1)}, s32[1,8,2,128,128]{4,3,2,1,0:T(8,128)}, u32[]{:S(2)}) copy-start(s32[1,8,2,128,128]{4,3,2,1,0:T(8,128)} %param.10) | copy-start | bytes 3145732
  25.9 19.5 %collective-permute-start.1 = (f32[1024,128]{1,0:T(8,128)S(1)}, f32[1024,128]{1,0:T(8,128)S(1)}, u32[]{:S(2)}, u32[]{:S(2)}) collective-permute-start(f32[1024,128]{1,0:T(8,128)S(1)} %collective-permute-done), channel_id=1, source_target_pairs={{31,0},{0,1},{1,2},{2,3},{3,4},{4,5},{5,6},{6,7},{7,8},{8,9},{9,10... | collective-permute-start | bytes 1572872 | tf_op jit(solution)/shard_map/ppermute | solution.py:12
  30.7 25.9 %collective-permute-start.4 = (f32[1024,128]{1,0:T(8,128)S(1)}, f32[1024,128]{1,0:T(8,128)S(1)}, u32[]{:S(2)}, u32[]{:S(2)}) collective-permute-start(f32[1024,128]{1,0:T(8,128)S(1)} %bitcast_add_fusion.5), channel_id=1, source_target_pairs={{31,0},{0,1},{1,2},{2,3},{3,4},{4,5},{5,6},{6,7},{7,8},{8,9},{9,10... | collective-permute-start | bytes 1572872 | tf_op jit(solution)/shard_map/ppermute | solution.py:12
  46.4 21.4 %collective-permute-start.2 = (f32[1024,128]{1,0:T(8,128)S(1)}, f32[1024,128]{1,0:T(8,128)S(1)}, u32[]{:S(2)}, u32[]{:S(2)}) collective-permute-start(f32[1024,128]{1,0:T(8,128)S(1)} %collective-permute-done.1), channel_id=1, source_target_pairs={{31,0},{0,1},{1,2},{2,3},{3,4},{4,5},{5,6},{6,7},{7,8},{8,9},{9,10... | collective-permute-start | bytes 1572872 | tf_op jit(solution)/shard_map/ppermute | solution.py:12
  56.6 20.7 %collective-permute-start.5 = (f32[1024,128]{1,0:T(8,128)S(1)}, f32[1024,128]{1,0:T(8,128)S(1)}, u32[]{:S(2)}, u32[]{:S(2)}) collective-permute-start(f32[1024,128]{1,0:T(8,128)S(1)} %bitcast_add_fusion.4), channel_id=1, source_target_pairs={{31,0},{0,1},{1,2},{2,3},{3,4},{4,5},{5,6},{6,7},{7,8},{8,9},{9,10... | collective-permute-start | bytes 1572872 | tf_op jit(solution)/shard_map/ppermute | solution.py:12
  77.3 16.8 %collective-permute-start.6 = (f32[1024,128]{1,0:T(8,128)S(1)}, f32[1024,128]{1,0:T(8,128)S(1)}, u32[]{:S(2)}, u32[]{:S(2)}) collective-permute-start(f32[1024,128]{1,0:T(8,128)S(1)} %bitcast_add_fusion.3), channel_id=1, source_target_pairs={{31,0},{0,1},{1,2},{2,3},{3,4},{4,5},{5,6},{6,7},{7,8},{8,9},{9,10... | collective-permute-start | bytes 1572872 | tf_op jit(solution)/shard_map/ppermute | solution.py:12
  94.1 18.5 %collective-permute-start.7 = (f32[1024,128]{1,0:T(8,128)S(1)}, f32[1024,128]{1,0:T(8,128)S(1)}, u32[]{:S(2)}, u32[]{:S(2)}) collective-permute-start(f32[1024,128]{1,0:T(8,128)S(1)} %collective-permute-done.6), channel_id=1, source_target_pairs={{4,0},{5,1},{6,2},{7,3},{8,4},{9,5},{10,6},{11,7},{12,8},{13,9},{1... | collective-permute-start | bytes 1572872 | tf_op jit(solution)/shard_map/ppermute | solution.py:12
  104.0 8.6 %copy-start.1 = (f32[1024,128]{1,0:T(8,128)S(1)}, f32[1024,128]{1,0:T(8,128)}, u32[]{:S(2)}) copy-start(f32[1024,128]{1,0:T(8,128)} %param.7) | copy-start | bytes 1572868
  112.7 13.6 %collective-permute-start.8 = (f32[1024,128]{1,0:T(8,128)S(1)}, f32[1024,128]{1,0:T(8,128)S(1)}, u32[]{:S(2)}, u32[]{:S(2)}) collective-permute-start(f32[1024,128]{1,0:T(8,128)S(1)} %multiply_subtract_fusion.1), channel_id=1, source_target_pairs={{28,0},{29,1},{30,2},{31,3},{0,4},{1,5},{2,6},{3,7},{4,8},{5,9},{6... | collective-permute-start | bytes 1572872 | tf_op jit(solution)/shard_map/ppermute | solution.py:12
  127.7 19.5 %collective-permute-start.9 = (f32[1024,128]{1,0:T(8,128)S(1)}, f32[1024,128]{1,0:T(8,128)S(1)}, u32[]{:S(2)}, u32[]{:S(2)}) collective-permute-start(f32[1024,128]{1,0:T(8,128)S(1)} %collective-permute-done.8), channel_id=1, source_target_pairs={{31,0},{0,1},{1,2},{2,3},{3,4},{4,5},{5,6},{6,7},{7,8},{8,9},{9,10... | collective-permute-start | bytes 1572872 | tf_op jit(solution)/shard_map/ppermute | solution.py:12
  130.3 28.1 %collective-permute-start.12 = (f32[1024,128]{1,0:T(8,128)S(1)}, f32[1024,128]{1,0:T(8,128)S(1)}, u32[]{:S(2)}, u32[]{:S(2)}) collective-permute-start(f32[1024,128]{1,0:T(8,128)S(1)} %bitcast.227), channel_id=1, source_target_pairs={{31,0},{0,1},{1,2},{2,3},{3,4},{4,5},{5,6},{6,7},{7,8},{8,9},{9,10... | collective-permute-start | bytes 1572872 | tf_op jit(solution)/shard_map/ppermute | solution.py:12
  148.3 21.4 %collective-permute-start.10 = (f32[1024,128]{1,0:T(8,128)S(1)}, f32[1024,128]{1,0:T(8,128)S(1)}, u32[]{:S(2)}, u32[]{:S(2)}) collective-permute-start(f32[1024,128]{1,0:T(8,128)S(1)} %collective-permute-done.9), channel_id=1, source_target_pairs={{31,0},{0,1},{1,2},{2,3},{3,4},{4,5},{5,6},{6,7},{7,8},{8,9},{9,10... | collective-permute-start | bytes 1572872 | tf_op jit(solution)/shard_map/ppermute | solution.py:12
  158.5 22.4 %collective-permute-start.13 = (f32[1024,128]{1,0:T(8,128)S(1)}, f32[1024,128]{1,0:T(8,128)S(1)}, u32[]{:S(2)}, u32[]{:S(2)}) collective-permute-start(f32[1024,128]{1,0:T(8,128)S(1)} %bitcast_add_fusion.2), channel_id=1, source_target_pairs={{31,0},{0,1},{1,2},{2,3},{3,4},{4,5},{5,6},{6,7},{7,8},{8,9},{9,10... | collective-permute-start | bytes 1572872 | tf_op jit(solution)/shard_map/ppermute | solution.py:12
  170.8 21.4 %collective-permute-start.11 = (f32[1024,128]{1,0:T(8,128)S(1)}, f32[1024,128]{1,0:T(8,128)S(1)}, u32[]{:S(2)}, u32[]{:S(2)}) collective-permute-start(f32[1024,128]{1,0:T(8,128)S(1)} %collective-permute-done.10), channel_id=1, source_target_pairs={{31,0},{0,1},{1,2},{2,3},{3,4},{4,5},{5,6},{6,7},{7,8},{8,9},{9,10... | collective-permute-start | bytes 1572872 | tf_op jit(solution)/shard_map/ppermute | solution.py:12
  180.9 17.8 %collective-permute-start.14 = (f32[1024,128]{1,0:T(8,128)S(1)}, f32[1024,128]{1,0:T(8,128)S(1)}, u32[]{:S(2)}, u32[]{:S(2)}) collective-permute-start(f32[1024,128]{1,0:T(8,128)S(1)} %bitcast_add_fusion.1), channel_id=1, source_target_pairs={{31,0},{0,1},{1,2},{2,3},{3,4},{4,5},{5,6},{6,7},{7,8},{8,9},{9,10... | collective-permute-start | bytes 1572872 | tf_op jit(solution)/shard_map/ppermute | solution.py:12
  198.8 13.9 %collective-permute-start.15 = (f32[1024,128]{1,0:T(8,128)S(1)}, f32[1024,128]{1,0:T(8,128)S(1)}, u32[]{:S(2)}, u32[]{:S(2)}) collective-permute-start(f32[1024,128]{1,0:T(8,128)S(1)} %bitcast_add_fusion), channel_id=1, source_target_pairs={{31,0},{0,1},{1,2},{2,3},{3,4},{4,5},{5,6},{6,7},{7,8},{8,9},{9,10... | collective-permute-start | bytes 1572872 | tf_op jit(solution)/shard_map/ppermute | solution.py:12
  212.8 23.1 %collective-permute-start.16 = (f32[1024,128]{1,0:T(8,128)S(1)}, f32[1024,128]{1,0:T(8,128)S(1)}, u32[]{:S(2)}, u32[]{:S(2)}) collective-permute-start(f32[1024,128]{1,0:T(8,128)S(1)} %collective-permute-done.15), channel_id=1, source_target_pairs={{8,0},{9,1},{10,2},{11,3},{12,4},{13,5},{14,6},{15,7},{16,8},{17,9... | collective-permute-start | bytes 1572872 | tf_op jit(solution)/shard_map/ppermute | solution.py:12
where the time goes:
time: 237 us
  waiting for transfers between devices  147 us (62%)
  starting transfers between devices  47.5 us (20%)
  matrix products  29.7 us (13%)
  other arithmetic  7.42 us (3%)
  local copies, waits for them, and re-layouts  3.94 us (2%)
    ppermute x17, waiting for transfers between devices, shifted(): return lax.ppermute(block, axis, route)  147 us
    ppermute x17, starting transfers between devices, shifted(): return lax.ppermute(block, axis, route)  47.5 us
    dot_general x8, matrix products, device_terms(): right = jnp.einsum('sr,rad->sad', cols_pick, ctx_tiles, precision=high)  6.34 us
    dot_general x8, matrix products, device_terms(): left = jnp.einsum('sr,rad->sad', rows_pick, vert_tiles, precision=high)  5.31 us
    convert_element_type x8, other arithmetic, device_terms(): mask = (jnp.arange(slots, dtype=jnp.int32) < live).astype(jnp.float32)  5.15 us
  transfers between devices with their start and end apart: 17, of which 16 were waited for; matrix products, arithmetic and copies ran while one was open for 16% of the time, Pallas kernels for 0%

commit v1 on v0

v1 whole, which is shorter than its diff:
```python
import jax
import jax.numpy as jnp
from jax import lax
from jax.experimental import pallas as pl
from jax.experimental.pallas import tpu as pltpu
from jax.sharding import PartitionSpec as P

RATES = (0.02, 0.01)
TILE = 128
SLOTS = 2
SUB = 4
VMEM_BYTES = 32 * 1024 * 1024

IN_VMEM = pl.BlockSpec(memory_space=pltpu.VMEM)
IN_SMEM = pl.BlockSpec(memory_space=pltpu.SMEM)
PARAMS = pltpu.CompilerParams(vmem_limit_bytes=VMEM_BYTES)
PAIR = jax.ShapeDtypeStruct((SLOTS, TILE, TILE), jnp.float32)


def tile_rows(index):
    return pl.ds(pl.multiple_of(index * TILE, TILE), TILE)


def from_peer(block, distance):
    size = lax.axis_size("blk")
    return lax.ppermute(block, "blk", [((i + distance) % size, i) for i in range(size)])


def product(left, right, dims):
    return lax.dot_general(
        left,
        right,
        (dims, ((), ())),
        precision=lax.Precision.HIGHEST,
        preferred_element_type=jnp.float32,
    )


def select_columns(context, ids, offset, row_tiles):
    def kernel(ids_ref, context_ref, out_ref):
        for s in range(SLOTS):
            out_ref[s] = context_ref[tile_rows(ids_ref[0, offset, s] % row_tiles), :]

    return pl.pallas_call(
        kernel,
        out_shape=PAIR,
        in_specs=[IN_SMEM, IN_VMEM],
        out_specs=IN_VMEM,
        compiler_params=PARAMS,
        name=f"select_{offset}",
    )(ids, context)


def pair_terms(vert, cols, ids, live, pos, neg, offset, row_tiles):
    def kernel(ids_ref, live_ref, vert_ref, cols_ref, pos_ref, neg_ref, gv_ref, gc_ref):
        for s in range(SLOTS):
            left = vert_ref[tile_rows(ids_ref[0, offset, s] // row_tiles), :]
            right = cols_ref[s]
            score = product(left, right, ((1,), (1,)))
            sig = jax.nn.sigmoid(score)
            pos_f = pos_ref[0, offset, s].astype(jnp.float32)
            neg_f = neg_ref[0, offset, s].astype(jnp.float32)
            grad = neg_f * sig - pos_f * (1.0 - sig)
            grad = jnp.where(s < live_ref[0, offset], grad, 0.0)
            gv_ref[s] = product(grad, right, ((1,), (0,)))
            gc_ref[s] = product(grad, left, ((0,), (0,)))

    return pl.pallas_call(
        kernel,
        out_shape=(PAIR, PAIR),
        in_specs=[IN_SMEM, IN_SMEM] + [IN_VMEM] * 4,
        out_specs=(IN_VMEM, IN_VMEM),
        compiler_params=PARAMS,
        name=f"terms_{offset}",
    )(ids, live, vert, cols, pos, neg)


def apply_vertex(vert, ids, grads, epoch, row_tiles):
    def kernel(ids_ref, vert_ref, *refs):
        *grad_refs, out_ref = refs
        out_ref[...] = vert_ref[...]
        for inner, grad_ref in enumerate(grad_refs):
            for s in range(SLOTS):
                rows = tile_rows(ids_ref[0, epoch * SUB + inner, s] // row_tiles)
                out_ref[rows, :] -= RATES[epoch] * grad_ref[s]

    return pl.pallas_call(
        kernel,
        out_shape=jax.ShapeDtypeStruct(vert.shape, vert.dtype),
        in_specs=[IN_SMEM, IN_VMEM] + [IN_VMEM] * len(grads),
        out_specs=IN_VMEM,
        compiler_params=PARAMS,
        name=f"vertex_{epoch}",
    )(ids, vert, *grads)


def apply_context(ctx, ids, grads, epoch, row_tiles, sends):
    n = len(grads)

    def kernel(*refs):
        id_refs, send_refs = refs[:n], refs[n : n + len(sends)]
        ctx_ref, *grad_refs = refs[n + len(sends) : 2 * n + len(sends) + 1]
        out_ref, *tile_refs = refs[2 * n + len(sends) + 1 :]
        out_ref[...] = ctx_ref[...]
        for inner in range(n):
            for s in range(SLOTS):
                rows = tile_rows(id_refs[inner][0, epoch * SUB + inner, s] % row_tiles)
                out_ref[rows, :] -= RATES[epoch] * grad_refs[inner][s]
        for (_, offset), send_ref, tile_ref in zip(sends, send_refs, tile_refs):
            for s in range(SLOTS):
                tile_ref[s] = out_ref[tile_rows(send_ref[0, offset, s] % row_tiles), :]

    return pl.pallas_call(
        kernel,
        out_shape=(jax.ShapeDtypeStruct(ctx.shape, ctx.dtype),) + (PAIR,) * len(sends),
        in_specs=[IN_SMEM] * (n + len(sends)) + [IN_VMEM] * (n + 1),
        out_specs=(IN_VMEM,) * (1 + len(sends)),
        compiler_params=PARAMS,
        name=f"context_{epoch}",
    )(*ids, *[peer for peer, _ in sends], ctx, *grads)


def per_device(vertex, context, tile_ids, live_tiles, pos_counts, neg_counts):
    row_tiles = vertex.shape[0] // TILE
    peer_ids = {0: tile_ids}
    for k in range(1, SUB):
        peer_ids[k] = from_peer(tile_ids, k)
    near = jnp.concatenate([peer_ids[k] for k in range(SUB)], axis=0)
    far = from_peer(near, SUB)
    for k in range(SUB):
        peer_ids[SUB + k] = far[k : k + 1]

    vert, ctx = vertex, context
    sends = {k: select_columns(ctx, peer_ids[k], k, row_tiles) for k in range(SUB)}
    for epoch in range(2):
        vert_grads, ctx_grads = [], []
        offsets = range(epoch * SUB, (epoch + 1) * SUB)
        for k in offsets:
            cols = from_peer(sends[k], -k) if k else sends[k]
            gv, gc = pair_terms(vert, cols, tile_ids, live_tiles, pos_counts, neg_counts, k, row_tiles)
            vert_grads.append(gv)
            ctx_grads.append(from_peer(gc, k) if k else gc)
        vert = apply_vertex(vert, tile_ids, vert_grads, epoch, row_tiles)
        following = range(SUB, 2 * SUB) if epoch == 0 else ()
        ctx, *tiles = apply_context(
            ctx,
            [peer_ids[k] for k in offsets],
            ctx_grads,
            epoch,
            row_tiles,
            [(peer_ids[k], k) for k in following],
        )
        sends = dict(zip(following, tiles))
    return vert, ctx


def solution(mesh):
    placed = (
        P(("ep", "blk"), None),
        P(("ep", "blk"), None),
        P(("ep", "blk"), None, None),
        P(("ep", "blk"), None),
        P(("ep", "blk"), None, None, None, None),
        P(("ep", "blk"), None, None, None, None),
    )
    return jax.shard_map(
        per_device,
        mesh=mesh,
        in_specs=placed,
        out_specs=(P(("ep", "blk"), None), P(("ep", "blk"), None)),
        check_vma=False,
    )
```

time: 237 us -> 122 us (0.51)
  the two profiles are of different devices: /device:TPU:66 before, /device:TPU:56 now
where the time goes in v1:
time: 122 us
  starting transfers between devices  76 us (62%)
  waiting for transfers between devices  22.1 us (18%)
  Pallas kernels  19.5 us (16%)
  local copies, waits for them, and re-layouts  2.86 us (2%)
    ppermute x18, starting transfers between devices, from_peer(): lax.ppermute(block, 'blk', [((i + distance) % size, i) for i in range(siz...  76 us
    ppermute x18, waiting for transfers between devices, from_peer(): lax.ppermute(block, 'blk', [((i + distance) % size, i) for i in range(siz...  22.1 us
    pallas_call x8, Pallas kernels, pair_terms(): pl.pallas_call(kernel, out_shape=(PAIR, PAIR), in_specs=[IN_SMEM, IN_SMEM...  11.9 us
    pallas_call x2, Pallas kernels, apply_context(): pl.pallas_call(kernel, out_shape=(jax.ShapeDtypeStruct(ctx.shape, ctx.dty...  2.91 us
    unnamed x15, local copies, waits for them, and re-layouts  2.86 us
    pallas_call x4, Pallas kernels, select_columns(): pl.pallas_call(kernel, out_shape=PAIR, in_specs=[IN_SMEM, IN_VMEM], out_s...  2.47 us
  transfers between devices with their start and end apart: 18, of which 7 were waited for; matrix products, arithmetic and copies ran while one was open for 0% of the time, Pallas kernels for 13%

profile of v1, /device:TPU:56, one launch (start us, length us, event | category | flops | bytes accessed | tf_op | source)
XLA Modules:
  0.0 121.5 jit_solution(8145721869235594082)
XLA Ops:
  1.4 4.8 %collective-permute-start.4 = (s32[1,8,2]{2,1,0:T(8,128)S(1)}, s32[1,8,2]{2,1,0:T(8,128)S(1)}, u32[]{:S(2)}, u32[]{:S(2)}) collective-permute-start(s32[1,8,2]{2,1,0:T(8,128)S(1)} %copy.59.ids_ref.refs_0_), channel_id=1, source_target_pairs={{3,0},{4,1},{5,2},{6,3},{7,4},{8,5},{9,6},{10,7},{11,8},{12,9},{13... | collective-permute-start | bytes 200 | tf_op jit(solution)/shard_map/ppermute | solution.py:26
  6.2 1.8 %collective-permute-done.4.ids_ref.refs_3_ = s32[1,8,2]{2,1,0:T(8,128)S(1)} collective-permute-done((s32[1,8,2]{2,1,0:T(8,128)S(1)}, s32[1,8,2]{2,1,0:T(8,128)S(1)}, u32[]{:S(2)}, u32[]{:S(2)}) %collective-permute-start.4) | collective-permute-done | bytes 96 | tf_op jit(solution)/shard_map/ppermute | solution.py:26
  9.7 5.2 %collective-permute-start.5 = (f32[2,128,128]{2,1,0:T(8,128)S(1)}, f32[2,128,128]{2,1,0:T(8,128)S(1)}, u32[]{:S(2)}, u32[]{:S(2)}) collective-permute-start(f32[2,128,128]{2,1,0:T(8,128)S(1)} %select_3.1), channel_id=1, source_target_pairs={{29,0},{30,1},{31,2},{0,3},{1,4},{2,5},{3,6},{4,7},{5,8},{6,9},{7,... | collective-permute-start | bytes 393224 | tf_op jit(solution)/shard_map/ppermute | solution.py:26
  14.9 6.6 %collective-permute-start.2 = (s32[1,8,2]{2,1,0:T(8,128)S(1)}, s32[1,8,2]{2,1,0:T(8,128)S(1)}, u32[]{:S(2)}, u32[]{:S(2)}) collective-permute-start(s32[1,8,2]{2,1,0:T(8,128)S(1)} %copy.59.ids_ref.refs_0_), channel_id=1, source_target_pairs={{2,0},{3,1},{4,2},{5,3},{6,4},{7,5},{8,6},{9,7},{10,8},{11,9},{12,... | collective-permute-start | bytes 200 | tf_op jit(solution)/shard_map/ppermute | solution.py:26
  23.6 4.8 %collective-permute-start.3 = (f32[2,128,128]{2,1,0:T(8,128)S(1)}, f32[2,128,128]{2,1,0:T(8,128)S(1)}, u32[]{:S(2)}, u32[]{:S(2)}) collective-permute-start(f32[2,128,128]{2,1,0:T(8,128)S(1)} %select_2.1), channel_id=1, source_target_pairs={{30,0},{31,1},{0,2},{1,3},{2,4},{3,5},{4,6},{5,7},{6,8},{7,9},{8,1... | collective-permute-start | bytes 393224 | tf_op jit(solution)/shard_map/ppermute | solution.py:26
  28.4 2.2 %collective-permute-start = (s32[1,8,2]{2,1,0:T(8,128)S(1)}, s32[1,8,2]{2,1,0:T(8,128)S(1)}, u32[]{:S(2)}, u32[]{:S(2)}) collective-permute-start(s32[1,8,2]{2,1,0:T(8,128)S(1)} %copy.59.ids_ref.refs_0_), channel_id=1, source_target_pairs={{1,0},{2,1},{3,2},{4,3},{5,4},{6,5},{7,6},{8,7},{9,8},{10,9},{11,1... | collective-permute-start | bytes 200 | tf_op jit(solution)/shard_map/ppermute | solution.py:26
  30.6 6.0 %collective-permute-done.ids_ref.refs_1_ = s32[1,8,2]{2,1,0:T(8,128)S(1)} collective-permute-done((s32[1,8,2]{2,1,0:T(8,128)S(1)}, s32[1,8,2]{2,1,0:T(8,128)S(1)}, u32[]{:S(2)}, u32[]{:S(2)}) %collective-permute-start) | collective-permute-done | bytes 96 | tf_op jit(solution)/shard_map/ppermute | solution.py:26
  37.3 1.9 %collective-permute-start.1 = (f32[2,128,128]{2,1,0:T(8,128)S(1)}, f32[2,128,128]{2,1,0:T(8,128)S(1)}, u32[]{:S(2)}, u32[]{:S(2)}) collective-permute-start(f32[2,128,128]{2,1,0:T(8,128)S(1)} %select_1.1), channel_id=1, source_target_pairs={{31,0},{0,1},{1,2},{2,3},{3,4},{4,5},{5,6},{6,7},{7,8},{8,9},{9,10... | collective-permute-start | bytes 393224 | tf_op jit(solution)/shard_map/ppermute | solution.py:26
  40.9 1.5 %terms_0.1 = (f32[2,128,128]{2,1,0:T(8,128)S(1)}, f32[2,128,128]{2,1,0:T(8,128)S(1)}) custom-call(s32[1,8,2]{2,1,0:T(8,128)S(1)} %copy.59.ids_ref.refs_0_, s32[1,8]{1,0:T(1,128)S(1)} %copy-done.6, f32[1024,128]{1,0:T(8,128)S(1)} %copy-done.4, f32[2,128,128]{2,1,0:T(8,128)S(1)} %select_0.1.cols_ref, s32[1,8,2,128,128]{4,3,2,1,0:T(8,128)S(1)} %copy-done, ...), custom_call_target="tpu_custom_call" | custom-call | tf_op jit(solution)/shard_map/terms_0/pallas_call | solution.py:68
  42.4 7.5 %collective-permute-start.6 = (s32[4,8,2]{2,1,0:T(8,128)S(1)}, s32[4,8,2]{2,1,0:T(8,128)S(1)}, u32[]{:S(2)}, u32[]{:S(2)}) collective-permute-start(s32[4,8,2]{2,1,0:T(8,128)S(1)} %pad_add_fusion), channel_id=1, source_target_pairs={{4,0},{5,1},{6,2},{7,3},{8,4},{9,5},{10,6},{11,7},{12,8},{13,9},{1... | collective-permute-start | bytes 776 | tf_op jit(solution)/shard_map/ppermute | solution.py:26
  50.0 1.5 %terms_3.1 = (f32[2,128,128]{2,1,0:T(8,128)S(1)}, f32[2,128,128]{2,1,0:T(8,128)S(1)}) custom-call(s32[1,8,2]{2,1,0:T(8,128)S(1)} %copy.59.ids_ref.refs_0_, s32[1,8]{1,0:T(1,128)S(1)} %copy-done.6, f32[1024,128]{1,0:T(8,128)S(1)} %copy-done.4, f32[2,128,128]{2,1,0:T(8,128)S(1)} %collective-permute-done.5.cols_ref, s32[1,8,2,128,128]{4,3,2,1,0:T(8,128)S(1)} %copy-done, ...), custom_call_target="tpu_custom_call" | custom-call | tf_op jit(solution)/shard_map/terms_3/pallas_call | solution.py:68
  51.5 2.3 %collective-permute-start.9 = (f32[2,128,128]{2,1,0:T(8,128)S(1)}, f32[2,128,128]{2,1,0:T(8,128)S(1)}, u32[]{:S(2)}, u32[]{:S(2)}) collective-permute-start(f32[2,128,128]{2,1,0:T(8,128)S(1)} %get-tuple-element.30), channel_id=1, source_target_pairs={{3,0},{4,1},{5,2},{6,3},{7,4},{8,5},{9,6},{10,7},{11,8},{12,9},{13... | collective-permute-start | bytes 393224 | tf_op jit(solution)/shard_map/ppermute | solution.py:26
  53.8 1.5 %terms_2.1 = (f32[2,128,128]{2,1,0:T(8,128)S(1)}, f32[2,128,128]{2,1,0:T(8,128)S(1)}) custom-call(s32[1,8,2]{2,1,0:T(8,128)S(1)} %copy.59.ids_ref.refs_0_, s32[1,8]{1,0:T(1,128)S(1)} %copy-done.6, f32[1024,128]{1,0:T(8,128)S(1)} %copy-done.4, f32[2,128,128]{2,1,0:T(8,128)S(1)} %collective-permute-done.3.cols_ref, s32[1,8,2,128,128]{4,3,2,1,0:T(8,128)S(1)} %copy-done, ...), custom_call_target="tpu_custom_call" | custom-call | tf_op jit(solution)/shard_map/terms_2/pallas_call | solution.py:68
  55.3 4.7 %collective-permute-start.8 = (f32[2,128,128]{2,1,0:T(8,128)S(1)}, f32[2,128,128]{2,1,0:T(8,128)S(1)}, u32[]{:S(2)}, u32[]{:S(2)}) collective-permute-start(f32[2,128,128]{2,1,0:T(8,128)S(1)} %get-tuple-element.29), channel_id=1, source_target_pairs={{2,0},{3,1},{4,2},{5,3},{6,4},{7,5},{8,6},{9,7},{10,8},{11,9},{12,... | collective-permute-start | bytes 393224 | tf_op jit(solution)/shard_map/ppermute | solution.py:26
  60.1 1.5 %terms_1.1 = (f32[2,128,128]{2,1,0:T(8,128)S(1)}, f32[2,128,128]{2,1,0:T(8,128)S(1)}) custom-call(s32[1,8,2]{2,1,0:T(8,128)S(1)} %copy.59.ids_ref.refs_0_, s32[1,8]{1,0:T(1,128)S(1)} %copy-done.6, f32[1024,128]{1,0:T(8,128)S(1)} %copy-done.4, f32[2,128,128]{2,1,0:T(8,128)S(1)} %collective-permute-done.1.cols_ref, s32[1,8,2,128,128]{4,3,2,1,0:T(8,128)S(1)} %copy-done, ...), custom_call_target="tpu_custom_call" | custom-call | tf_op jit(solution)/shard_map/terms_1/pallas_call | solution.py:68
  61.6 1.9 %collective-permute-start.7 = (f32[2,128,128]{2,1,0:T(8,128)S(1)}, f32[2,128,128]{2,1,0:T(8,128)S(1)}, u32[]{:S(2)}, u32[]{:S(2)}) collective-permute-start(f32[2,128,128]{2,1,0:T(8,128)S(1)} %get-tuple-element.28), channel_id=1, source_target_pairs={{1,0},{2,1},{3,2},{4,3},{5,4},{6,5},{7,6},{8,7},{9,8},{10,9},{11,1... | collective-permute-start | bytes 393224 | tf_op jit(solution)/shard_map/ppermute | solution.py:26
  64.1 7.0 %collective-permute-done.7.refs_10_ = f32[2,128,128]{2,1,0:T(8,128)S(1)} collective-permute-done((f32[2,128,128]{2,1,0:T(8,128)S(1)}, f32[2,128,128]{2,1,0:T(8,128)S(1)}, u32[]{:S(2)}, u32[]{:S(2)}) %collective-permute-start.7) | collective-permute-done | bytes 131104 | tf_op jit(solution)/shard_map/ppermute | solution.py:26
  72.4 3.6 %collective-permute-start.10 = (f32[2,128,128]{2,1,0:T(8,128)S(1)}, f32[2,128,128]{2,1,0:T(8,128)S(1)}, u32[]{:S(2)}, u32[]{:S(2)}) collective-permute-start(f32[2,128,128]{2,1,0:T(8,128)S(1)} %get-tuple-element.31), channel_id=1, source_target_pairs={{28,0},{29,1},{30,2},{31,3},{0,4},{1,5},{2,6},{3,7},{4,8},{5,9},{6... | collective-permute-start | bytes 393224 | tf_op jit(solution)/shard_map/ppermute | solution.py:26
  76.0 1.9 %collective-permute-start.11 = (f32[2,128,128]{2,1,0:T(8,128)S(1)}, f32[2,128,128]{2,1,0:T(8,128)S(1)}, u32[]{:S(2)}, u32[]{:S(2)}) collective-permute-start(f32[2,128,128]{2,1,0:T(8,128)S(1)} %get-tuple-element.33), channel_id=1, source_target_pairs={{27,0},{28,1},{29,2},{30,3},{31,4},{0,5},{1,6},{2,7},{3,8},{4,9},{... | collective-permute-start | bytes 393224 | tf_op jit(solution)/shard_map/ppermute | solution.py:26
  77.9 3.2 %collective-permute-start.12 = (f32[2,128,128]{2,1,0:T(8,128)S(1)}, f32[2,128,128]{2,1,0:T(8,128)S(1)}, u32[]{:S(2)}, u32[]{:S(2)}) collective-permute-start(f32[2,128,128]{2,1,0:T(8,128)S(1)} %get-tuple-element.35), channel_id=1, source_target_pairs={{26,0},{27,1},{28,2},{29,3},{30,4},{31,5},{0,6},{1,7},{2,8},{3,9},... | collective-permute-start | bytes 393224 | tf_op jit(solution)/shard_map/ppermute | solution.py:26
  81.1 5.2 %collective-permute-start.13 = (f32[2,128,128]{2,1,0:T(8,128)S(1)}, f32[2,128,128]{2,1,0:T(8,128)S(1)}, u32[]{:S(2)}, u32[]{:S(2)}) collective-permute-start(f32[2,128,128]{2,1,0:T(8,128)S(1)} %get-tuple-element.37), channel_id=1, source_target_pairs={{25,0},{26,1},{27,2},{28,3},{29,4},{30,5},{31,6},{0,7},{1,8},{2,9}... | collective-permute-start | bytes 393224 | tf_op jit(solution)/shard_map/ppermute | solution.py:26
  87.0 1.5 %terms_4.1 = (f32[2,128,128]{2,1,0:T(8,128)S(1)}, f32[2,128,128]{2,1,0:T(8,128)S(1)}) custom-call(s32[1,8,2]{2,1,0:T(8,128)S(1)} %copy.59.ids_ref.refs_0_, s32[1,8]{1,0:T(1,128)S(1)} %copy-done.6, f32[1024,128]{1,0:T(8,128)S(1)} %vertex_0.1.vert_ref, f32[2,128,128]{2,1,0:T(8,128)S(1)} %collective-permute-done.10.cols_ref, ...), custom_call_target="tpu_custom_call" | custom-call | tf_op jit(solution)/shard_map/terms_4/pallas_call | solution.py:68
  88.6 3.3 %collective-permute-start.14 = (f32[2,128,128]{2,1,0:T(8,128)S(1)}, f32[2,128,128]{2,1,0:T(8,128)S(1)}, u32[]{:S(2)}, u32[]{:S(2)}) collective-permute-start(f32[2,128,128]{2,1,0:T(8,128)S(1)} %get-tuple-element.40), channel_id=1, source_target_pairs={{4,0},{5,1},{6,2},{7,3},{8,4},{9,5},{10,6},{11,7},{12,8},{13,9},{1... | collective-permute-start | bytes 393224 | tf_op jit(solution)/shard_map/ppermute | solution.py:26
  91.9 1.5 %terms_5.1 = (f32[2,128,128]{2,1,0:T(8,128)S(1)}, f32[2,128,128]{2,1,0:T(8,128)S(1)}) custom-call(s32[1,8,2]{2,1,0:T(8,128)S(1)} %copy.59.ids_ref.refs_0_, s32[1,8]{1,0:T(1,128)S(1)} %copy-done.6, f32[1024,128]{1,0:T(8,128)S(1)} %vertex_0.1.vert_ref, f32[2,128,128]{2,1,0:T(8,128)S(1)} %collective-permute-done.11.cols_ref, ...), custom_call_target="tpu_custom_call" | custom-call | tf_op jit(solution)/shard_map/terms_5/pallas_call | solution.py:68
  93.4 3.7 %collective-permute-start.15 = (f32[2,128,128]{2,1,0:T(8,128)S(1)}, f32[2,128,128]{2,1,0:T(8,128)S(1)}, u32[]{:S(2)}, u32[]{:S(2)}) collective-permute-start(f32[2,128,128]{2,1,0:T(8,128)S(1)} %get-tuple-element.41), channel_id=1, source_target_pairs={{5,0},{6,1},{7,2},{8,3},{9,4},{10,5},{11,6},{12,7},{13,8},{14,9},{... | collective-permute-start | bytes 393224 | tf_op jit(solution)/shard_map/ppermute | solution.py:26
  97.1 1.5 %terms_6.1 = (f32[2,128,128]{2,1,0:T(8,128)S(1)}, f32[2,128,128]{2,1,0:T(8,128)S(1)}) custom-call(s32[1,8,2]{2,1,0:T(8,128)S(1)} %copy.59.ids_ref.refs_0_, s32[1,8]{1,0:T(1,128)S(1)} %copy-done.6, f32[1024,128]{1,0:T(8,128)S(1)} %vertex_0.1.vert_ref, f32[2,128,128]{2,1,0:T(8,128)S(1)} %collective-permute-done.12.cols_ref, ...), custom_call_target="tpu_custom_call" | custom-call | tf_op jit(solution)/shard_map/terms_6/pallas_call | solution.py:68
  98.6 11.0 %collective-permute-start.16 = (f32[2,128,128]{2,1,0:T(8,128)S(1)}, f32[2,128,128]{2,1,0:T(8,128)S(1)}, u32[]{:S(2)}, u32[]{:S(2)}) collective-permute-start(f32[2,128,128]{2,1,0:T(8,128)S(1)} %get-tuple-element.42), channel_id=1, source_target_pairs={{6,0},{7,1},{8,2},{9,3},{10,4},{11,5},{12,6},{13,7},{14,8},{15,9},... | collective-permute-start | bytes 393224 | tf_op jit(solution)/shard_map/ppermute | solution.py:26
  109.7 1.5 %terms_7.1 = (f32[2,128,128]{2,1,0:T(8,128)S(1)}, f32[2,128,128]{2,1,0:T(8,128)S(1)}) custom-call(s32[1,8,2]{2,1,0:T(8,128)S(1)} %copy.59.ids_ref.refs_0_, s32[1,8]{1,0:T(1,128)S(1)} %copy-done.6, f32[1024,128]{1,0:T(8,128)S(1)} %vertex_0.1.vert_ref, f32[2,128,128]{2,1,0:T(8,128)S(1)} %collective-permute-done.13.cols_ref, ...), custom_call_target="tpu_custom_call" | custom-call | tf_op jit(solution)/shard_map/terms_7/pallas_call | solution.py:68
  111.2 1.9 %collective-permute-start.17 = (f32[2,128,128]{2,1,0:T(8,128)S(1)}, f32[2,128,128]{2,1,0:T(8,128)S(1)}, u32[]{:S(2)}, u32[]{:S(2)}) collective-permute-start(f32[2,128,128]{2,1,0:T(8,128)S(1)} %get-tuple-element.43), channel_id=1, source_target_pairs={{7,0},{8,1},{9,2},{10,3},{11,4},{12,5},{13,6},{14,7},{15,8},{16,9}... | collective-permute-start | bytes 393224 | tf_op jit(solution)/shard_map/ppermute | solution.py:26
  113.1 1.5 %vertex_1.1 = f32[1024,128]{1,0:T(8,128)} custom-call(s32[1,8,2]{2,1,0:T(8,128)S(1)} %copy.59.ids_ref.refs_0_, f32[1024,128]{1,0:T(8,128)S(1)} %vertex_0.1.vert_ref, f32[2,128,128]{2,1,0:T(8,128)S(1)} %get-tuple-element.32.refs_0_, f32[2,128,128]{2,1,0:T(8,128)S(1)} %get-tuple-element.34.refs_1_, f32[2,128,128]{2,1,0:T(8,128)S(1)} %get-tuple-element.36.refs_2_, ...), custom_call_target="tpu_custom_call" | custom-call | tf_op jit(solution)/shard_map/vertex_1/pallas_call | solution.py:87
  114.7 5.1 %collective-permute-done.17.refs_8_ = f32[2,128,128]{2,1,0:T(8,128)S(1)} collective-permute-done((f32[2,128,128]{2,1,0:T(8,128)S(1)}, f32[2,128,128]{2,1,0:T(8,128)S(1)}, u32[]{:S(2)}, u32[]{:S(2)}) %collective-permute-start.17) | collective-permute-done | bytes 131104 | tf_op jit(solution)/shard_map/ppermute | solution.py:26
  119.9 1.7 %context_1.1 = f32[1024,128]{1,0:T(8,128)} custom-call(s32[1,8,2]{2,1,0:T(8,128)S(1)} %get-tuple-element.47.refs_4_.refs_0_, s32[1,8,2]{2,1,0:T(8,128)S(1)} %get-tuple-element.46.refs_5_.refs_1_, s32[1,8,2]{2,1,0:T(8,128)S(1)} %get-tuple-element.45.refs_6_.refs_2_, s32[1,8,2]{2,1,0:T(8,128)S(1)} %get-tuple-element.44.refs_7_.refs_3_, ...), custom_call_target="tpu_custom_call" | custom-call | tf_op jit(solution)/shard_map/context_1/pallas_call | solution.py:113
  (37 shorter events, 9.4 us)
Async XLA Ops:
  1.4 6.6 %collective-permute-start.4 = (s32[1,8,2]{2,1,0:T(8,128)S(1)}, s32[1,8,2]{2,1,0:T(8,128)S(1)}, u32[]{:S(2)}, u32[]{:S(2)}) collective-permute-start(s32[1,8,2]{2,1,0:T(8,128)S(1)} %copy.59.ids_ref.refs_0_), channel_id=1, source_target_pairs={{3,0},{4,1},{5,2},{6,3},{7,4},{8,5},{9,6},{10,7},{11,8},{12,9},{13... | collective-permute-start | bytes 200 | tf_op jit(solution)/shard_map/ppermute | solution.py:26
  8.0 1.0 copy-start.2
  9.1 30.1 %copy-start.3 = (f32[1024,128]{1,0:T(8,128)S(1)}, f32[1024,128]{1,0:T(8,128)}, u32[]{:S(2)}) copy-start(f32[1024,128]{1,0:T(8,128)} %refs_8_.1) | copy-start | bytes 1572868
  9.1 30.8 %copy-start.1 = (s32[1,8,2,128,128]{4,3,2,1,0:T(8,128)S(1)}, s32[1,8,2,128,128]{4,3,2,1,0:T(8,128)}, u32[]{:S(2)}) copy-start(s32[1,8,2,128,128]{4,3,2,1,0:T(8,128)} %neg_ref.15) | copy-start | bytes 3145732
  9.7 30.2 %copy-start = (s32[1,8,2,128,128]{4,3,2,1,0:T(8,128)S(1)}, s32[1,8,2,128,128]{4,3,2,1,0:T(8,128)}, u32[]{:S(2)}) copy-start(s32[1,8,2,128,128]{4,3,2,1,0:T(8,128)} %pos_ref.15) | copy-start | bytes 3145732
  9.7 40.3 %collective-permute-start.5 = (f32[2,128,128]{2,1,0:T(8,128)S(1)}, f32[2,128,128]{2,1,0:T(8,128)S(1)}, u32[]{:S(2)}, u32[]{:S(2)}) collective-permute-start(f32[2,128,128]{2,1,0:T(8,128)S(1)} %select_3.1), channel_id=1, source_target_pairs={{29,0},{30,1},{31,2},{0,3},{1,4},{2,5},{3,6},{4,7},{5,8},{6,9},{7,... | collective-permute-start | bytes 393224 | tf_op jit(solution)/shard_map/ppermute | solution.py:26
  14.9 8.1 %collective-permute-start.2 = (s32[1,8,2]{2,1,0:T(8,128)S(1)}, s32[1,8,2]{2,1,0:T(8,128)S(1)}, u32[]{:S(2)}, u32[]{:S(2)}) collective-permute-start(s32[1,8,2]{2,1,0:T(8,128)S(1)} %copy.59.ids_ref.refs_0_), channel_id=1, source_target_pairs={{2,0},{3,1},{4,2},{5,3},{6,4},{7,5},{8,6},{9,7},{10,8},{11,9},{12,... | collective-permute-start | bytes 200 | tf_op jit(solution)/shard_map/ppermute | solution.py:26
  23.6 30.2 %collective-permute-start.3 = (f32[2,128,128]{2,1,0:T(8,128)S(1)}, f32[2,128,128]{2,1,0:T(8,128)S(1)}, u32[]{:S(2)}, u32[]{:S(2)}) collective-permute-start(f32[2,128,128]{2,1,0:T(8,128)S(1)} %select_2.1), channel_id=1, source_target_pairs={{30,0},{31,1},{0,2},{1,3},{2,4},{3,5},{4,6},{5,7},{6,8},{7,9},{8,1... | collective-permute-start | bytes 393224 | tf_op jit(solution)/shard_map/ppermute | solution.py:26
  28.4 8.2 %collective-permute-start = (s32[1,8,2]{2,1,0:T(8,128)S(1)}, s32[1,8,2]{2,1,0:T(8,128)S(1)}, u32[]{:S(2)}, u32[]{:S(2)}) collective-permute-start(s32[1,8,2]{2,1,0:T(8,128)S(1)} %copy.59.ids_ref.refs_0_), channel_id=1, source_target_pairs={{1,0},{2,1},{3,2},{4,3},{5,4},{6,5},{7,6},{8,7},{9,8},{10,9},{11,1... | collective-permute-start | bytes 200 | tf_op jit(solution)/shard_map/ppermute | solution.py:26
  37.3 2.6 %copy-start.6 = (s32[1,8]{1,0:T(1,128)S(1)}, s32[1,8]{1,0:T(1,128)}, u32[]{:S(2)}) copy-start(s32[1,8]{1,0:T(1,128)} %live_ref.15) | copy-start | bytes 100
  37.3 22.8 %collective-permute-start.1 = (f32[2,128,128]{2,1,0:T(8,128)S(1)}, f32[2,128,128]{2,1,0:T(8,128)S(1)}, u32[]{:S(2)}, u32[]{:S(2)}) collective-permute-start(f32[2,128,128]{2,1,0:T(8,128)S(1)} %select_1.1), channel_id=1, source_target_pairs={{31,0},{0,1},{1,2},{2,3},{3,4},{4,5},{5,6},{6,7},{7,8},{8,9},{9,10... | collective-permute-start | bytes 393224 | tf_op jit(solution)/shard_map/ppermute | solution.py:26
  39.9 1.0 copy-start.4
  42.4 21.1 %collective-permute-start.6 = (s32[4,8,2]{2,1,0:T(8,128)S(1)}, s32[4,8,2]{2,1,0:T(8,128)S(1)}, u32[]{:S(2)}, u32[]{:S(2)}) collective-permute-start(s32[4,8,2]{2,1,0:T(8,128)S(1)} %pad_add_fusion), channel_id=1, source_target_pairs={{4,0},{5,1},{6,2},{7,3},{8,4},{9,5},{10,6},{11,7},{12,8},{13,9},{1... | collective-permute-start | bytes 776 | tf_op jit(solution)/shard_map/ppermute | solution.py:26
  51.5 12.1 %collective-permute-start.9 = (f32[2,128,128]{2,1,0:T(8,128)S(1)}, f32[2,128,128]{2,1,0:T(8,128)S(1)}, u32[]{:S(2)}, u32[]{:S(2)}) collective-permute-start(f32[2,128,128]{2,1,0:T(8,128)S(1)} %get-tuple-element.30), channel_id=1, source_target_pairs={{3,0},{4,1},{5,2},{6,3},{7,4},{8,5},{9,6},{10,7},{11,8},{12,9},{13... | collective-permute-start | bytes 393224 | tf_op jit(solution)/shard_map/ppermute | solution.py:26
  55.3 8.8 %collective-permute-start.8 = (f32[2,128,128]{2,1,0:T(8,128)S(1)}, f32[2,128,128]{2,1,0:T(8,128)S(1)}, u32[]{:S(2)}, u32[]{:S(2)}) collective-permute-start(f32[2,128,128]{2,1,0:T(8,128)S(1)} %get-tuple-element.29), channel_id=1, source_target_pairs={{2,0},{3,1},{4,2},{5,3},{6,4},{7,5},{8,6},{9,7},{10,8},{11,9},{12,... | collective-permute-start | bytes 393224 | tf_op jit(solution)/shard_map/ppermute | solution.py:26
  61.6 9.6 %collective-permute-start.7 = (f32[2,128,128]{2,1,0:T(8,128)S(1)}, f32[2,128,128]{2,1,0:T(8,128)S(1)}, u32[]{:S(2)}, u32[]{:S(2)}) collective-permute-start(f32[2,128,128]{2,1,0:T(8,128)S(1)} %get-tuple-element.28), channel_id=1, source_target_pairs={{1,0},{2,1},{3,2},{4,3},{5,4},{6,5},{7,6},{8,7},{9,8},{10,9},{11,1... | collective-permute-start | bytes 393224 | tf_op jit(solution)/shard_map/ppermute | solution.py:26
  71.2 15.2 %copy-start.5 = (f32[1024,128]{1,0:T(8,128)S(1)}, f32[1024,128]{1,0:T(8,128)}, u32[]{:S(2)}) copy-start(f32[1024,128]{1,0:T(8,128)} %vert_ref.9) | copy-start | bytes 1572868
  72.4 14.7 %collective-permute-start.10 = (f32[2,128,128]{2,1,0:T(8,128)S(1)}, f32[2,128,128]{2,1,0:T(8,128)S(1)}, u32[]{:S(2)}, u32[]{:S(2)}) collective-permute-start(f32[2,128,128]{2,1,0:T(8,128)S(1)} %get-tuple-element.31), channel_id=1, source_target_pairs={{28,0},{29,1},{30,2},{31,3},{0,4},{1,5},{2,6},{3,7},{4,8},{5,9},{6... | collective-permute-start | bytes 393224 | tf_op jit(solution)/shard_map/ppermute | solution.py:26
  76.0 15.9 %collective-permute-start.11 = (f32[2,128,128]{2,1,0:T(8,128)S(1)}, f32[2,128,128]{2,1,0:T(8,128)S(1)}, u32[]{:S(2)}, u32[]{:S(2)}) collective-permute-start(f32[2,128,128]{2,1,0:T(8,128)S(1)} %get-tuple-element.33), channel_id=1, source_target_pairs={{27,0},{28,1},{29,2},{30,3},{31,4},{0,5},{1,6},{2,7},{3,8},{4,9},{... | collective-permute-start | bytes 393224 | tf_op jit(solution)/shard_map/ppermute | solution.py:26
  77.9 19.2 %collective-permute-start.12 = (f32[2,128,128]{2,1,0:T(8,128)S(1)}, f32[2,128,128]{2,1,0:T(8,128)S(1)}, u32[]{:S(2)}, u32[]{:S(2)}) collective-permute-start(f32[2,128,128]{2,1,0:T(8,128)S(1)} %get-tuple-element.35), channel_id=1, source_target_pairs={{26,0},{27,1},{28,2},{29,3},{30,4},{31,5},{0,6},{1,7},{2,8},{3,9},... | collective-permute-start | bytes 393224 | tf_op jit(solution)/shard_map/ppermute | solution.py:26
  81.1 28.6 %collective-permute-start.13 = (f32[2,128,128]{2,1,0:T(8,128)S(1)}, f32[2,128,128]{2,1,0:T(8,128)S(1)}, u32[]{:S(2)}, u32[]{:S(2)}) collective-permute-start(f32[2,128,128]{2,1,0:T(8,128)S(1)} %get-tuple-element.37), channel_id=1, source_target_pairs={{25,0},{26,1},{27,2},{28,3},{29,4},{30,5},{31,6},{0,7},{1,8},{2,9}... | collective-permute-start | bytes 393224 | tf_op jit(solution)/shard_map/ppermute | solution.py:26
  88.6 26.1 %collective-permute-start.14 = (f32[2,128,128]{2,1,0:T(8,128)S(1)}, f32[2,128,128]{2,1,0:T(8,128)S(1)}, u32[]{:S(2)}, u32[]{:S(2)}) collective-permute-start(f32[2,128,128]{2,1,0:T(8,128)S(1)} %get-tuple-element.40), channel_id=1, source_target_pairs={{4,0},{5,1},{6,2},{7,3},{8,4},{9,5},{10,6},{11,7},{12,8},{13,9},{1... | collective-permute-start | bytes 393224 | tf_op jit(solution)/shard_map/ppermute | solution.py:26
  93.4 21.2 %collective-permute-start.15 = (f32[2,128,128]{2,1,0:T(8,128)S(1)}, f32[2,128,128]{2,1,0:T(8,128)S(1)}, u32[]{:S(2)}, u32[]{:S(2)}) collective-permute-start(f32[2,128,128]{2,1,0:T(8,128)S(1)} %get-tuple-element.41), channel_id=1, source_target_pairs={{5,0},{6,1},{7,2},{8,3},{9,4},{10,5},{11,6},{12,7},{13,8},{14,9},{... | collective-permute-start | bytes 393224 | tf_op jit(solution)/shard_map/ppermute | solution.py:26
  98.6 16.1 %collective-permute-start.16 = (f32[2,128,128]{2,1,0:T(8,128)S(1)}, f32[2,128,128]{2,1,0:T(8,128)S(1)}, u32[]{:S(2)}, u32[]{:S(2)}) collective-permute-start(f32[2,128,128]{2,1,0:T(8,128)S(1)} %get-tuple-element.42), channel_id=1, source_target_pairs={{6,0},{7,1},{8,2},{9,3},{10,4},{11,5},{12,6},{13,7},{14,8},{15,9},... | collective-permute-start | bytes 393224 | tf_op jit(solution)/shard_map/ppermute | solution.py:26
  111.2 8.7 %collective-permute-start.17 = (f32[2,128,128]{2,1,0:T(8,128)S(1)}, f32[2,128,128]{2,1,0:T(8,128)S(1)}, u32[]{:S(2)}, u32[]{:S(2)}) collective-permute-start(f32[2,128,128]{2,1,0:T(8,128)S(1)} %get-tuple-element.43), channel_id=1, source_target_pairs={{7,0},{8,1},{9,2},{10,3},{11,4},{12,5},{13,6},{14,7},{15,8},{16,9}... | collective-permute-start | bytes 393224 | tf_op jit(solution)/shard_map/ppermute | solution.py:26

commit v2 on v0

v2 whole, which is shorter than its diff:
```python
import jax
import jax.numpy as jnp
from jax import lax
from jax.experimental import pallas as pl
from jax.experimental.pallas import tpu as pltpu
from jax.sharding import PartitionSpec as P

RATES = (0.02, 0.01)
TILE = 128
SLOTS = 2
SUB = 4
STEPS = 2 * SUB
CLASSES = (3, 2, 1, 0)
OTHERS = (3, 2, 1)
PAIR_ROWS = SLOTS * TILE
META = 32
LIVE_AT = SLOTS * STEPS
ODD_AT = LIVE_AT + STEPS
NOTE_ROWS = 8
VMEM_BYTES = 8 * 1024 * 1024

IN_VMEM = pl.BlockSpec(memory_space=pltpu.VMEM)
IN_SMEM = pl.BlockSpec(memory_space=pltpu.SMEM)
IN_HBM = pl.BlockSpec(memory_space=pltpu.HBM)
PARAMS = pltpu.CompilerParams(vmem_limit_bytes=VMEM_BYTES)
PAIR = jax.ShapeDtypeStruct((PAIR_ROWS, TILE), jnp.float32)
NOTED = jax.ShapeDtypeStruct((PAIR_ROWS + NOTE_ROWS, TILE), jnp.float32)
COUNTS = jax.ShapeDtypeStruct((2 * PAIR_ROWS + NOTE_ROWS, TILE), jnp.float32)


def ahead(place, cls):
    return ((place ^ ((SUB - cls) % SUB)) - place) & (SUB - 1)


def to_users(block, cls, extra=0):
    size = lax.axis_size("blk")
    return lax.ppermute(block, "blk", [(j, (j + ahead(j % SUB, cls) + extra) % size) for j in range(size)])


def to_owners(block, cls, extra=0):
    size = lax.axis_size("blk")
    return lax.ppermute(block, "blk", [((j + ahead(j % SUB, cls) + extra) % size, j) for j in range(size)])


def user_offset(cls, epoch, odd):
    return SUB * epoch + (0, 1 + 2 * odd, 2, 3 - 2 * odd)[cls]


def owner_offset(cls, epoch, odd):
    return SUB * epoch + (0, 3 - 2 * odd, 2, 1 + 2 * odd)[cls]


def tile_rows(index):
    return pl.ds(pl.multiple_of(index * TILE, TILE), TILE)


def slot_rows(slot, part=0):
    return pl.ds(part * PAIR_ROWS + slot * TILE, TILE)


def split(x):
    high = x.astype(jnp.bfloat16)
    return high, (x - high.astype(jnp.float32)).astype(jnp.bfloat16)


def product(left, right, dims):
    def dot(a, b):
        return lax.dot_general(a, b, (dims, ((), ())), preferred_element_type=jnp.float32)

    return dot(left[0], right[0]) + (dot(left[0], right[1]) + dot(left[1], right[0]))


def slot_terms(left, right, pos, neg):
    left, right = split(left), split(right)
    sig = jax.nn.sigmoid(product(left, right, ((1,), (1,))))
    grad = split(neg * sig - pos * (1.0 - sig))
    return product(grad, right, ((1,), (0,))), product(grad, left, ((0,), (0,)))


def call(kernel, name, out_shape, in_specs, args, cost, scratch=()):
    several = isinstance(out_shape, tuple)
    return pl.pallas_call(
        kernel,
        out_shape=out_shape,
        in_specs=in_specs,
        out_specs=(IN_VMEM,) * len(out_shape) if several else IN_VMEM,
        scratch_shapes=scratch,
        compiler_params=PARAMS,
        cost_estimate=pl.CostEstimate(flops=int(cost * 1e9), bytes_accessed=0, transcendentals=0),
        name=name,
    )(*args)


def in_hbm(x):
    return pltpu.with_memory_space_constraint(x, pltpu.HBM)


def note_rows(values):
    row = lax.broadcasted_iota(jnp.int32, (NOTE_ROWS, TILE), 0)
    note = jnp.zeros((NOTE_ROWS, TILE), jnp.int32)
    for n, value in enumerate(values):
        note = jnp.where(row == n, value, note)
    return note.astype(jnp.float32)


def stage_pairs(meta, vert, ctx, pos, neg, row_tiles):
    def kernel(meta_ref, vert_ref, ctx_ref, pos_ref, neg_ref, *refs):
        own_ref, vert_refs = refs[0], refs[1 : 1 + SUB]
        count_refs = refs[1 + SUB : -2]
        staged, sems = refs[-2:]
        odd = meta_ref[ODD_AT]
        copies = []
        for n, ref in enumerate((pos_ref, neg_ref)):
            copies.append(pltpu.make_async_copy(ref.at[0], staged.at[n], sems.at[n]))
        for s in range(SLOTS):
            rows = tile_rows(meta_ref[s * STEPS] % row_tiles)
            copies.append(pltpu.make_async_copy(ctx_ref.at[rows], own_ref.at[slot_rows(s)], sems.at[len(copies)]))
        for cls, out_ref in zip(CLASSES, vert_refs):
            for s in range(SLOTS):
                rows = tile_rows(meta_ref[s * STEPS + user_offset(cls, 0, odd)] // row_tiles)
                copies.append(pltpu.make_async_copy(vert_ref.at[rows], out_ref.at[slot_rows(s)], sems.at[len(copies)]))
        for copy in copies:
            copy.start()
        for copy in copies:
            copy.wait()
        for m, out_ref in enumerate(count_refs):
            k = user_offset(CLASSES[m % SUB], m // SUB, odd)
            for n in range(2):
                for s in range(SLOTS):
                    live = s < meta_ref[LIVE_AT + k]
                    out_ref[slot_rows(s, n), :] = jnp.where(live, staged[n, k, s].astype(jnp.float32), 0.0)
            out_ref[2 * PAIR_ROWS :, :] = note_rows([meta_ref[s * STEPS + k] % row_tiles for s in range(SLOTS)])

    n_copies = 2 + SLOTS * (1 + SUB)
    own, *rest = call(
        kernel,
        "stage",
        (PAIR,) * (1 + SUB) + (COUNTS,) * (2 * SUB),
        [IN_SMEM] + [IN_HBM] * 4,
        [meta, in_hbm(vert), in_hbm(ctx), in_hbm(pos), in_hbm(neg)],
        2,
        [pltpu.VMEM((2, STEPS, SLOTS, TILE, TILE), jnp.int32), pltpu.SemaphoreType.DMA((n_copies,))],
    )
    keys = [(cls, epoch) for epoch in range(2) for cls in CLASSES]
    return own, dict(zip(CLASSES, rest)), dict(zip(keys, rest[SUB:]))


def select_columns(meta, ctx, cls, row_tiles):
    def kernel(meta_ref, ctx_ref, out_ref):
        k = user_offset(cls, 0, meta_ref[ODD_AT])
        for s in range(SLOTS):
            out_ref[slot_rows(s), :] = ctx_ref[tile_rows(meta_ref[s * STEPS + k] % row_tiles), :]

    return call(kernel, f"select_{cls}", PAIR, [IN_SMEM, IN_VMEM], [meta, ctx], 1)


def pair_terms(rows, cols, counts, noted, name):
    def kernel(rows_ref, cols_ref, counts_ref, gv_ref, gc_ref):
        for s in range(SLOTS):
            gv_ref[slot_rows(s), :], gc_ref[slot_rows(s), :] = slot_terms(
                rows_ref[slot_rows(s), :],
                cols_ref[slot_rows(s), :],
                counts_ref[slot_rows(s), :],
                counts_ref[slot_rows(s, 1), :],
            )
        if noted:
            gc_ref[PAIR_ROWS:, :] = counts_ref[2 * PAIR_ROWS :, :]

    return call(kernel, name, (PAIR, NOTED if noted else PAIR), [IN_VMEM] * 3, [rows, cols, counts], 4)


def apply_vertex(meta, vert, grads, epoch, row_tiles):
    def kernel(meta_ref, vert_ref, *refs):
        grad_refs, out_ref, next_refs = refs[:SUB], refs[SUB], refs[SUB + 1 :]
        odd = meta_ref[ODD_AT]
        out_ref[...] = vert_ref[...]
        for cls, grad_ref in zip(CLASSES, grad_refs):
            for s in range(SLOTS):
                rows = tile_rows(meta_ref[s * STEPS + user_offset(cls, epoch, odd)] // row_tiles)
                out_ref[rows, :] -= RATES[epoch] * grad_ref[slot_rows(s), :]
        for cls, next_ref in zip(CLASSES, next_refs):
            for s in range(SLOTS):
                rows = tile_rows(meta_ref[s * STEPS + user_offset(cls, 1, odd)] // row_tiles)
                next_ref[slot_rows(s), :] = out_ref[rows, :]

    shapes = (jax.ShapeDtypeStruct(vert.shape, vert.dtype),) + (PAIR,) * (SUB if epoch == 0 else 0)
    args = [meta, vert] + [grads[cls] for cls in CLASSES]
    return call(kernel, f"vertex_{epoch}", shapes, [IN_SMEM] + [IN_VMEM] * (1 + SUB), args, 1)


def first_context(meta, ctx, grad, row_tiles):
    def kernel(meta_ref, ctx_ref, grad_ref, out_ref):
        out_ref[...] = ctx_ref[...]
        for s in range(SLOTS):
            out_ref[tile_rows(meta_ref[s * STEPS] % row_tiles), :] -= RATES[0] * grad_ref[slot_rows(s), :]

    shape = jax.ShapeDtypeStruct(ctx.shape, ctx.dtype)
    return call(kernel, "first_context", shape, [IN_SMEM] + [IN_VMEM] * 2, [meta, ctx, grad], 1)


def gather_context(near, ctx, grads, row_tiles):
    def kernel(near_ref, ctx_ref, *refs):
        grad_refs, out_ref, send_refs = refs[: SUB - 1], refs[SUB - 1], refs[SUB:]
        odd = near_ref[0, ODD_AT]
        tiles = []
        for grad_ref in grad_refs:
            for s in range(SLOTS):
                tiles.append(jnp.max(grad_ref[PAIR_ROWS + s : PAIR_ROWS + s + 1, :]).astype(jnp.int32))
        out_ref[...] = ctx_ref[...]
        for n, grad_ref in enumerate(grad_refs):
            for s in range(SLOTS):
                out_ref[tile_rows(tiles[n * SLOTS + s]), :] -= RATES[0] * grad_ref[slot_rows(s), :]
        for cls, send_ref in zip(CLASSES, send_refs):
            for s in range(SLOTS):
                tile = near_ref[cls, s * STEPS + owner_offset(cls, 1, odd)] % row_tiles
                send_ref[slot_rows(s), :] = out_ref[tile_rows(tile), :]

    shapes = (jax.ShapeDtypeStruct(ctx.shape, ctx.dtype),) + (PAIR,) * SUB
    return call(kernel, "gather_context", shapes, [IN_SMEM] + [IN_VMEM] * SUB, [near, ctx, *grads], 1)


def returned_context(near, ctx, grad, row_tiles):
    rows = ctx.shape[0]

    def kernel(near_ref, ctx_ref, grad_ref, out_ref):
        odd = near_ref[0, ODD_AT]
        out_ref[:rows, :] = ctx_ref[...]
        for s in range(SLOTS):
            tile = tile_rows(near_ref[0, s * STEPS + SUB] % row_tiles)
            out_ref[tile, :] -= RATES[1] * grad_ref[slot_rows(s), :]
        notes = []
        for cls in OTHERS:
            for s in range(SLOTS):
                notes.append(near_ref[cls, s * STEPS + owner_offset(cls, 1, odd)] % row_tiles)
        out_ref[rows:, :] = note_rows(notes)

    shape = jax.ShapeDtypeStruct((rows + NOTE_ROWS, TILE), ctx.dtype)
    return call(kernel, "returned_context", shape, [IN_SMEM] + [IN_VMEM] * 2, [near, ctx, grad], 1)


def last_context(notes, ctx, grads):
    rows = ctx.shape[0] - NOTE_ROWS

    def kernel(notes_ref, ctx_ref, *refs):
        *grad_refs, out_ref = refs
        out_ref[...] = ctx_ref[:rows, :]
        for n, grad_ref in enumerate(grad_refs):
            for s in range(SLOTS):
                out_ref[tile_rows(notes_ref[n * SLOTS + s]), :] -= RATES[1] * grad_ref[slot_rows(s), :]

    shape = jax.ShapeDtypeStruct((rows, TILE), ctx.dtype)
    return call(kernel, "last_context", shape, [IN_SMEM] + [IN_VMEM] * SUB, [notes, ctx, *grads], 1)


def per_device(vertex, context, tile_ids, live_tiles, pos_counts, neg_counts):
    row_tiles = vertex.shape[0] // TILE
    odd = (lax.axis_index("blk") & 1)[None]
    pad = jnp.zeros((META - ODD_AT - 1,), jnp.int32)
    meta = jnp.concatenate([jnp.swapaxes(tile_ids, 1, 2).reshape(-1), live_tiles.reshape(-1), odd, pad])

    ids = {0: meta}
    for cls in OTHERS:
        ids[cls] = to_owners(meta, cls)
    ids[3], ids[2], ids[1] = lax.optimization_barrier((ids[3], ids[2], ids[1]))
    own, rows, counts = stage_pairs(meta, vertex, context, pos_counts, neg_counts, row_tiles)
    cols = {cls: to_users(select_columns(ids[cls], context, cls, row_tiles), cls) for cls in OTHERS}
    gv, gc = {}, {}
    gv[0], gc[0] = pair_terms(rows[0], own, counts[0, 0], False, "terms_0_0")
    handed = to_users(first_context(meta, context, gc[0], row_tiles), 0, SUB)
    for cls in OTHERS:
        gv[cls], gc[cls] = pair_terms(rows[cls], cols[cls], counts[cls, 0], True, f"terms_0_{cls}")
        gc[cls] = to_users(gc[cls], cls)
    near = jnp.stack([ids[cls] for cls in range(SUB)])
    vert, *rows = apply_vertex(meta, vertex, gv, 0, row_tiles)
    ctx, *cols = gather_context(near, handed, [gc[cls] for cls in OTHERS], row_tiles)

    rows, cols = dict(zip(CLASSES, rows)), dict(zip(CLASSES, cols))
    cols.update({cls: to_users(cols[cls], cls) for cls in OTHERS})
    gv[0], gc[0] = pair_terms(rows[0], cols[0], counts[0, 1], False, "terms_1_0")
    back = to_owners(returned_context(near, ctx, gc[0], row_tiles), 0, SUB)
    notes = back[-NOTE_ROWS:, 0].astype(jnp.int32)
    for cls in OTHERS:
        gv[cls], grad = pair_terms(rows[cls], cols[cls], counts[cls, 1], False, f"terms_1_{cls}")
        gc[cls] = to_owners(grad, cls, SUB)
    (vert,) = apply_vertex(meta, vert, gv, 1, row_tiles)
    ctx = last_context(notes, back, [gc[cls] for cls in OTHERS])
    return vert, ctx


def solution(mesh):
    placed = (
        P(("ep", "blk"), None),
        P(("ep", "blk"), None),
        P(("ep", "blk"), None, None),
        P(("ep", "blk"), None),
        P(("ep", "blk"), None, None, None, None),
        P(("ep", "blk"), None, None, None, None),
    )
    return jax.shard_map(
        per_device,
        mesh=mesh,
        in_specs=placed,
        out_specs=(P(("ep", "blk"), None), P(("ep", "blk"), None)),
        check_vma=False,
    )
```

time: 237 us -> 100 us (0.42)
  the two profiles are of different devices: /device:TPU:66 before, /device:TPU:56 now
where the time goes in v2:
time: 100 us; the launch traced here: 99.4 us
  starting transfers between devices  63.1 us (63%)
  waiting for transfers between devices  19 us (19%)
  Pallas kernels  14.2 us (14%)
  local copies, waits for them, and re-layouts  1.88 us (2%)
    ppermute x7, starting transfers between devices, to_owners(): lax.ppermute(block, 'blk', [((j + ahead(j % SUB, cls) + extra) % size, j)...  37.2 us
    ppermute x10, starting transfers between devices, to_users(): lax.ppermute(block, 'blk', [(j, (j + ahead(j % SUB, cls) + extra) % size)...  25.9 us
    pallas_call x18, Pallas kernels, call(): pl.pallas_call(kernel, out_shape=out_shape, in_specs=in_specs, out_specs=...  14.2 us
    ppermute x10, waiting for transfers between devices, to_users(): lax.ppermute(block, 'blk', [(j, (j + ahead(j % SUB, cls) + extra) % size)...  10.6 us
    ppermute x7, waiting for transfers between devices, to_owners(): lax.ppermute(block, 'blk', [((j + ahead(j % SUB, cls) + extra) % size, j)...  8.38 us
  transfers between devices with their start and end apart: 17, of which 6 were waited for; matrix products, arithmetic and copies ran while one was open for 0% of the time, Pallas kernels for 12%

profile of v2, /device:TPU:56, one launch (start us, length us, event | category | flops | bytes accessed | tf_op | source)
XLA Modules:
  0.0 99.4 jit_solution(1510950910128749249)
XLA Ops:
  0.6 0.7 copy-done.3
  1.4 0.7 copy-done.2
  2.1 3.2 %collective-permute-start = (s32[32]{0:T(128)S(1)}, s32[32]{0:T(128)S(1)}, u32[]{:S(2)}, u32[]{:S(2)}) collective-permute-start(s32[32]{0:T(128)S(1)} %pad_add_fusion.1.meta_ref), channel_id=1, source_target_pairs={{1,0},{4,1},{3,2},{6,3},{5,4},{8,5},{7,6},{10,7},{9,8},{12,9},{11,... | collective-permute-start | bytes 392 | tf_op jit(solution)/shard_map/ppermute | solution.py:42
  5.4 4.0 %collective-permute-start.1 = (s32[32]{0:T(128)S(1)}, s32[32]{0:T(128)S(1)}, u32[]{:S(2)}, u32[]{:S(2)}) collective-permute-start(s32[32]{0:T(128)S(1)} %pad_add_fusion.1.meta_ref), channel_id=1, source_target_pairs={{2,0},{3,1},{4,2},{5,3},{6,4},{7,5},{8,6},{9,7},{10,8},{11,9},{12,... | collective-permute-start | bytes 392 | tf_op jit(solution)/shard_map/ppermute | solution.py:42
  9.4 11.3 %collective-permute-start.2 = (s32[32]{0:T(128)S(1)}, s32[32]{0:T(128)S(1)}, u32[]{:S(2)}, u32[]{:S(2)}) collective-permute-start(s32[32]{0:T(128)S(1)} %pad_add_fusion.1.meta_ref), channel_id=1, source_target_pairs={{3,0},{2,1},{5,2},{4,3},{7,4},{6,5},{9,6},{8,7},{11,8},{10,9},{13,... | collective-permute-start | bytes 392 | tf_op jit(solution)/shard_map/ppermute | solution.py:42
  20.7 2.5 %stage.1 = (f32[256,128]{1,0:T(8,128)S(1)}, f32[256,128]{1,0:T(8,128)S(1)}, f32[256,128]{1,0:T(8,128)S(1)}, f32[256,128]{1,0:T(8,128)S(1)}, f32[256,128]{1,0:T(8...) custom-call(s32[32]{0:T(128)S(1)} %pad_add_fusion.1.meta_ref, ...), custom_call_target="tpu_custom_call" | custom-call | flops 2000000000 | tf_op jit(solution)/shard_map/stage/pallas_call | solution.py:82
  24.2 0.6 first_context.1
  24.8 3.4 %collective-permute-start.6 = (f32[1024,128]{1,0:T(8,128)S(1)}, f32[1024,128]{1,0:T(8,128)S(1)}, u32[]{:S(2)}, u32[]{:S(2)}) collective-permute-start(f32[1024,128]{1,0:T(8,128)S(1)} %first_context.1), channel_id=1, source_target_pairs={{0,4},{1,5},{2,6},{3,7},{4,8},{5,9},{6,10},{7,11},{8,12},{9,13},{1... | collective-permute-start | bytes 1572872 | tf_op jit(solution)/shard_map/ppermute | solution.py:37
  28.8 1.9 %collective-permute-start.5 = (f32[256,128]{1,0:T(8,128)S(1)}, f32[256,128]{1,0:T(8,128)S(1)}, u32[]{:S(2)}, u32[]{:S(2)}) collective-permute-start(f32[256,128]{1,0:T(8,128)S(1)} %select_1.1), channel_id=1, source_target_pairs={{0,3},{1,2},{2,5},{3,4},{4,7},{5,6},{6,9},{7,8},{8,11},{9,10},{10,... | collective-permute-start | bytes 393224 | tf_op jit(solution)/shard_map/ppermute | solution.py:37
  31.3 2.6 %collective-permute-start.4 = (f32[256,128]{1,0:T(8,128)S(1)}, f32[256,128]{1,0:T(8,128)S(1)}, u32[]{:S(2)}, u32[]{:S(2)}) collective-permute-start(f32[256,128]{1,0:T(8,128)S(1)} %select_2.1), channel_id=1, source_target_pairs={{0,2},{1,3},{2,4},{3,5},{4,6},{5,7},{6,8},{7,9},{8,10},{9,11},{10,... | collective-permute-start | bytes 393224 | tf_op jit(solution)/shard_map/ppermute | solution.py:37
  34.5 1.9 %collective-permute-start.3 = (f32[256,128]{1,0:T(8,128)S(1)}, f32[256,128]{1,0:T(8,128)S(1)}, u32[]{:S(2)}, u32[]{:S(2)}) collective-permute-start(f32[256,128]{1,0:T(8,128)S(1)} %select_3.1), channel_id=1, source_target_pairs={{0,1},{1,4},{2,3},{3,6},{4,5},{5,8},{6,7},{7,10},{8,9},{9,12},{10,... | collective-permute-start | bytes 393224 | tf_op jit(solution)/shard_map/ppermute | solution.py:37
  36.4 2.3 %collective-permute-done.5.cols_ref = f32[256,128]{1,0:T(8,128)S(1)} collective-permute-done((f32[256,128]{1,0:T(8,128)S(1)}, f32[256,128]{1,0:T(8,128)S(1)}, u32[]{:S(2)}, u32[]{:S(2)}) %collective-permute-start.5) | collective-permute-done | bytes 131104 | tf_op jit(solution)/shard_map/ppermute | solution.py:37
  39.3 2.7 %collective-permute-start.9 = (f32[264,128]{1,0:T(8,128)S(1)}, f32[264,128]{1,0:T(8,128)S(1)}, u32[]{:S(2)}, u32[]{:S(2)}) collective-permute-start(f32[264,128]{1,0:T(8,128)S(1)} %get-tuple-element.65), channel_id=1, source_target_pairs={{0,3},{1,2},{2,5},{3,4},{4,7},{5,6},{6,9},{7,8},{8,11},{9,10},{10,... | collective-permute-start | bytes 405512 | tf_op jit(solution)/shard_map/ppermute | solution.py:37
  42.1 3.4 %collective-permute-done.4.cols_ref = f32[256,128]{1,0:T(8,128)S(1)} collective-permute-done((f32[256,128]{1,0:T(8,128)S(1)}, f32[256,128]{1,0:T(8,128)S(1)}, u32[]{:S(2)}, u32[]{:S(2)}) %collective-permute-start.4) | collective-permute-done | bytes 131104 | tf_op jit(solution)/shard_map/ppermute | solution.py:37
  46.0 2.0 %collective-permute-start.8 = (f32[264,128]{1,0:T(8,128)S(1)}, f32[264,128]{1,0:T(8,128)S(1)}, u32[]{:S(2)}, u32[]{:S(2)}) collective-permute-start(f32[264,128]{1,0:T(8,128)S(1)} %get-tuple-element.64), channel_id=1, source_target_pairs={{0,2},{1,3},{2,4},{3,5},{4,6},{5,7},{6,8},{7,9},{8,10},{9,11},{10,... | collective-permute-start | bytes 405512 | tf_op jit(solution)/shard_map/ppermute | solution.py:37
  48.6 2.7 %collective-permute-start.7 = (f32[264,128]{1,0:T(8,128)S(1)}, f32[264,128]{1,0:T(8,128)S(1)}, u32[]{:S(2)}, u32[]{:S(2)}) collective-permute-start(f32[264,128]{1,0:T(8,128)S(1)} %get-tuple-element.63), channel_id=1, source_target_pairs={{0,1},{1,4},{2,3},{3,6},{4,5},{5,8},{6,7},{7,10},{8,9},{9,12},{10,... | collective-permute-start | bytes 405512 | tf_op jit(solution)/shard_map/ppermute | solution.py:37
  51.3 0.7 vertex_0.1
  52.0 3.8 %collective-permute-done.8.refs_1_ = f32[264,128]{1,0:T(8,128)S(1)} collective-permute-done((f32[264,128]{1,0:T(8,128)S(1)}, f32[264,128]{1,0:T(8,128)S(1)}, u32[]{:S(2)}, u32[]{:S(2)}) %collective-permute-start.8) | collective-permute-done | bytes 135200 | tf_op jit(solution)/shard_map/ppermute | solution.py:37
  55.9 1.1 %collective-permute-done.7.refs_0_ = f32[264,128]{1,0:T(8,128)S(1)} collective-permute-done((f32[264,128]{1,0:T(8,128)S(1)}, f32[264,128]{1,0:T(8,128)S(1)}, u32[]{:S(2)}, u32[]{:S(2)}) %collective-permute-start.7) | collective-permute-done | bytes 135200 | tf_op jit(solution)/shard_map/ppermute | solution.py:37
  57.0 0.8 gather_context.1
  57.8 4.8 %collective-permute-start.12 = (f32[256,128]{1,0:T(8,128)S(1)}, f32[256,128]{1,0:T(8,128)S(1)}, u32[]{:S(2)}, u32[]{:S(2)}) collective-permute-start(f32[256,128]{1,0:T(8,128)S(1)} %get-tuple-element.74), channel_id=1, source_target_pairs={{0,3},{1,2},{2,5},{3,4},{4,7},{5,6},{6,9},{7,8},{8,11},{9,10},{10,... | collective-permute-start | bytes 393224 | tf_op jit(solution)/shard_map/ppermute | solution.py:37
  63.2 0.6 returned_context.1
  63.8 6.4 %collective-permute-start.13 = (f32[1032,128]{1,0:T(8,128)S(1)}, f32[1032,128]{1,0:T(8,128)S(1)}, u32[]{:S(2)}, u32[]{:S(2)}) collective-permute-start(f32[1032,128]{1,0:T(8,128)S(1)} %returned_context.1), channel_id=1, source_target_pairs={{4,0},{5,1},{6,2},{7,3},{8,4},{9,5},{10,6},{11,7},{12,8},{13,9},{1... | collective-permute-start | bytes 1585160 | tf_op jit(solution)/shard_map/ppermute | solution.py:42
  70.2 1.9 %collective-permute-start.11 = (f32[256,128]{1,0:T(8,128)S(1)}, f32[256,128]{1,0:T(8,128)S(1)}, u32[]{:S(2)}, u32[]{:S(2)}) collective-permute-start(f32[256,128]{1,0:T(8,128)S(1)} %get-tuple-element.70), channel_id=1, source_target_pairs={{0,2},{1,3},{2,4},{3,5},{4,6},{5,7},{6,8},{7,9},{8,10},{9,11},{10,... | collective-permute-start | bytes 393224 | tf_op jit(solution)/shard_map/ppermute | solution.py:37
  72.1 1.9 %collective-permute-start.10 = (f32[256,128]{1,0:T(8,128)S(1)}, f32[256,128]{1,0:T(8,128)S(1)}, u32[]{:S(2)}, u32[]{:S(2)}) collective-permute-start(f32[256,128]{1,0:T(8,128)S(1)} %get-tuple-element.66), channel_id=1, source_target_pairs={{0,1},{1,4},{2,3},{3,6},{4,5},{5,8},{6,7},{7,10},{8,9},{9,12},{10,... | collective-permute-start | bytes 393224 | tf_op jit(solution)/shard_map/ppermute | solution.py:37
  74.6 6.3 %collective-permute-start.16 = (f32[256,128]{1,0:T(8,128)S(1)}, f32[256,128]{1,0:T(8,128)S(1)}, u32[]{:S(2)}, u32[]{:S(2)}) collective-permute-start(f32[256,128]{1,0:T(8,128)S(1)} %get-tuple-element.85), channel_id=1, source_target_pairs={{7,0},{6,1},{9,2},{8,3},{11,4},{10,5},{13,6},{12,7},{15,8},{14,9},... | collective-permute-start | bytes 393224 | tf_op jit(solution)/shard_map/ppermute | solution.py:42
  81.6 1.9 %collective-permute-start.15 = (f32[256,128]{1,0:T(8,128)S(1)}, f32[256,128]{1,0:T(8,128)S(1)}, u32[]{:S(2)}, u32[]{:S(2)}) collective-permute-start(f32[256,128]{1,0:T(8,128)S(1)} %get-tuple-element.84), channel_id=1, source_target_pairs={{6,0},{7,1},{8,2},{9,3},{10,4},{11,5},{12,6},{13,7},{14,8},{15,9},... | collective-permute-start | bytes 393224 | tf_op jit(solution)/shard_map/ppermute | solution.py:42
  84.1 4.0 %collective-permute-start.14 = (f32[256,128]{1,0:T(8,128)S(1)}, f32[256,128]{1,0:T(8,128)S(1)}, u32[]{:S(2)}, u32[]{:S(2)}) collective-permute-start(f32[256,128]{1,0:T(8,128)S(1)} %get-tuple-element.83), channel_id=1, source_target_pairs={{5,0},{8,1},{7,2},{10,3},{9,4},{12,5},{11,6},{14,7},{13,8},{16,9},... | collective-permute-start | bytes 393224 | tf_op jit(solution)/shard_map/ppermute | solution.py:42
  88.0 1.4 %vertex_1.1 = f32[1024,128]{1,0:T(8,128)} custom-call(s32[32]{0:T(128)S(1)} %pad_add_fusion.1.meta_ref, f32[1024,128]{1,0:T(8,128)S(1)} %get-tuple-element.60.vert_ref, f32[256,128]{1,0:T(8,128)S(1)} %get-tuple-element.68.refs_0_, f32[256,128]{1,0:T(8,128)S(1)} %get-tuple-element.72.refs_1_, f32[256,128]{1,0:T(8,128)S(1)} %get-tuple-element.76.refs_2_, ...), custom_call_target="tpu_custom_call" | custom-call | flops 1000000000 | tf_op jit(solution)/shard_map/vertex_1/pallas_call | solution.py:82
  89.6 4.7 %collective-permute-done.15.refs_1_ = f32[256,128]{1,0:T(8,128)S(1)} collective-permute-done((f32[256,128]{1,0:T(8,128)S(1)}, f32[256,128]{1,0:T(8,128)S(1)}, u32[]{:S(2)}, u32[]{:S(2)}) %collective-permute-start.15) | collective-permute-done | bytes 131104 | tf_op jit(solution)/shard_map/ppermute | solution.py:42
  94.3 3.7 %collective-permute-done.14.refs_0_ = f32[256,128]{1,0:T(8,128)S(1)} collective-permute-done((f32[256,128]{1,0:T(8,128)S(1)}, f32[256,128]{1,0:T(8,128)S(1)}, u32[]{:S(2)}, u32[]{:S(2)}) %collective-permute-start.14) | collective-permute-done | bytes 131104 | tf_op jit(solution)/shard_map/ppermute | solution.py:42
  98.0 1.4 %last_context.1 = f32[1024,128]{1,0:T(8,128)} custom-call(s32[8]{0:T(128)S(1)} %fusion.notes_ref, f32[1032,128]{1,0:T(8,128)S(1)} %collective-permute-done.13.ctx_ref, f32[256,128]{1,0:T(8,128)S(1)} %collective-permute-done.14.refs_0_, f32[256,128]{1,0:T(8,128)S(1)} %collective-permute-done.15.refs_1_, f32[256,128]{1,0:T(8,128)S(1)} %collective-permute-done.16.refs_2_), custom_call_target="tpu_custom_call" | custom-call | flops 1000000000 | tf_op jit(solution)/shard_map/last_context/pallas_call | solution.py:82
  (33 shorter events, 7.0 us)
Async XLA Ops:
  0.6 0.7 copy-start.3
  1.4 0.7 copy-start.2
  2.1 26.1 %collective-permute-start = (s32[32]{0:T(128)S(1)}, s32[32]{0:T(128)S(1)}, u32[]{:S(2)}, u32[]{:S(2)}) collective-permute-start(s32[32]{0:T(128)S(1)} %pad_add_fusion.1.meta_ref), channel_id=1, source_target_pairs={{1,0},{4,1},{3,2},{6,3},{5,4},{8,5},{7,6},{10,7},{9,8},{12,9},{11,... | collective-permute-start | bytes 392 | tf_op jit(solution)/shard_map/ppermute | solution.py:42
  5.4 22.9 %collective-permute-start.1 = (s32[32]{0:T(128)S(1)}, s32[32]{0:T(128)S(1)}, u32[]{:S(2)}, u32[]{:S(2)}) collective-permute-start(s32[32]{0:T(128)S(1)} %pad_add_fusion.1.meta_ref), channel_id=1, source_target_pairs={{2,0},{3,1},{4,2},{5,3},{6,4},{7,5},{8,6},{9,7},{10,8},{11,9},{12,... | collective-permute-start | bytes 392 | tf_op jit(solution)/shard_map/ppermute | solution.py:42
  9.4 18.8 %collective-permute-start.2 = (s32[32]{0:T(128)S(1)}, s32[32]{0:T(128)S(1)}, u32[]{:S(2)}, u32[]{:S(2)}) collective-permute-start(s32[32]{0:T(128)S(1)} %pad_add_fusion.1.meta_ref), channel_id=1, source_target_pairs={{3,0},{2,1},{5,2},{4,3},{7,4},{6,5},{9,6},{8,7},{11,8},{10,9},{13,... | collective-permute-start | bytes 392 | tf_op jit(solution)/shard_map/ppermute | solution.py:42
  23.2 1.0 %copy-start = (f32[1024,128]{1,0:T(8,128)S(1)}, f32[1024,128]{1,0:T(8,128)}, u32[]{:S(2)}) copy-start(f32[1024,128]{1,0:T(8,128)} %ctx_ref.9) | copy-start | bytes 1572868
  24.8 32.1 %collective-permute-start.6 = (f32[1024,128]{1,0:T(8,128)S(1)}, f32[1024,128]{1,0:T(8,128)S(1)}, u32[]{:S(2)}, u32[]{:S(2)}) collective-permute-start(f32[1024,128]{1,0:T(8,128)S(1)} %first_context.1), channel_id=1, source_target_pairs={{0,4},{1,5},{2,6},{3,7},{4,8},{5,9},{6,10},{7,11},{8,12},{9,13},{1... | collective-permute-start | bytes 1572872 | tf_op jit(solution)/shard_map/ppermute | solution.py:37
  28.8 9.9 %collective-permute-start.5 = (f32[256,128]{1,0:T(8,128)S(1)}, f32[256,128]{1,0:T(8,128)S(1)}, u32[]{:S(2)}, u32[]{:S(2)}) collective-permute-start(f32[256,128]{1,0:T(8,128)S(1)} %select_1.1), channel_id=1, source_target_pairs={{0,3},{1,2},{2,5},{3,4},{4,7},{5,6},{6,9},{7,8},{8,11},{9,10},{10,... | collective-permute-start | bytes 393224 | tf_op jit(solution)/shard_map/ppermute | solution.py:37
  31.3 14.1 %collective-permute-start.4 = (f32[256,128]{1,0:T(8,128)S(1)}, f32[256,128]{1,0:T(8,128)S(1)}, u32[]{:S(2)}, u32[]{:S(2)}) collective-permute-start(f32[256,128]{1,0:T(8,128)S(1)} %select_2.1), channel_id=1, source_target_pairs={{0,2},{1,3},{2,4},{3,5},{4,6},{5,7},{6,8},{7,9},{8,10},{9,11},{10,... | collective-permute-start | bytes 393224 | tf_op jit(solution)/shard_map/ppermute | solution.py:37
  34.5 13.5 %collective-permute-start.3 = (f32[256,128]{1,0:T(8,128)S(1)}, f32[256,128]{1,0:T(8,128)S(1)}, u32[]{:S(2)}, u32[]{:S(2)}) collective-permute-start(f32[256,128]{1,0:T(8,128)S(1)} %select_3.1), channel_id=1, source_target_pairs={{0,1},{1,4},{2,3},{3,6},{4,5},{5,8},{6,7},{7,10},{8,9},{9,12},{10,... | collective-permute-start | bytes 393224 | tf_op jit(solution)/shard_map/ppermute | solution.py:37
  39.3 12.7 %collective-permute-start.9 = (f32[264,128]{1,0:T(8,128)S(1)}, f32[264,128]{1,0:T(8,128)S(1)}, u32[]{:S(2)}, u32[]{:S(2)}) collective-permute-start(f32[264,128]{1,0:T(8,128)S(1)} %get-tuple-element.65), channel_id=1, source_target_pairs={{0,3},{1,2},{2,5},{3,4},{4,7},{5,6},{6,9},{7,8},{8,11},{9,10},{10,... | collective-permute-start | bytes 405512 | tf_op jit(solution)/shard_map/ppermute | solution.py:37
  46.0 9.9 %collective-permute-start.8 = (f32[264,128]{1,0:T(8,128)S(1)}, f32[264,128]{1,0:T(8,128)S(1)}, u32[]{:S(2)}, u32[]{:S(2)}) collective-permute-start(f32[264,128]{1,0:T(8,128)S(1)} %get-tuple-element.64), channel_id=1, source_target_pairs={{0,2},{1,3},{2,4},{3,5},{4,6},{5,7},{6,8},{7,9},{8,10},{9,11},{10,... | collective-permute-start | bytes 405512 | tf_op jit(solution)/shard_map/ppermute | solution.py:37
  48.0 3.3 %copy-start.1 = (f32[1024,128]{1,0:T(8,128)S(1)}, f32[1024,128]{1,0:T(8,128)}, u32[]{:S(2)}) copy-start(f32[1024,128]{1,0:T(8,128)} %vert_ref.3) | copy-start | bytes 1572868
  48.6 8.4 %collective-permute-start.7 = (f32[264,128]{1,0:T(8,128)S(1)}, f32[264,128]{1,0:T(8,128)S(1)}, u32[]{:S(2)}, u32[]{:S(2)}) collective-permute-start(f32[264,128]{1,0:T(8,128)S(1)} %get-tuple-element.63), channel_id=1, source_target_pairs={{0,1},{1,4},{2,3},{3,6},{4,5},{5,8},{6,7},{7,10},{8,9},{9,12},{10,... | collective-permute-start | bytes 405512 | tf_op jit(solution)/shard_map/ppermute | solution.py:37
  57.8 16.3 %collective-permute-start.12 = (f32[256,128]{1,0:T(8,128)S(1)}, f32[256,128]{1,0:T(8,128)S(1)}, u32[]{:S(2)}, u32[]{:S(2)}) collective-permute-start(f32[256,128]{1,0:T(8,128)S(1)} %get-tuple-element.74), channel_id=1, source_target_pairs={{0,3},{1,2},{2,5},{3,4},{4,7},{5,6},{6,9},{7,8},{8,11},{9,10},{10,... | collective-permute-start | bytes 393224 | tf_op jit(solution)/shard_map/ppermute | solution.py:37
  63.8 25.7 %collective-permute-start.13 = (f32[1032,128]{1,0:T(8,128)S(1)}, f32[1032,128]{1,0:T(8,128)S(1)}, u32[]{:S(2)}, u32[]{:S(2)}) collective-permute-start(f32[1032,128]{1,0:T(8,128)S(1)} %returned_context.1), channel_id=1, source_target_pairs={{4,0},{5,1},{6,2},{7,3},{8,4},{9,5},{10,6},{11,7},{12,8},{13,9},{1... | collective-permute-start | bytes 1585160 | tf_op jit(solution)/shard_map/ppermute | solution.py:42
  70.2 10.8 %collective-permute-start.11 = (f32[256,128]{1,0:T(8,128)S(1)}, f32[256,128]{1,0:T(8,128)S(1)}, u32[]{:S(2)}, u32[]{:S(2)}) collective-permute-start(f32[256,128]{1,0:T(8,128)S(1)} %get-tuple-element.70), channel_id=1, source_target_pairs={{0,2},{1,3},{2,4},{3,5},{4,6},{5,7},{6,8},{7,9},{8,10},{9,11},{10,... | collective-permute-start | bytes 393224 | tf_op jit(solution)/shard_map/ppermute | solution.py:37
  72.1 11.3 %collective-permute-start.10 = (f32[256,128]{1,0:T(8,128)S(1)}, f32[256,128]{1,0:T(8,128)S(1)}, u32[]{:S(2)}, u32[]{:S(2)}) collective-permute-start(f32[256,128]{1,0:T(8,128)S(1)} %get-tuple-element.66), channel_id=1, source_target_pairs={{0,1},{1,4},{2,3},{3,6},{4,5},{5,8},{6,7},{7,10},{8,9},{9,12},{10,... | collective-permute-start | bytes 393224 | tf_op jit(solution)/shard_map/ppermute | solution.py:37
  74.6 14.9 %collective-permute-start.16 = (f32[256,128]{1,0:T(8,128)S(1)}, f32[256,128]{1,0:T(8,128)S(1)}, u32[]{:S(2)}, u32[]{:S(2)}) collective-permute-start(f32[256,128]{1,0:T(8,128)S(1)} %get-tuple-element.85), channel_id=1, source_target_pairs={{7,0},{6,1},{9,2},{8,3},{11,4},{10,5},{13,6},{12,7},{15,8},{14,9},... | collective-permute-start | bytes 393224 | tf_op jit(solution)/shard_map/ppermute | solution.py:42
  81.6 12.7 %collective-permute-start.15 = (f32[256,128]{1,0:T(8,128)S(1)}, f32[256,128]{1,0:T(8,128)S(1)}, u32[]{:S(2)}, u32[]{:S(2)}) collective-permute-start(f32[256,128]{1,0:T(8,128)S(1)} %get-tuple-element.84), channel_id=1, source_target_pairs={{6,0},{7,1},{8,2},{9,3},{10,4},{11,5},{12,6},{13,7},{14,8},{15,9},... | collective-permute-start | bytes 393224 | tf_op jit(solution)/shard_map/ppermute | solution.py:42
  84.1 13.9 %collective-permute-start.14 = (f32[256,128]{1,0:T(8,128)S(1)}, f32[256,128]{1,0:T(8,128)S(1)}, u32[]{:S(2)}, u32[]{:S(2)}) collective-permute-start(f32[256,128]{1,0:T(8,128)S(1)} %get-tuple-element.83), channel_id=1, source_target_pairs={{5,0},{8,1},{7,2},{10,3},{9,4},{12,5},{11,6},{14,7},{13,8},{16,9},... | collective-permute-start | bytes 393224 | tf_op jit(solution)/shard_map/ppermute | solution.py:42

commit v3 on v2

--- a/solution.py
+++ b/solution.py
@@ -14,8 +14,7 @@
 OTHERS = (3, 2, 1)
 PAIR_ROWS = SLOTS * TILE
 META = 32
-LIVE_AT = SLOTS * STEPS
-ODD_AT = LIVE_AT + STEPS
+ODD_AT = SLOTS * STEPS
 NOTE_ROWS = 8
 VMEM_BYTES = 8 * 1024 * 1024
 
@@ -103,8 +102,8 @@
     return note.astype(jnp.float32)
 
 
-def stage_pairs(meta, vert, ctx, pos, neg, row_tiles):
-    def kernel(meta_ref, vert_ref, ctx_ref, pos_ref, neg_ref, *refs):
+def stage_pairs(meta, live, vert, ctx, pos, neg, row_tiles):
+    def kernel(meta_ref, live_ref, vert_ref, ctx_ref, pos_ref, neg_ref, *refs):
         own_ref, vert_refs = refs[0], refs[1 : 1 + SUB]
         count_refs = refs[1 + SUB : -2]
         staged, sems = refs[-2:]
@@ -127,7 +126,7 @@
             k = user_offset(CLASSES[m % SUB], m // SUB, odd)
             for n in range(2):
                 for s in range(SLOTS):
-                    live = s < meta_ref[LIVE_AT + k]
+                    live = s < live_ref[0, k]
                     out_ref[slot_rows(s, n), :] = jnp.where(live, staged[n, k, s].astype(jnp.float32), 0.0)
             out_ref[2 * PAIR_ROWS :, :] = note_rows([meta_ref[s * STEPS + k] % row_tiles for s in range(SLOTS)])
 
@@ -136,8 +135,8 @@
         kernel,
         "stage",
         (PAIR,) * (1 + SUB) + (COUNTS,) * (2 * SUB),
-        [IN_SMEM] + [IN_HBM] * 4,
-        [meta, in_hbm(vert), in_hbm(ctx), in_hbm(pos), in_hbm(neg)],
+        [IN_SMEM] * 2 + [IN_HBM] * 4,
+        [meta, live, in_hbm(vert), in_hbm(ctx), in_hbm(pos), in_hbm(neg)],
         2,
         [pltpu.VMEM((2, STEPS, SLOTS, TILE, TILE), jnp.int32), pltpu.SemaphoreType.DMA((n_copies,))],
     )
@@ -256,13 +255,13 @@
     row_tiles = vertex.shape[0] // TILE
     odd = (lax.axis_index("blk") & 1)[None]
     pad = jnp.zeros((META - ODD_AT - 1,), jnp.int32)
-    meta = jnp.concatenate([jnp.swapaxes(tile_ids, 1, 2).reshape(-1), live_tiles.reshape(-1), odd, pad])
+    meta = jnp.concatenate([jnp.swapaxes(tile_ids, 1, 2).reshape(-1), odd, pad])
 
     ids = {0: meta}
     for cls in OTHERS:
         ids[cls] = to_owners(meta, cls)
     ids[3], ids[2], ids[1] = lax.optimization_barrier((ids[3], ids[2], ids[1]))
-    own, rows, counts = stage_pairs(meta, vertex, context, pos_counts, neg_counts, row_tiles)
+    own, rows, counts = stage_pairs(meta, live_tiles, vertex, context, pos_counts, neg_counts, row_tiles)
     cols = {cls: to_users(select_columns(ids[cls], context, cls, row_tiles), cls) for cls in OTHERS}
     gv, gc = {}, {}
     gv[0], gc[0] = pair_terms(rows[0], own, counts[0, 0], False, "terms_0_0")

time: 100 us -> 99.6 us (level)
  no operation moved by 1% of the time
where the time goes in v3:
time: 99.6 us; the launch traced here: 98.9 us
  starting transfers between devices  63.1 us (63%)
  waiting for transfers between devices  19.1 us (19%)
  Pallas kernels  14.2 us (14%)
  local copies, waits for them, and re-layouts  1.23 us (1%)
    ppermute x7, starting transfers between devices, to_owners(): lax.ppermute(block, 'blk', [((j + ahead(j % SUB, cls) + extra) % size, j)...  37.2 us
    ppermute x10, starting transfers between devices, to_users(): lax.ppermute(block, 'blk', [(j, (j + ahead(j % SUB, cls) + extra) % size)...  25.9 us
    pallas_call x18, Pallas kernels, call(): pl.pallas_call(kernel, out_shape=out_shape, in_specs=in_specs, out_specs=...  14.2 us
    ppermute x10, waiting for transfers between devices, to_users(): lax.ppermute(block, 'blk', [(j, (j + ahead(j % SUB, cls) + extra) % size)...  10.6 us
    ppermute x7, waiting for transfers between devices, to_owners(): lax.ppermute(block, 'blk', [((j + ahead(j % SUB, cls) + extra) % size, j)...  8.51 us
  transfers between devices with their start and end apart: 17, of which 6 were waited for; matrix products, arithmetic and copies ran while one was open for 0% of the time, Pallas kernels for 12%

profile of v3, /device:TPU:56, one launch (start us, length us, event | category | flops | bytes accessed | tf_op | source)
XLA Modules:
  0.0 98.9 jit_solution(13511243874798411912)
XLA Ops:
  0.6 0.7 copy-done.3
  1.5 3.2 %collective-permute-start = (s32[32]{0:T(128)S(1)}, s32[32]{0:T(128)S(1)}, u32[]{:S(2)}, u32[]{:S(2)}) collective-permute-start(s32[32]{0:T(128)S(1)} %pad_add_fusion.1.meta_ref), channel_id=1, source_target_pairs={{1,0},{4,1},{3,2},{6,3},{5,4},{8,5},{7,6},{10,7},{9,8},{12,9},{11,... | collective-permute-start | bytes 392 | tf_op jit(solution)/shard_map/ppermute | solution.py:41
  4.7 4.0 %collective-permute-start.1 = (s32[32]{0:T(128)S(1)}, s32[32]{0:T(128)S(1)}, u32[]{:S(2)}, u32[]{:S(2)}) collective-permute-start(s32[32]{0:T(128)S(1)} %pad_add_fusion.1.meta_ref), channel_id=1, source_target_pairs={{2,0},{3,1},{4,2},{5,3},{6,4},{7,5},{8,6},{9,7},{10,8},{11,9},{12,... | collective-permute-start | bytes 392 | tf_op jit(solution)/shard_map/ppermute | solution.py:41
  8.8 11.3 %collective-permute-start.2 = (s32[32]{0:T(128)S(1)}, s32[32]{0:T(128)S(1)}, u32[]{:S(2)}, u32[]{:S(2)}) collective-permute-start(s32[32]{0:T(128)S(1)} %pad_add_fusion.1.meta_ref), channel_id=1, source_target_pairs={{3,0},{2,1},{5,2},{4,3},{7,4},{6,5},{9,6},{8,7},{11,8},{10,9},{13,... | collective-permute-start | bytes 392 | tf_op jit(solution)/shard_map/ppermute | solution.py:41
  20.1 2.5 %stage.1 = (f32[256,128]{1,0:T(8,128)S(1)}, f32[256,128]{1,0:T(8,128)S(1)}, f32[256,128]{1,0:T(8,128)S(1)}, f32[256,128]{1,0:T(8,128)S(1)}, f32[256,128]{1,0:T(8...) custom-call(s32[32]{0:T(128)S(1)} %pad_add_fusion.1.meta_ref, ...), custom_call_target="tpu_custom_call" | custom-call | flops 2000000000 | tf_op jit(solution)/shard_map/stage/pallas_call | solution.py:81
  22.6 0.6 terms_0_0.1
  23.6 0.6 first_context.1
  24.2 3.4 %collective-permute-start.6 = (f32[1024,128]{1,0:T(8,128)S(1)}, f32[1024,128]{1,0:T(8,128)S(1)}, u32[]{:S(2)}, u32[]{:S(2)}) collective-permute-start(f32[1024,128]{1,0:T(8,128)S(1)} %first_context.1), channel_id=1, source_target_pairs={{0,4},{1,5},{2,6},{3,7},{4,8},{5,9},{6,10},{7,11},{8,12},{9,13},{1... | collective-permute-start | bytes 1572872 | tf_op jit(solution)/shard_map/ppermute | solution.py:36
  28.3 1.9 %collective-permute-start.5 = (f32[256,128]{1,0:T(8,128)S(1)}, f32[256,128]{1,0:T(8,128)S(1)}, u32[]{:S(2)}, u32[]{:S(2)}) collective-permute-start(f32[256,128]{1,0:T(8,128)S(1)} %select_1.1), channel_id=1, source_target_pairs={{0,3},{1,2},{2,5},{3,4},{4,7},{5,6},{6,9},{7,8},{8,11},{9,10},{10,... | collective-permute-start | bytes 393224 | tf_op jit(solution)/shard_map/ppermute | solution.py:36
  30.8 2.6 %collective-permute-start.4 = (f32[256,128]{1,0:T(8,128)S(1)}, f32[256,128]{1,0:T(8,128)S(1)}, u32[]{:S(2)}, u32[]{:S(2)}) collective-permute-start(f32[256,128]{1,0:T(8,128)S(1)} %select_2.1), channel_id=1, source_target_pairs={{0,2},{1,3},{2,4},{3,5},{4,6},{5,7},{6,8},{7,9},{8,10},{9,11},{10,... | collective-permute-start | bytes 393224 | tf_op jit(solution)/shard_map/ppermute | solution.py:36
  33.9 1.9 %collective-permute-start.3 = (f32[256,128]{1,0:T(8,128)S(1)}, f32[256,128]{1,0:T(8,128)S(1)}, u32[]{:S(2)}, u32[]{:S(2)}) collective-permute-start(f32[256,128]{1,0:T(8,128)S(1)} %select_3.1), channel_id=1, source_target_pairs={{0,1},{1,4},{2,3},{3,6},{4,5},{5,8},{6,7},{7,10},{8,9},{9,12},{10,... | collective-permute-start | bytes 393224 | tf_op jit(solution)/shard_map/ppermute | solution.py:36
  35.9 2.3 %collective-permute-done.5.cols_ref = f32[256,128]{1,0:T(8,128)S(1)} collective-permute-done((f32[256,128]{1,0:T(8,128)S(1)}, f32[256,128]{1,0:T(8,128)S(1)}, u32[]{:S(2)}, u32[]{:S(2)}) %collective-permute-start.5) | collective-permute-done | bytes 131104 | tf_op jit(solution)/shard_map/ppermute | solution.py:36
  38.7 2.7 %collective-permute-start.9 = (f32[264,128]{1,0:T(8,128)S(1)}, f32[264,128]{1,0:T(8,128)S(1)}, u32[]{:S(2)}, u32[]{:S(2)}) collective-permute-start(f32[264,128]{1,0:T(8,128)S(1)} %get-tuple-element.65), channel_id=1, source_target_pairs={{0,3},{1,2},{2,5},{3,4},{4,7},{5,6},{6,9},{7,8},{8,11},{9,10},{10,... | collective-permute-start | bytes 405512 | tf_op jit(solution)/shard_map/ppermute | solution.py:36
  41.5 3.3 %collective-permute-done.4.cols_ref = f32[256,128]{1,0:T(8,128)S(1)} collective-permute-done((f32[256,128]{1,0:T(8,128)S(1)}, f32[256,128]{1,0:T(8,128)S(1)}, u32[]{:S(2)}, u32[]{:S(2)}) %collective-permute-start.4) | collective-permute-done | bytes 131104 | tf_op jit(solution)/shard_map/ppermute | solution.py:36
  45.4 2.0 %collective-permute-start.8 = (f32[264,128]{1,0:T(8,128)S(1)}, f32[264,128]{1,0:T(8,128)S(1)}, u32[]{:S(2)}, u32[]{:S(2)}) collective-permute-start(f32[264,128]{1,0:T(8,128)S(1)} %get-tuple-element.64), channel_id=1, source_target_pairs={{0,2},{1,3},{2,4},{3,5},{4,6},{5,7},{6,8},{7,9},{8,10},{9,11},{10,... | collective-permute-start | bytes 405512 | tf_op jit(solution)/shard_map/ppermute | solution.py:36
  48.0 2.7 %collective-permute-start.7 = (f32[264,128]{1,0:T(8,128)S(1)}, f32[264,128]{1,0:T(8,128)S(1)}, u32[]{:S(2)}, u32[]{:S(2)}) collective-permute-start(f32[264,128]{1,0:T(8,128)S(1)} %get-tuple-element.63), channel_id=1, source_target_pairs={{0,1},{1,4},{2,3},{3,6},{4,5},{5,8},{6,7},{7,10},{8,9},{9,12},{10,... | collective-permute-start | bytes 405512 | tf_op jit(solution)/shard_map/ppermute | solution.py:36
  50.8 0.7 vertex_0.1
  51.5 3.8 %collective-permute-done.8.refs_1_ = f32[264,128]{1,0:T(8,128)S(1)} collective-permute-done((f32[264,128]{1,0:T(8,128)S(1)}, f32[264,128]{1,0:T(8,128)S(1)}, u32[]{:S(2)}, u32[]{:S(2)}) %collective-permute-start.8) | collective-permute-done | bytes 135200 | tf_op jit(solution)/shard_map/ppermute | solution.py:36
  55.3 1.1 %collective-permute-done.7.refs_0_ = f32[264,128]{1,0:T(8,128)S(1)} collective-permute-done((f32[264,128]{1,0:T(8,128)S(1)}, f32[264,128]{1,0:T(8,128)S(1)}, u32[]{:S(2)}, u32[]{:S(2)}) %collective-permute-start.7) | collective-permute-done | bytes 135200 | tf_op jit(solution)/shard_map/ppermute | solution.py:36
  56.4 0.8 gather_context.1
  57.2 4.8 %collective-permute-start.12 = (f32[256,128]{1,0:T(8,128)S(1)}, f32[256,128]{1,0:T(8,128)S(1)}, u32[]{:S(2)}, u32[]{:S(2)}) collective-permute-start(f32[256,128]{1,0:T(8,128)S(1)} %get-tuple-element.74), channel_id=1, source_target_pairs={{0,3},{1,2},{2,5},{3,4},{4,7},{5,6},{6,9},{7,8},{8,11},{9,10},{10,... | collective-permute-start | bytes 393224 | tf_op jit(solution)/shard_map/ppermute | solution.py:36
  62.6 0.6 returned_context.1
  63.2 6.4 %collective-permute-start.13 = (f32[1032,128]{1,0:T(8,128)S(1)}, f32[1032,128]{1,0:T(8,128)S(1)}, u32[]{:S(2)}, u32[]{:S(2)}) collective-permute-start(f32[1032,128]{1,0:T(8,128)S(1)} %returned_context.1), channel_id=1, source_target_pairs={{4,0},{5,1},{6,2},{7,3},{8,4},{9,5},{10,6},{11,7},{12,8},{13,9},{1... | collective-permute-start | bytes 1585160 | tf_op jit(solution)/shard_map/ppermute | solution.py:41
  69.6 1.9 %collective-permute-start.11 = (f32[256,128]{1,0:T(8,128)S(1)}, f32[256,128]{1,0:T(8,128)S(1)}, u32[]{:S(2)}, u32[]{:S(2)}) collective-permute-start(f32[256,128]{1,0:T(8,128)S(1)} %get-tuple-element.70), channel_id=1, source_target_pairs={{0,2},{1,3},{2,4},{3,5},{4,6},{5,7},{6,8},{7,9},{8,10},{9,11},{10,... | collective-permute-start | bytes 393224 | tf_op jit(solution)/shard_map/ppermute | solution.py:36
  71.6 1.9 %collective-permute-start.10 = (f32[256,128]{1,0:T(8,128)S(1)}, f32[256,128]{1,0:T(8,128)S(1)}, u32[]{:S(2)}, u32[]{:S(2)}) collective-permute-start(f32[256,128]{1,0:T(8,128)S(1)} %get-tuple-element.66), channel_id=1, source_target_pairs={{0,1},{1,4},{2,3},{3,6},{4,5},{5,8},{6,7},{7,10},{8,9},{9,12},{10,... | collective-permute-start | bytes 393224 | tf_op jit(solution)/shard_map/ppermute | solution.py:36
  74.1 6.3 %collective-permute-start.16 = (f32[256,128]{1,0:T(8,128)S(1)}, f32[256,128]{1,0:T(8,128)S(1)}, u32[]{:S(2)}, u32[]{:S(2)}) collective-permute-start(f32[256,128]{1,0:T(8,128)S(1)} %get-tuple-element.85), channel_id=1, source_target_pairs={{7,0},{6,1},{9,2},{8,3},{11,4},{10,5},{13,6},{12,7},{15,8},{14,9},... | collective-permute-start | bytes 393224 | tf_op jit(solution)/shard_map/ppermute | solution.py:41
  81.0 1.9 %collective-permute-start.15 = (f32[256,128]{1,0:T(8,128)S(1)}, f32[256,128]{1,0:T(8,128)S(1)}, u32[]{:S(2)}, u32[]{:S(2)}) collective-permute-start(f32[256,128]{1,0:T(8,128)S(1)} %get-tuple-element.84), channel_id=1, source_target_pairs={{6,0},{7,1},{8,2},{9,3},{10,4},{11,5},{12,6},{13,7},{14,8},{15,9},... | collective-permute-start | bytes 393224 | tf_op jit(solution)/shard_map/ppermute | solution.py:41
  83.5 4.0 %collective-permute-start.14 = (f32[256,128]{1,0:T(8,128)S(1)}, f32[256,128]{1,0:T(8,128)S(1)}, u32[]{:S(2)}, u32[]{:S(2)}) collective-permute-start(f32[256,128]{1,0:T(8,128)S(1)} %get-tuple-element.83), channel_id=1, source_target_pairs={{5,0},{8,1},{7,2},{10,3},{9,4},{12,5},{11,6},{14,7},{13,8},{16,9},... | collective-permute-start | bytes 393224 | tf_op jit(solution)/shard_map/ppermute | solution.py:41
  87.5 1.4 %vertex_1.1 = f32[1024,128]{1,0:T(8,128)} custom-call(s32[32]{0:T(128)S(1)} %pad_add_fusion.1.meta_ref, f32[1024,128]{1,0:T(8,128)S(1)} %get-tuple-element.60.vert_ref, f32[256,128]{1,0:T(8,128)S(1)} %get-tuple-element.68.refs_0_, f32[256,128]{1,0:T(8,128)S(1)} %get-tuple-element.72.refs_1_, f32[256,128]{1,0:T(8,128)S(1)} %get-tuple-element.76.refs_2_, ...), custom_call_target="tpu_custom_call" | custom-call | flops 1000000000 | tf_op jit(solution)/shard_map/vertex_1/pallas_call | solution.py:81
  89.0 4.7 %collective-permute-done.15.refs_1_ = f32[256,128]{1,0:T(8,128)S(1)} collective-permute-done((f32[256,128]{1,0:T(8,128)S(1)}, f32[256,128]{1,0:T(8,128)S(1)}, u32[]{:S(2)}, u32[]{:S(2)}) %collective-permute-start.15) | collective-permute-done | bytes 131104 | tf_op jit(solution)/shard_map/ppermute | solution.py:41
  93.7 3.8 %collective-permute-done.14.refs_0_ = f32[256,128]{1,0:T(8,128)S(1)} collective-permute-done((f32[256,128]{1,0:T(8,128)S(1)}, f32[256,128]{1,0:T(8,128)S(1)}, u32[]{:S(2)}, u32[]{:S(2)}) %collective-permute-start.14) | collective-permute-done | bytes 131104 | tf_op jit(solution)/shard_map/ppermute | solution.py:41
  97.5 1.4 %last_context.1 = f32[1024,128]{1,0:T(8,128)} custom-call(s32[8]{0:T(128)S(1)} %fusion.notes_ref, f32[1032,128]{1,0:T(8,128)S(1)} %collective-permute-done.13.ctx_ref, f32[256,128]{1,0:T(8,128)S(1)} %collective-permute-done.14.refs_0_, f32[256,128]{1,0:T(8,128)S(1)} %collective-permute-done.15.refs_1_, f32[256,128]{1,0:T(8,128)S(1)} %collective-permute-done.16.refs_2_), custom_call_target="tpu_custom_call" | custom-call | flops 1000000000 | tf_op jit(solution)/shard_map/last_context/pallas_call | solution.py:81
  (34 shorter events, 6.5 us)
Async XLA Ops:
  0.6 0.7 copy-start.3
  1.4 18.7 %copy-start.2 = (s32[1,8]{1,0:T(1,128)S(1)}, s32[1,8]{1,0:T(1,128)}, u32[]{:S(2)}) copy-start(s32[1,8]{1,0:T(1,128)} %live_ref.1) | copy-start | bytes 100
  1.5 26.2 %collective-permute-start = (s32[32]{0:T(128)S(1)}, s32[32]{0:T(128)S(1)}, u32[]{:S(2)}, u32[]{:S(2)}) collective-permute-start(s32[32]{0:T(128)S(1)} %pad_add_fusion.1.meta_ref), channel_id=1, source_target_pairs={{1,0},{4,1},{3,2},{6,3},{5,4},{8,5},{7,6},{10,7},{9,8},{12,9},{11,... | collective-permute-start | bytes 392 | tf_op jit(solution)/shard_map/ppermute | solution.py:41
  4.7 22.9 %collective-permute-start.1 = (s32[32]{0:T(128)S(1)}, s32[32]{0:T(128)S(1)}, u32[]{:S(2)}, u32[]{:S(2)}) collective-permute-start(s32[32]{0:T(128)S(1)} %pad_add_fusion.1.meta_ref), channel_id=1, source_target_pairs={{2,0},{3,1},{4,2},{5,3},{6,4},{7,5},{8,6},{9,7},{10,8},{11,9},{12,... | collective-permute-start | bytes 392 | tf_op jit(solution)/shard_map/ppermute | solution.py:41
  8.8 18.9 %collective-permute-start.2 = (s32[32]{0:T(128)S(1)}, s32[32]{0:T(128)S(1)}, u32[]{:S(2)}, u32[]{:S(2)}) collective-permute-start(s32[32]{0:T(128)S(1)} %pad_add_fusion.1.meta_ref), channel_id=1, source_target_pairs={{3,0},{2,1},{5,2},{4,3},{7,4},{6,5},{9,6},{8,7},{11,8},{10,9},{13,... | collective-permute-start | bytes 392 | tf_op jit(solution)/shard_map/ppermute | solution.py:41
  22.6 1.0 %copy-start = (f32[1024,128]{1,0:T(8,128)S(1)}, f32[1024,128]{1,0:T(8,128)}, u32[]{:S(2)}) copy-start(f32[1024,128]{1,0:T(8,128)} %ctx_ref.9) | copy-start | bytes 1572868
  24.2 32.2 %collective-permute-start.6 = (f32[1024,128]{1,0:T(8,128)S(1)}, f32[1024,128]{1,0:T(8,128)S(1)}, u32[]{:S(2)}, u32[]{:S(2)}) collective-permute-start(f32[1024,128]{1,0:T(8,128)S(1)} %first_context.1), channel_id=1, source_target_pairs={{0,4},{1,5},{2,6},{3,7},{4,8},{5,9},{6,10},{7,11},{8,12},{9,13},{1... | collective-permute-start | bytes 1572872 | tf_op jit(solution)/shard_map/ppermute | solution.py:36
  28.3 9.9 %collective-permute-start.5 = (f32[256,128]{1,0:T(8,128)S(1)}, f32[256,128]{1,0:T(8,128)S(1)}, u32[]{:S(2)}, u32[]{:S(2)}) collective-permute-start(f32[256,128]{1,0:T(8,128)S(1)} %select_1.1), channel_id=1, source_target_pairs={{0,3},{1,2},{2,5},{3,4},{4,7},{5,6},{6,9},{7,8},{8,11},{9,10},{10,... | collective-permute-start | bytes 393224 | tf_op jit(solution)/shard_map/ppermute | solution.py:36
  30.8 14.1 %collective-permute-start.4 = (f32[256,128]{1,0:T(8,128)S(1)}, f32[256,128]{1,0:T(8,128)S(1)}, u32[]{:S(2)}, u32[]{:S(2)}) collective-permute-start(f32[256,128]{1,0:T(8,128)S(1)} %select_2.1), channel_id=1, source_target_pairs={{0,2},{1,3},{2,4},{3,5},{4,6},{5,7},{6,8},{7,9},{8,10},{9,11},{10,... | collective-permute-start | bytes 393224 | tf_op jit(solution)/shard_map/ppermute | solution.py:36
  33.9 13.5 %collective-permute-start.3 = (f32[256,128]{1,0:T(8,128)S(1)}, f32[256,128]{1,0:T(8,128)S(1)}, u32[]{:S(2)}, u32[]{:S(2)}) collective-permute-start(f32[256,128]{1,0:T(8,128)S(1)} %select_3.1), channel_id=1, source_target_pairs={{0,1},{1,4},{2,3},{3,6},{4,5},{5,8},{6,7},{7,10},{8,9},{9,12},{10,... | collective-permute-start | bytes 393224 | tf_op jit(solution)/shard_map/ppermute | solution.py:36
  38.7 12.7 %collective-permute-start.9 = (f32[264,128]{1,0:T(8,128)S(1)}, f32[264,128]{1,0:T(8,128)S(1)}, u32[]{:S(2)}, u32[]{:S(2)}) collective-permute-start(f32[264,128]{1,0:T(8,128)S(1)} %get-tuple-element.65), channel_id=1, source_target_pairs={{0,3},{1,2},{2,5},{3,4},{4,7},{5,6},{6,9},{7,8},{8,11},{9,10},{10,... | collective-permute-start | bytes 405512 | tf_op jit(solution)/shard_map/ppermute | solution.py:36
  45.4 9.9 %collective-permute-start.8 = (f32[264,128]{1,0:T(8,128)S(1)}, f32[264,128]{1,0:T(8,128)S(1)}, u32[]{:S(2)}, u32[]{:S(2)}) collective-permute-start(f32[264,128]{1,0:T(8,128)S(1)} %get-tuple-element.64), channel_id=1, source_target_pairs={{0,2},{1,3},{2,4},{3,5},{4,6},{5,7},{6,8},{7,9},{8,10},{9,11},{10,... | collective-permute-start | bytes 405512 | tf_op jit(solution)/shard_map/ppermute | solution.py:36
  47.4 3.3 %copy-start.1 = (f32[1024,128]{1,0:T(8,128)S(1)}, f32[1024,128]{1,0:T(8,128)}, u32[]{:S(2)}) copy-start(f32[1024,128]{1,0:T(8,128)} %vert_ref.3) | copy-start | bytes 1572868
  48.0 8.4 %collective-permute-start.7 = (f32[264,128]{1,0:T(8,128)S(1)}, f32[264,128]{1,0:T(8,128)S(1)}, u32[]{:S(2)}, u32[]{:S(2)}) collective-permute-start(f32[264,128]{1,0:T(8,128)S(1)} %get-tuple-element.63), channel_id=1, source_target_pairs={{0,1},{1,4},{2,3},{3,6},{4,5},{5,8},{6,7},{7,10},{8,9},{9,12},{10,... | collective-permute-start | bytes 405512 | tf_op jit(solution)/shard_map/ppermute | solution.py:36
  57.2 16.3 %collective-permute-start.12 = (f32[256,128]{1,0:T(8,128)S(1)}, f32[256,128]{1,0:T(8,128)S(1)}, u32[]{:S(2)}, u32[]{:S(2)}) collective-permute-start(f32[256,128]{1,0:T(8,128)S(1)} %get-tuple-element.74), channel_id=1, source_target_pairs={{0,3},{1,2},{2,5},{3,4},{4,7},{5,6},{6,9},{7,8},{8,11},{9,10},{10,... | collective-permute-start | bytes 393224 | tf_op jit(solution)/shard_map/ppermute | solution.py:36
  63.2 25.7 %collective-permute-start.13 = (f32[1032,128]{1,0:T(8,128)S(1)}, f32[1032,128]{1,0:T(8,128)S(1)}, u32[]{:S(2)}, u32[]{:S(2)}) collective-permute-start(f32[1032,128]{1,0:T(8,128)S(1)} %returned_context.1), channel_id=1, source_target_pairs={{4,0},{5,1},{6,2},{7,3},{8,4},{9,5},{10,6},{11,7},{12,8},{13,9},{1... | collective-permute-start | bytes 1585160 | tf_op jit(solution)/shard_map/ppermute | solution.py:41
  69.6 10.8 %collective-permute-start.11 = (f32[256,128]{1,0:T(8,128)S(1)}, f32[256,128]{1,0:T(8,128)S(1)}, u32[]{:S(2)}, u32[]{:S(2)}) collective-permute-start(f32[256,128]{1,0:T(8,128)S(1)} %get-tuple-element.70), channel_id=1, source_target_pairs={{0,2},{1,3},{2,4},{3,5},{4,6},{5,7},{6,8},{7,9},{8,10},{9,11},{10,... | collective-permute-start | bytes 393224 | tf_op jit(solution)/shard_map/ppermute | solution.py:36
  71.6 11.4 %collective-permute-start.10 = (f32[256,128]{1,0:T(8,128)S(1)}, f32[256,128]{1,0:T(8,128)S(1)}, u32[]{:S(2)}, u32[]{:S(2)}) collective-permute-start(f32[256,128]{1,0:T(8,128)S(1)} %get-tuple-element.66), channel_id=1, source_target_pairs={{0,1},{1,4},{2,3},{3,6},{4,5},{5,8},{6,7},{7,10},{8,9},{9,12},{10,... | collective-permute-start | bytes 393224 | tf_op jit(solution)/shard_map/ppermute | solution.py:36
  74.1 15.0 %collective-permute-start.16 = (f32[256,128]{1,0:T(8,128)S(1)}, f32[256,128]{1,0:T(8,128)S(1)}, u32[]{:S(2)}, u32[]{:S(2)}) collective-permute-start(f32[256,128]{1,0:T(8,128)S(1)} %get-tuple-element.85), channel_id=1, source_target_pairs={{7,0},{6,1},{9,2},{8,3},{11,4},{10,5},{13,6},{12,7},{15,8},{14,9},... | collective-permute-start | bytes 393224 | tf_op jit(solution)/shard_map/ppermute | solution.py:41
  81.0 12.7 %collective-permute-start.15 = (f32[256,128]{1,0:T(8,128)S(1)}, f32[256,128]{1,0:T(8,128)S(1)}, u32[]{:S(2)}, u32[]{:S(2)}) collective-permute-start(f32[256,128]{1,0:T(8,128)S(1)} %get-tuple-element.84), channel_id=1, source_target_pairs={{6,0},{7,1},{8,2},{9,3},{10,4},{11,5},{12,6},{13,7},{14,8},{15,9},... | collective-permute-start | bytes 393224 | tf_op jit(solution)/shard_map/ppermute | solution.py:41
  83.5 14.0 %collective-permute-start.14 = (f32[256,128]{1,0:T(8,128)S(1)}, f32[256,128]{1,0:T(8,128)S(1)}, u32[]{:S(2)}, u32[]{:S(2)}) collective-permute-start(f32[256,128]{1,0:T(8,128)S(1)} %get-tuple-element.83), channel_id=1, source_target_pairs={{5,0},{8,1},{7,2},{10,3},{9,4},{12,5},{11,6},{14,7},{13,8},{16,9},... | collective-permute-start | bytes 393224 | tf_op jit(solution)/shard_map/ppermute | solution.py:41

commit v4 on v3

--- a/solution.py
+++ b/solution.py
@@ -187,14 +187,21 @@
     return call(kernel, f"vertex_{epoch}", shapes, [IN_SMEM] + [IN_VMEM] * (1 + SUB), args, 1)
 
 
-def first_context(meta, ctx, grad, row_tiles):
-    def kernel(meta_ref, ctx_ref, grad_ref, out_ref):
+def first_context(meta, ctx, rows, cols, counts, row_tiles):
+    def kernel(meta_ref, ctx_ref, rows_ref, cols_ref, counts_ref, gv_ref, out_ref):
         out_ref[...] = ctx_ref[...]
         for s in range(SLOTS):
-            out_ref[tile_rows(meta_ref[s * STEPS] % row_tiles), :] -= RATES[0] * grad_ref[slot_rows(s), :]
-
-    shape = jax.ShapeDtypeStruct(ctx.shape, ctx.dtype)
-    return call(kernel, "first_context", shape, [IN_SMEM] + [IN_VMEM] * 2, [meta, ctx, grad], 1)
+            gv_ref[slot_rows(s), :], grad = slot_terms(
+                rows_ref[slot_rows(s), :],
+                cols_ref[slot_rows(s), :],
+                counts_ref[slot_rows(s), :],
+                counts_ref[slot_rows(s, 1), :],
+            )
+            out_ref[tile_rows(meta_ref[s * STEPS] % row_tiles), :] -= RATES[0] * grad
+
+    shapes = (PAIR, jax.ShapeDtypeStruct(ctx.shape, ctx.dtype))
+    args = [meta, ctx, rows, cols, counts]
+    return call(kernel, "first_context", shapes, [IN_SMEM] + [IN_VMEM] * 4, args, 4)
 
 
 def gather_context(near, ctx, grads, row_tiles):
@@ -218,23 +225,29 @@
     return call(kernel, "gather_context", shapes, [IN_SMEM] + [IN_VMEM] * SUB, [near, ctx, *grads], 1)
 
 
-def returned_context(near, ctx, grad, row_tiles):
-    rows = ctx.shape[0]
-
-    def kernel(near_ref, ctx_ref, grad_ref, out_ref):
+def returned_context(near, ctx, rows, cols, counts, row_tiles):
+    n_rows = ctx.shape[0]
+
+    def kernel(near_ref, ctx_ref, rows_ref, cols_ref, counts_ref, gv_ref, out_ref):
         odd = near_ref[0, ODD_AT]
-        out_ref[:rows, :] = ctx_ref[...]
-        for s in range(SLOTS):
-            tile = tile_rows(near_ref[0, s * STEPS + SUB] % row_tiles)
-            out_ref[tile, :] -= RATES[1] * grad_ref[slot_rows(s), :]
+        out_ref[:n_rows, :] = ctx_ref[...]
+        for s in range(SLOTS):
+            gv_ref[slot_rows(s), :], grad = slot_terms(
+                rows_ref[slot_rows(s), :],
+                cols_ref[slot_rows(s), :],
+                counts_ref[slot_rows(s), :],
+                counts_ref[slot_rows(s, 1), :],
+            )
+            out_ref[tile_rows(near_ref[0, s * STEPS + SUB] % row_tiles), :] -= RATES[1] * grad
         notes = []
         for cls in OTHERS:
             for s in range(SLOTS):
                 notes.append(near_ref[cls, s * STEPS + owner_offset(cls, 1, odd)] % row_tiles)
-        out_ref[rows:, :] = note_rows(notes)
-
-    shape = jax.ShapeDtypeStruct((rows + NOTE_ROWS, TILE), ctx.dtype)
-    return call(kernel, "returned_context", shape, [IN_SMEM] + [IN_VMEM] * 2, [near, ctx, grad], 1)
+        out_ref[n_rows:, :] = note_rows(notes)
+
+    shapes = (PAIR, jax.ShapeDtypeStruct((n_rows + NOTE_ROWS, TILE), ctx.dtype))
+    args = [near, ctx, rows, cols, counts]
+    return call(kernel, "returned_context", shapes, [IN_SMEM] + [IN_VMEM] * 4, args, 4)
 
 
 def last_context(notes, ctx, grads):
@@ -264,8 +277,8 @@
     own, rows, counts = stage_pairs(meta, live_tiles, vertex, context, pos_counts, neg_counts, row_tiles)
     cols = {cls: to_users(select_columns(ids[cls], context, cls, row_tiles), cls) for cls in OTHERS}
     gv, gc = {}, {}
-    gv[0], gc[0] = pair_terms(rows[0], own, counts[0, 0], False, "terms_0_0")
-    handed = to_users(first_context(meta, context, gc[0], row_tiles), 0, SUB)
+    gv[0], handed = first_context(meta, context, rows[0], own, counts[0, 0], row_tiles)
+    handed = to_users(handed, 0, SUB)
     for cls in OTHERS:
         gv[cls], gc[cls] = pair_terms(rows[cls], cols[cls], counts[cls, 0], True, f"terms_0_{cls}")
         gc[cls] = to_users(gc[cls], cls)
@@ -275,8 +288,8 @@
 
     rows, cols = dict(zip(CLASSES, rows)), dict(zip(CLASSES, cols))
     cols.update({cls: to_users(cols[cls], cls) for cls in OTHERS})
-    gv[0], gc[0] = pair_terms(rows[0], cols[0], counts[0, 1], False, "terms_1_0")
-    back = to_owners(returned_context(near, ctx, gc[0], row_tiles), 0, SUB)
+    gv[0], back = returned_context(near, ctx, rows[0], cols[0], counts[0, 1], row_tiles)
+    back = to_owners(back, 0, SUB)
     notes = back[-NOTE_ROWS:, 0].astype(jnp.int32)
     for cls in OTHERS:
         gv[cls], grad = pair_terms(rows[cls], cols[cls], counts[cls, 1], False, f"terms_1_{cls}")

time: 99.6 us -> 99.2 us (level)
    pallas_call x18 -> x16, Pallas kernels: 14.2 us -> 14.1 us  [call(): pl.pallas_call(kernel, out_shape=out_shape, in_specs=in_specs, out_specs=...]
where the time goes in v4:
time: 99.2 us; the launch traced here: 98.5 us
  starting transfers between devices  63.2 us (64%)
  waiting for transfers between devices  19.1 us (19%)
  Pallas kernels  14.1 us (14%)
    ppermute x7, starting transfers between devices, to_owners(): lax.ppermute(block, 'blk', [((j + ahead(j % SUB, cls) + extra) % size, j)...  37.3 us
    ppermute x10, starting transfers between devices, to_users(): lax.ppermute(block, 'blk', [(j, (j + ahead(j % SUB, cls) + extra) % size)...  25.9 us
    pallas_call x16, Pallas kernels, call(): pl.pallas_call(kernel, out_shape=out_shape, in_specs=in_specs, out_specs=...  14.1 us
    ppermute x10, waiting for transfers between devices, to_users(): lax.ppermute(block, 'blk', [(j, (j + ahead(j % SUB, cls) + extra) % size)...  10.6 us
    ppermute x7, waiting for transfers between devices, to_owners(): lax.ppermute(block, 'blk', [((j + ahead(j % SUB, cls) + extra) % size, j)...  8.5 us
  transfers between devices with their start and end apart: 17, of which 6 were waited for; matrix products, arithmetic and copies ran while one was open for 0% of the time, Pallas kernels for 12%

profile of v4, /device:TPU:56, one launch (start us, length us, event | category | flops | bytes accessed | tf_op | source)
XLA Modules:
  0.0 98.5 jit_solution(18434400502498868375)
XLA Ops:
  0.6 0.7 copy-done.3
  1.5 3.4 %collective-permute-start = (s32[32]{0:T(128)S(1)}, s32[32]{0:T(128)S(1)}, u32[]{:S(2)}, u32[]{:S(2)}) collective-permute-start(s32[32]{0:T(128)S(1)} %pad_add_fusion.1.meta_ref), channel_id=1, source_target_pairs={{1,0},{4,1},{3,2},{6,3},{5,4},{8,5},{7,6},{10,7},{9,8},{12,9},{11,... | collective-permute-start | bytes 392 | tf_op jit(solution)/shard_map/ppermute | solution.py:41
  4.9 4.0 %collective-permute-start.1 = (s32[32]{0:T(128)S(1)}, s32[32]{0:T(128)S(1)}, u32[]{:S(2)}, u32[]{:S(2)}) collective-permute-start(s32[32]{0:T(128)S(1)} %pad_add_fusion.1.meta_ref), channel_id=1, source_target_pairs={{2,0},{3,1},{4,2},{5,3},{6,4},{7,5},{8,6},{9,7},{10,8},{11,9},{12,... | collective-permute-start | bytes 392 | tf_op jit(solution)/shard_map/ppermute | solution.py:41
  8.9 11.3 %collective-permute-start.2 = (s32[32]{0:T(128)S(1)}, s32[32]{0:T(128)S(1)}, u32[]{:S(2)}, u32[]{:S(2)}) collective-permute-start(s32[32]{0:T(128)S(1)} %pad_add_fusion.1.meta_ref), channel_id=1, source_target_pairs={{3,0},{2,1},{5,2},{4,3},{7,4},{6,5},{9,6},{8,7},{11,8},{10,9},{13,... | collective-permute-start | bytes 392 | tf_op jit(solution)/shard_map/ppermute | solution.py:41
  20.2 2.5 %stage.1 = (f32[256,128]{1,0:T(8,128)S(1)}, f32[256,128]{1,0:T(8,128)S(1)}, f32[256,128]{1,0:T(8,128)S(1)}, f32[256,128]{1,0:T(8,128)S(1)}, f32[256,128]{1,0:T(8...) custom-call(s32[32]{0:T(128)S(1)} %pad_add_fusion.1.meta_ref, ...), custom_call_target="tpu_custom_call" | custom-call | flops 2000000000 | tf_op jit(solution)/shard_map/stage/pallas_call | solution.py:81
  22.7 1.1 %first_context.1 = (f32[256,128]{1,0:T(8,128)S(1)}, f32[1024,128]{1,0:T(8,128)S(1)}) custom-call(s32[32]{0:T(128)S(1)} %pad_add_fusion.1.meta_ref, f32[1024,128]{1,0:T(8,128)S(1)} %copy-done, f32[256,128]{1,0:T(8,128)S(1)} %get-tuple-element.56.rows_ref, f32[256,128]{1,0:T(8,128)S(1)} %get-tuple-element.57.cols_ref, f32[520,128]{1,0:T(8,128)S(1)} %get-tuple-element.58.counts_ref), custom_call_target="tpu_custom_call" | custom-call | flops 4000000000 | tf_op jit(solution)/shard_map/first_context/pallas_call | solution.py:81
  23.8 3.4 %collective-permute-start.6 = (f32[1024,128]{1,0:T(8,128)S(1)}, f32[1024,128]{1,0:T(8,128)S(1)}, u32[]{:S(2)}, u32[]{:S(2)}) collective-permute-start(f32[1024,128]{1,0:T(8,128)S(1)} %get-tuple-element.62), channel_id=1, source_target_pairs={{0,4},{1,5},{2,6},{3,7},{4,8},{5,9},{6,10},{7,11},{8,12},{9,13},{1... | collective-permute-start | bytes 1572872 | tf_op jit(solution)/shard_map/ppermute | solution.py:36
  27.9 1.9 %collective-permute-start.5 = (f32[256,128]{1,0:T(8,128)S(1)}, f32[256,128]{1,0:T(8,128)S(1)}, u32[]{:S(2)}, u32[]{:S(2)}) collective-permute-start(f32[256,128]{1,0:T(8,128)S(1)} %select_1.1), channel_id=1, source_target_pairs={{0,3},{1,2},{2,5},{3,4},{4,7},{5,6},{6,9},{7,8},{8,11},{9,10},{10,... | collective-permute-start | bytes 393224 | tf_op jit(solution)/shard_map/ppermute | solution.py:36
  30.4 2.6 %collective-permute-start.4 = (f32[256,128]{1,0:T(8,128)S(1)}, f32[256,128]{1,0:T(8,128)S(1)}, u32[]{:S(2)}, u32[]{:S(2)}) collective-permute-start(f32[256,128]{1,0:T(8,128)S(1)} %select_2.1), channel_id=1, source_target_pairs={{0,2},{1,3},{2,4},{3,5},{4,6},{5,7},{6,8},{7,9},{8,10},{9,11},{10,... | collective-permute-start | bytes 393224 | tf_op jit(solution)/shard_map/ppermute | solution.py:36
  33.5 1.9 %collective-permute-start.3 = (f32[256,128]{1,0:T(8,128)S(1)}, f32[256,128]{1,0:T(8,128)S(1)}, u32[]{:S(2)}, u32[]{:S(2)}) collective-permute-start(f32[256,128]{1,0:T(8,128)S(1)} %select_3.1), channel_id=1, source_target_pairs={{0,1},{1,4},{2,3},{3,6},{4,5},{5,8},{6,7},{7,10},{8,9},{9,12},{10,... | collective-permute-start | bytes 393224 | tf_op jit(solution)/shard_map/ppermute | solution.py:36
  35.5 2.3 %collective-permute-done.5.cols_ref = f32[256,128]{1,0:T(8,128)S(1)} collective-permute-done((f32[256,128]{1,0:T(8,128)S(1)}, f32[256,128]{1,0:T(8,128)S(1)}, u32[]{:S(2)}, u32[]{:S(2)}) %collective-permute-start.5) | collective-permute-done | bytes 131104 | tf_op jit(solution)/shard_map/ppermute | solution.py:36
  38.4 2.7 %collective-permute-start.9 = (f32[264,128]{1,0:T(8,128)S(1)}, f32[264,128]{1,0:T(8,128)S(1)}, u32[]{:S(2)}, u32[]{:S(2)}) collective-permute-start(f32[264,128]{1,0:T(8,128)S(1)} %get-tuple-element.65), channel_id=1, source_target_pairs={{0,3},{1,2},{2,5},{3,4},{4,7},{5,6},{6,9},{7,8},{8,11},{9,10},{10,... | collective-permute-start | bytes 405512 | tf_op jit(solution)/shard_map/ppermute | solution.py:36
  41.1 3.3 %collective-permute-done.4.cols_ref = f32[256,128]{1,0:T(8,128)S(1)} collective-permute-done((f32[256,128]{1,0:T(8,128)S(1)}, f32[256,128]{1,0:T(8,128)S(1)}, u32[]{:S(2)}, u32[]{:S(2)}) %collective-permute-start.4) | collective-permute-done | bytes 131104 | tf_op jit(solution)/shard_map/ppermute | solution.py:36
  45.0 2.0 %collective-permute-start.8 = (f32[264,128]{1,0:T(8,128)S(1)}, f32[264,128]{1,0:T(8,128)S(1)}, u32[]{:S(2)}, u32[]{:S(2)}) collective-permute-start(f32[264,128]{1,0:T(8,128)S(1)} %get-tuple-element.64), channel_id=1, source_target_pairs={{0,2},{1,3},{2,4},{3,5},{4,6},{5,7},{6,8},{7,9},{8,10},{9,11},{10,... | collective-permute-start | bytes 405512 | tf_op jit(solution)/shard_map/ppermute | solution.py:36
  47.6 2.7 %collective-permute-start.7 = (f32[264,128]{1,0:T(8,128)S(1)}, f32[264,128]{1,0:T(8,128)S(1)}, u32[]{:S(2)}, u32[]{:S(2)}) collective-permute-start(f32[264,128]{1,0:T(8,128)S(1)} %get-tuple-element.63), channel_id=1, source_target_pairs={{0,1},{1,4},{2,3},{3,6},{4,5},{5,8},{6,7},{7,10},{8,9},{9,12},{10,... | collective-permute-start | bytes 405512 | tf_op jit(solution)/shard_map/ppermute | solution.py:36
  50.4 0.7 vertex_0.1
  51.1 3.8 %collective-permute-done.8.refs_1_ = f32[264,128]{1,0:T(8,128)S(1)} collective-permute-done((f32[264,128]{1,0:T(8,128)S(1)}, f32[264,128]{1,0:T(8,128)S(1)}, u32[]{:S(2)}, u32[]{:S(2)}) %collective-permute-start.8) | collective-permute-done | bytes 135200 | tf_op jit(solution)/shard_map/ppermute | solution.py:36
  54.9 1.1 %collective-permute-done.7.refs_0_ = f32[264,128]{1,0:T(8,128)S(1)} collective-permute-done((f32[264,128]{1,0:T(8,128)S(1)}, f32[264,128]{1,0:T(8,128)S(1)}, u32[]{:S(2)}, u32[]{:S(2)}) %collective-permute-start.7) | collective-permute-done | bytes 135200 | tf_op jit(solution)/shard_map/ppermute | solution.py:36
  56.0 0.8 gather_context.1
  56.8 4.8 %collective-permute-start.12 = (f32[256,128]{1,0:T(8,128)S(1)}, f32[256,128]{1,0:T(8,128)S(1)}, u32[]{:S(2)}, u32[]{:S(2)}) collective-permute-start(f32[256,128]{1,0:T(8,128)S(1)} %get-tuple-element.74), channel_id=1, source_target_pairs={{0,3},{1,2},{2,5},{3,4},{4,7},{5,6},{6,9},{7,8},{8,11},{9,10},{10,... | collective-permute-start | bytes 393224 | tf_op jit(solution)/shard_map/ppermute | solution.py:36
  61.6 1.1 %returned_context.1 = (f32[256,128]{1,0:T(8,128)S(1)}, f32[1032,128]{1,0:T(8,128)S(1)}) custom-call(s32[4,32]{1,0:T(4,128)S(1)} %pad_add_fusion.near_ref, f32[1024,128]{1,0:T(8,128)S(1)} %get-tuple-element.77.ctx_ref, f32[256,128]{1,0:T(8,128)S(1)} %get-tuple-element.78.rows_ref, f32[256,128]{1,0:T(8,128)S(1)} %get-tuple-element.79.cols_ref, ...), custom_call_target="tpu_custom_call" | custom-call | flops 4000000000 | tf_op jit(solution)/shard_map/returned_context/pallas_call | solution.py:81
  62.8 6.4 %collective-permute-start.13 = (f32[1032,128]{1,0:T(8,128)S(1)}, f32[1032,128]{1,0:T(8,128)S(1)}, u32[]{:S(2)}, u32[]{:S(2)}) collective-permute-start(f32[1032,128]{1,0:T(8,128)S(1)} %get-tuple-element.82), channel_id=1, source_target_pairs={{4,0},{5,1},{6,2},{7,3},{8,4},{9,5},{10,6},{11,7},{12,8},{13,9},{1... | collective-permute-start | bytes 1585160 | tf_op jit(solution)/shard_map/ppermute | solution.py:41
  69.2 1.9 %collective-permute-start.11 = (f32[256,128]{1,0:T(8,128)S(1)}, f32[256,128]{1,0:T(8,128)S(1)}, u32[]{:S(2)}, u32[]{:S(2)}) collective-permute-start(f32[256,128]{1,0:T(8,128)S(1)} %get-tuple-element.70), channel_id=1, source_target_pairs={{0,2},{1,3},{2,4},{3,5},{4,6},{5,7},{6,8},{7,9},{8,10},{9,11},{10,... | collective-permute-start | bytes 393224 | tf_op jit(solution)/shard_map/ppermute | solution.py:36
  71.1 1.9 %collective-permute-start.10 = (f32[256,128]{1,0:T(8,128)S(1)}, f32[256,128]{1,0:T(8,128)S(1)}, u32[]{:S(2)}, u32[]{:S(2)}) collective-permute-start(f32[256,128]{1,0:T(8,128)S(1)} %get-tuple-element.66), channel_id=1, source_target_pairs={{0,1},{1,4},{2,3},{3,6},{4,5},{5,8},{6,7},{7,10},{8,9},{9,12},{10,... | collective-permute-start | bytes 393224 | tf_op jit(solution)/shard_map/ppermute | solution.py:36
  73.6 6.3 %collective-permute-start.16 = (f32[256,128]{1,0:T(8,128)S(1)}, f32[256,128]{1,0:T(8,128)S(1)}, u32[]{:S(2)}, u32[]{:S(2)}) collective-permute-start(f32[256,128]{1,0:T(8,128)S(1)} %get-tuple-element.85), channel_id=1, source_target_pairs={{7,0},{6,1},{9,2},{8,3},{11,4},{10,5},{13,6},{12,7},{15,8},{14,9},... | collective-permute-start | bytes 393224 | tf_op jit(solution)/shard_map/ppermute | solution.py:41
  80.0 0.6 terms_1_2.1
  80.5 1.9 %collective-permute-start.15 = (f32[256,128]{1,0:T(8,128)S(1)}, f32[256,128]{1,0:T(8,128)S(1)}, u32[]{:S(2)}, u32[]{:S(2)}) collective-permute-start(f32[256,128]{1,0:T(8,128)S(1)} %get-tuple-element.84), channel_id=1, source_target_pairs={{6,0},{7,1},{8,2},{9,3},{10,4},{11,5},{12,6},{13,7},{14,8},{15,9},... | collective-permute-start | bytes 393224 | tf_op jit(solution)/shard_map/ppermute | solution.py:41
  83.1 4.0 %collective-permute-start.14 = (f32[256,128]{1,0:T(8,128)S(1)}, f32[256,128]{1,0:T(8,128)S(1)}, u32[]{:S(2)}, u32[]{:S(2)}) collective-permute-start(f32[256,128]{1,0:T(8,128)S(1)} %get-tuple-element.83), channel_id=1, source_target_pairs={{5,0},{8,1},{7,2},{10,3},{9,4},{12,5},{11,6},{14,7},{13,8},{16,9},... | collective-permute-start | bytes 393224 | tf_op jit(solution)/shard_map/ppermute | solution.py:41
  87.0 1.4 %vertex_1.1 = f32[1024,128]{1,0:T(8,128)} custom-call(s32[32]{0:T(128)S(1)} %pad_add_fusion.1.meta_ref, f32[1024,128]{1,0:T(8,128)S(1)} %get-tuple-element.60.vert_ref, f32[256,128]{1,0:T(8,128)S(1)} %get-tuple-element.68.refs_0_, f32[256,128]{1,0:T(8,128)S(1)} %get-tuple-element.72.refs_1_, f32[256,128]{1,0:T(8,128)S(1)} %get-tuple-element.76.refs_2_, ...), custom_call_target="tpu_custom_call" | custom-call | flops 1000000000 | tf_op jit(solution)/shard_map/vertex_1/pallas_call | solution.py:81
  88.6 4.7 %collective-permute-done.15.refs_1_ = f32[256,128]{1,0:T(8,128)S(1)} collective-permute-done((f32[256,128]{1,0:T(8,128)S(1)}, f32[256,128]{1,0:T(8,128)S(1)}, u32[]{:S(2)}, u32[]{:S(2)}) %collective-permute-start.15) | collective-permute-done | bytes 131104 | tf_op jit(solution)/shard_map/ppermute | solution.py:41
  93.3 3.8 %collective-permute-done.14.refs_0_ = f32[256,128]{1,0:T(8,128)S(1)} collective-permute-done((f32[256,128]{1,0:T(8,128)S(1)}, f32[256,128]{1,0:T(8,128)S(1)}, u32[]{:S(2)}, u32[]{:S(2)}) %collective-permute-start.14) | collective-permute-done | bytes 131104 | tf_op jit(solution)/shard_map/ppermute | solution.py:41
  97.1 1.4 %last_context.1 = f32[1024,128]{1,0:T(8,128)} custom-call(s32[8]{0:T(128)S(1)} %fusion.notes_ref, f32[1032,128]{1,0:T(8,128)S(1)} %collective-permute-done.13.ctx_ref, f32[256,128]{1,0:T(8,128)S(1)} %collective-permute-done.14.refs_0_, f32[256,128]{1,0:T(8,128)S(1)} %collective-permute-done.15.refs_1_, f32[256,128]{1,0:T(8,128)S(1)} %collective-permute-done.16.refs_2_), custom_call_target="tpu_custom_call" | custom-call | flops 1000000000 | tf_op jit(solution)/shard_map/last_context/pallas_call | solution.py:81
  (32 shorter events, 4.9 us)
Async XLA Ops:
  0.6 0.7 copy-start.3
  1.4 18.8 %copy-start.2 = (s32[1,8]{1,0:T(1,128)S(1)}, s32[1,8]{1,0:T(1,128)}, u32[]{:S(2)}) copy-start(s32[1,8]{1,0:T(1,128)} %live_ref.1) | copy-start | bytes 100
  1.5 21.2 %copy-start = (f32[1024,128]{1,0:T(8,128)S(1)}, f32[1024,128]{1,0:T(8,128)}, u32[]{:S(2)}) copy-start(f32[1024,128]{1,0:T(8,128)} %ctx_ref.9) | copy-start | bytes 1572868
  1.5 25.8 %collective-permute-start = (s32[32]{0:T(128)S(1)}, s32[32]{0:T(128)S(1)}, u32[]{:S(2)}, u32[]{:S(2)}) collective-permute-start(s32[32]{0:T(128)S(1)} %pad_add_fusion.1.meta_ref), channel_id=1, source_target_pairs={{1,0},{4,1},{3,2},{6,3},{5,4},{8,5},{7,6},{10,7},{9,8},{12,9},{11,... | collective-permute-start | bytes 392 | tf_op jit(solution)/shard_map/ppermute | solution.py:41
  4.9 22.4 %collective-permute-start.1 = (s32[32]{0:T(128)S(1)}, s32[32]{0:T(128)S(1)}, u32[]{:S(2)}, u32[]{:S(2)}) collective-permute-start(s32[32]{0:T(128)S(1)} %pad_add_fusion.1.meta_ref), channel_id=1, source_target_pairs={{2,0},{3,1},{4,2},{5,3},{6,4},{7,5},{8,6},{9,7},{10,8},{11,9},{12,... | collective-permute-start | bytes 392 | tf_op jit(solution)/shard_map/ppermute | solution.py:41
  8.9 18.4 %collective-permute-start.2 = (s32[32]{0:T(128)S(1)}, s32[32]{0:T(128)S(1)}, u32[]{:S(2)}, u32[]{:S(2)}) collective-permute-start(s32[32]{0:T(128)S(1)} %pad_add_fusion.1.meta_ref), channel_id=1, source_target_pairs={{3,0},{2,1},{5,2},{4,3},{7,4},{6,5},{9,6},{8,7},{11,8},{10,9},{13,... | collective-permute-start | bytes 392 | tf_op jit(solution)/shard_map/ppermute | solution.py:41
  23.8 32.2 %collective-permute-start.6 = (f32[1024,128]{1,0:T(8,128)S(1)}, f32[1024,128]{1,0:T(8,128)S(1)}, u32[]{:S(2)}, u32[]{:S(2)}) collective-permute-start(f32[1024,128]{1,0:T(8,128)S(1)} %get-tuple-element.62), channel_id=1, source_target_pairs={{0,4},{1,5},{2,6},{3,7},{4,8},{5,9},{6,10},{7,11},{8,12},{9,13},{1... | collective-permute-start | bytes 1572872 | tf_op jit(solution)/shard_map/ppermute | solution.py:36
  27.9 9.9 %collective-permute-start.5 = (f32[256,128]{1,0:T(8,128)S(1)}, f32[256,128]{1,0:T(8,128)S(1)}, u32[]{:S(2)}, u32[]{:S(2)}) collective-permute-start(f32[256,128]{1,0:T(8,128)S(1)} %select_1.1), channel_id=1, source_target_pairs={{0,3},{1,2},{2,5},{3,4},{4,7},{5,6},{6,9},{7,8},{8,11},{9,10},{10,... | collective-permute-start | bytes 393224 | tf_op jit(solution)/shard_map/ppermute | solution.py:36
  30.4 14.1 %collective-permute-start.4 = (f32[256,128]{1,0:T(8,128)S(1)}, f32[256,128]{1,0:T(8,128)S(1)}, u32[]{:S(2)}, u32[]{:S(2)}) collective-permute-start(f32[256,128]{1,0:T(8,128)S(1)} %select_2.1), channel_id=1, source_target_pairs={{0,2},{1,3},{2,4},{3,5},{4,6},{5,7},{6,8},{7,9},{8,10},{9,11},{10,... | collective-permute-start | bytes 393224 | tf_op jit(solution)/shard_map/ppermute | solution.py:36
  33.5 13.5 %collective-permute-start.3 = (f32[256,128]{1,0:T(8,128)S(1)}, f32[256,128]{1,0:T(8,128)S(1)}, u32[]{:S(2)}, u32[]{:S(2)}) collective-permute-start(f32[256,128]{1,0:T(8,128)S(1)} %select_3.1), channel_id=1, source_target_pairs={{0,1},{1,4},{2,3},{3,6},{4,5},{5,8},{6,7},{7,10},{8,9},{9,12},{10,... | collective-permute-start | bytes 393224 | tf_op jit(solution)/shard_map/ppermute | solution.py:36
  38.4 12.7 %collective-permute-start.9 = (f32[264,128]{1,0:T(8,128)S(1)}, f32[264,128]{1,0:T(8,128)S(1)}, u32[]{:S(2)}, u32[]{:S(2)}) collective-permute-start(f32[264,128]{1,0:T(8,128)S(1)} %get-tuple-element.65), channel_id=1, source_target_pairs={{0,3},{1,2},{2,5},{3,4},{4,7},{5,6},{6,9},{7,8},{8,11},{9,10},{10,... | collective-permute-start | bytes 405512 | tf_op jit(solution)/shard_map/ppermute | solution.py:36
  45.0 9.9 %collective-permute-start.8 = (f32[264,128]{1,0:T(8,128)S(1)}, f32[264,128]{1,0:T(8,128)S(1)}, u32[]{:S(2)}, u32[]{:S(2)}) collective-permute-start(f32[264,128]{1,0:T(8,128)S(1)} %get-tuple-element.64), channel_id=1, source_target_pairs={{0,2},{1,3},{2,4},{3,5},{4,6},{5,7},{6,8},{7,9},{8,10},{9,11},{10,... | collective-permute-start | bytes 405512 | tf_op jit(solution)/shard_map/ppermute | solution.py:36
  47.1 3.3 %copy-start.1 = (f32[1024,128]{1,0:T(8,128)S(1)}, f32[1024,128]{1,0:T(8,128)}, u32[]{:S(2)}) copy-start(f32[1024,128]{1,0:T(8,128)} %vert_ref.3) | copy-start | bytes 1572868
  47.6 8.4 %collective-permute-start.7 = (f32[264,128]{1,0:T(8,128)S(1)}, f32[264,128]{1,0:T(8,128)S(1)}, u32[]{:S(2)}, u32[]{:S(2)}) collective-permute-start(f32[264,128]{1,0:T(8,128)S(1)} %get-tuple-element.63), channel_id=1, source_target_pairs={{0,1},{1,4},{2,3},{3,6},{4,5},{5,8},{6,7},{7,10},{8,9},{9,12},{10,... | collective-permute-start | bytes 405512 | tf_op jit(solution)/shard_map/ppermute | solution.py:36
  56.8 16.2 %collective-permute-start.12 = (f32[256,128]{1,0:T(8,128)S(1)}, f32[256,128]{1,0:T(8,128)S(1)}, u32[]{:S(2)}, u32[]{:S(2)}) collective-permute-start(f32[256,128]{1,0:T(8,128)S(1)} %get-tuple-element.74), channel_id=1, source_target_pairs={{0,3},{1,2},{2,5},{3,4},{4,7},{5,6},{6,9},{7,8},{8,11},{9,10},{10,... | collective-permute-start | bytes 393224 | tf_op jit(solution)/shard_map/ppermute | solution.py:36
  62.8 25.7 %collective-permute-start.13 = (f32[1032,128]{1,0:T(8,128)S(1)}, f32[1032,128]{1,0:T(8,128)S(1)}, u32[]{:S(2)}, u32[]{:S(2)}) collective-permute-start(f32[1032,128]{1,0:T(8,128)S(1)} %get-tuple-element.82), channel_id=1, source_target_pairs={{4,0},{5,1},{6,2},{7,3},{8,4},{9,5},{10,6},{11,7},{12,8},{13,9},{1... | collective-permute-start | bytes 1585160 | tf_op jit(solution)/shard_map/ppermute | solution.py:41
  69.2 10.8 %collective-permute-start.11 = (f32[256,128]{1,0:T(8,128)S(1)}, f32[256,128]{1,0:T(8,128)S(1)}, u32[]{:S(2)}, u32[]{:S(2)}) collective-permute-start(f32[256,128]{1,0:T(8,128)S(1)} %get-tuple-element.70), channel_id=1, source_target_pairs={{0,2},{1,3},{2,4},{3,5},{4,6},{5,7},{6,8},{7,9},{8,10},{9,11},{10,... | collective-permute-start | bytes 393224 | tf_op jit(solution)/shard_map/ppermute | solution.py:36
  71.1 11.4 %collective-permute-start.10 = (f32[256,128]{1,0:T(8,128)S(1)}, f32[256,128]{1,0:T(8,128)S(1)}, u32[]{:S(2)}, u32[]{:S(2)}) collective-permute-start(f32[256,128]{1,0:T(8,128)S(1)} %get-tuple-element.66), channel_id=1, source_target_pairs={{0,1},{1,4},{2,3},{3,6},{4,5},{5,8},{6,7},{7,10},{8,9},{9,12},{10,... | collective-permute-start | bytes 393224 | tf_op jit(solution)/shard_map/ppermute | solution.py:36
  73.6 15.0 %collective-permute-start.16 = (f32[256,128]{1,0:T(8,128)S(1)}, f32[256,128]{1,0:T(8,128)S(1)}, u32[]{:S(2)}, u32[]{:S(2)}) collective-permute-start(f32[256,128]{1,0:T(8,128)S(1)} %get-tuple-element.85), channel_id=1, source_target_pairs={{7,0},{6,1},{9,2},{8,3},{11,4},{10,5},{13,6},{12,7},{15,8},{14,9},... | collective-permute-start | bytes 393224 | tf_op jit(solution)/shard_map/ppermute | solution.py:41
  80.5 12.7 %collective-permute-start.15 = (f32[256,128]{1,0:T(8,128)S(1)}, f32[256,128]{1,0:T(8,128)S(1)}, u32[]{:S(2)}, u32[]{:S(2)}) collective-permute-start(f32[256,128]{1,0:T(8,128)S(1)} %get-tuple-element.84), channel_id=1, source_target_pairs={{6,0},{7,1},{8,2},{9,3},{10,4},{11,5},{12,6},{13,7},{14,8},{15,9},... | collective-permute-start | bytes 393224 | tf_op jit(solution)/shard_map/ppermute | solution.py:41
  83.1 14.0 %collective-permute-start.14 = (f32[256,128]{1,0:T(8,128)S(1)}, f32[256,128]{1,0:T(8,128)S(1)}, u32[]{:S(2)}, u32[]{:S(2)}) collective-permute-start(f32[256,128]{1,0:T(8,128)S(1)} %get-tuple-element.83), channel_id=1, source_target_pairs={{5,0},{8,1},{7,2},{10,3},{9,4},{12,5},{11,6},{14,7},{13,8},{16,9},... | collective-permute-start | bytes 393224 | tf_op jit(solution)/shard_map/ppermute | solution.py:41

commit v5 on v4

--- a/solution.py
+++ b/solution.py
@@ -109,8 +109,10 @@
         staged, sems = refs[-2:]
         odd = meta_ref[ODD_AT]
         copies = []
-        for n, ref in enumerate((pos_ref, neg_ref)):
-            copies.append(pltpu.make_async_copy(ref.at[0], staged.at[n], sems.at[n]))
+        for half in range(2):
+            steps = pl.ds(SUB * half, SUB)
+            for n, ref in enumerate((pos_ref, neg_ref)):
+                copies.append(pltpu.make_async_copy(ref.at[0, steps], staged.at[n, steps], sems.at[len(copies)]))
         for s in range(SLOTS):
             rows = tile_rows(meta_ref[s * STEPS] % row_tiles)
             copies.append(pltpu.make_async_copy(ctx_ref.at[rows], own_ref.at[slot_rows(s)], sems.at[len(copies)]))
@@ -120,17 +122,20 @@
                 copies.append(pltpu.make_async_copy(vert_ref.at[rows], out_ref.at[slot_rows(s)], sems.at[len(copies)]))
         for copy in copies:
             copy.start()
-        for copy in copies:
-            copy.wait()
         for m, out_ref in enumerate(count_refs):
             k = user_offset(CLASSES[m % SUB], m // SUB, odd)
+            if m % SUB == 0:
+                for copy in copies[2 * (m // SUB) : 2 * (m // SUB) + 2]:
+                    copy.wait()
             for n in range(2):
                 for s in range(SLOTS):
                     live = s < live_ref[0, k]
                     out_ref[slot_rows(s, n), :] = jnp.where(live, staged[n, k, s].astype(jnp.float32), 0.0)
             out_ref[2 * PAIR_ROWS :, :] = note_rows([meta_ref[s * STEPS + k] % row_tiles for s in range(SLOTS)])
-
-    n_copies = 2 + SLOTS * (1 + SUB)
+        for copy in copies[4:]:
+            copy.wait()
+
+    n_copies = 4 + SLOTS * (1 + SUB)
     own, *rest = call(
         kernel,
         "stage",

time: 99.2 us -> 99 us (level)
  no operation moved by 1% of the time
where the time goes in v5:
time: 99 us; the launch traced here: 98.4 us
  starting transfers between devices  63.2 us (64%)
  waiting for transfers between devices  19.2 us (19%)
  Pallas kernels  14 us (14%)
    ppermute x7, starting transfers between devices, to_owners(): lax.ppermute(block, 'blk', [((j + ahead(j % SUB, cls) + extra) % size, j)...  37.3 us
    ppermute x10, starting transfers between devices, to_users(): lax.ppermute(block, 'blk', [(j, (j + ahead(j % SUB, cls) + extra) % size)...  25.9 us
    pallas_call x16, Pallas kernels, call(): pl.pallas_call(kernel, out_shape=out_shape, in_specs=in_specs, out_specs=...  14 us
    ppermute x10, waiting for transfers between devices, to_users(): lax.ppermute(block, 'blk', [(j, (j + ahead(j % SUB, cls) + extra) % size)...  10.7 us
    ppermute x7, waiting for transfers between devices, to_owners(): lax.ppermute(block, 'blk', [((j + ahead(j % SUB, cls) + extra) % size, j)...  8.51 us
  transfers between devices with their start and end apart: 17, of which 6 were waited for; matrix products, arithmetic and copies ran while one was open for 0% of the time, Pallas kernels for 12%

profile of v5, /device:TPU:56, one launch (start us, length us, event | category | flops | bytes accessed | tf_op | source)
XLA Modules:
  0.0 98.4 jit_solution(12887897983214471047)
XLA Ops:
  0.6 0.7 copy-done.3
  1.5 3.4 %collective-permute-start = (s32[32]{0:T(128)S(1)}, s32[32]{0:T(128)S(1)}, u32[]{:S(2)}, u32[]{:S(2)}) collective-permute-start(s32[32]{0:T(128)S(1)} %pad_add_fusion.1.meta_ref), channel_id=1, source_target_pairs={{1,0},{4,1},{3,2},{6,3},{5,4},{8,5},{7,6},{10,7},{9,8},{12,9},{11,... | collective-permute-start | bytes 392 | tf_op jit(solution)/shard_map/ppermute | solution.py:41
  4.9 4.0 %collective-permute-start.1 = (s32[32]{0:T(128)S(1)}, s32[32]{0:T(128)S(1)}, u32[]{:S(2)}, u32[]{:S(2)}) collective-permute-start(s32[32]{0:T(128)S(1)} %pad_add_fusion.1.meta_ref), channel_id=1, source_target_pairs={{2,0},{3,1},{4,2},{5,3},{6,4},{7,5},{8,6},{9,7},{10,8},{11,9},{12,... | collective-permute-start | bytes 392 | tf_op jit(solution)/shard_map/ppermute | solution.py:41
  8.9 11.3 %collective-permute-start.2 = (s32[32]{0:T(128)S(1)}, s32[32]{0:T(128)S(1)}, u32[]{:S(2)}, u32[]{:S(2)}) collective-permute-start(s32[32]{0:T(128)S(1)} %pad_add_fusion.1.meta_ref), channel_id=1, source_target_pairs={{3,0},{2,1},{5,2},{4,3},{7,4},{6,5},{9,6},{8,7},{11,8},{10,9},{13,... | collective-permute-start | bytes 392 | tf_op jit(solution)/shard_map/ppermute | solution.py:41
  20.2 2.3 %stage.1 = (f32[256,128]{1,0:T(8,128)S(1)}, f32[256,128]{1,0:T(8,128)S(1)}, f32[256,128]{1,0:T(8,128)S(1)}, f32[256,128]{1,0:T(8,128)S(1)}, f32[256,128]{1,0:T(8...) custom-call(s32[32]{0:T(128)S(1)} %pad_add_fusion.1.meta_ref, ...), custom_call_target="tpu_custom_call" | custom-call | flops 2000000000 | tf_op jit(solution)/shard_map/stage/pallas_call | solution.py:81
  22.6 1.1 %first_context.1 = (f32[256,128]{1,0:T(8,128)S(1)}, f32[1024,128]{1,0:T(8,128)S(1)}) custom-call(s32[32]{0:T(128)S(1)} %pad_add_fusion.1.meta_ref, f32[1024,128]{1,0:T(8,128)S(1)} %copy-done, f32[256,128]{1,0:T(8,128)S(1)} %get-tuple-element.56.rows_ref, f32[256,128]{1,0:T(8,128)S(1)} %get-tuple-element.57.cols_ref, f32[520,128]{1,0:T(8,128)S(1)} %get-tuple-element.58.counts_ref), custom_call_target="tpu_custom_call" | custom-call | flops 4000000000 | tf_op jit(solution)/shard_map/first_context/pallas_call | solution.py:81
  23.7 3.4 %collective-permute-start.6 = (f32[1024,128]{1,0:T(8,128)S(1)}, f32[1024,128]{1,0:T(8,128)S(1)}, u32[]{:S(2)}, u32[]{:S(2)}) collective-permute-start(f32[1024,128]{1,0:T(8,128)S(1)} %get-tuple-element.62), channel_id=1, source_target_pairs={{0,4},{1,5},{2,6},{3,7},{4,8},{5,9},{6,10},{7,11},{8,12},{9,13},{1... | collective-permute-start | bytes 1572872 | tf_op jit(solution)/shard_map/ppermute | solution.py:36
  27.8 1.9 %collective-permute-start.5 = (f32[256,128]{1,0:T(8,128)S(1)}, f32[256,128]{1,0:T(8,128)S(1)}, u32[]{:S(2)}, u32[]{:S(2)}) collective-permute-start(f32[256,128]{1,0:T(8,128)S(1)} %select_1.1), channel_id=1, source_target_pairs={{0,3},{1,2},{2,5},{3,4},{4,7},{5,6},{6,9},{7,8},{8,11},{9,10},{10,... | collective-permute-start | bytes 393224 | tf_op jit(solution)/shard_map/ppermute | solution.py:36
  30.2 2.6 %collective-permute-start.4 = (f32[256,128]{1,0:T(8,128)S(1)}, f32[256,128]{1,0:T(8,128)S(1)}, u32[]{:S(2)}, u32[]{:S(2)}) collective-permute-start(f32[256,128]{1,0:T(8,128)S(1)} %select_2.1), channel_id=1, source_target_pairs={{0,2},{1,3},{2,4},{3,5},{4,6},{5,7},{6,8},{7,9},{8,10},{9,11},{10,... | collective-permute-start | bytes 393224 | tf_op jit(solution)/shard_map/ppermute | solution.py:36
  33.4 1.9 %collective-permute-start.3 = (f32[256,128]{1,0:T(8,128)S(1)}, f32[256,128]{1,0:T(8,128)S(1)}, u32[]{:S(2)}, u32[]{:S(2)}) collective-permute-start(f32[256,128]{1,0:T(8,128)S(1)} %select_3.1), channel_id=1, source_target_pairs={{0,1},{1,4},{2,3},{3,6},{4,5},{5,8},{6,7},{7,10},{8,9},{9,12},{10,... | collective-permute-start | bytes 393224 | tf_op jit(solution)/shard_map/ppermute | solution.py:36
  35.3 2.4 %collective-permute-done.5.cols_ref = f32[256,128]{1,0:T(8,128)S(1)} collective-permute-done((f32[256,128]{1,0:T(8,128)S(1)}, f32[256,128]{1,0:T(8,128)S(1)}, u32[]{:S(2)}, u32[]{:S(2)}) %collective-permute-start.5) | collective-permute-done | bytes 131104 | tf_op jit(solution)/shard_map/ppermute | solution.py:36
  38.3 2.7 %collective-permute-start.9 = (f32[264,128]{1,0:T(8,128)S(1)}, f32[264,128]{1,0:T(8,128)S(1)}, u32[]{:S(2)}, u32[]{:S(2)}) collective-permute-start(f32[264,128]{1,0:T(8,128)S(1)} %get-tuple-element.65), channel_id=1, source_target_pairs={{0,3},{1,2},{2,5},{3,4},{4,7},{5,6},{6,9},{7,8},{8,11},{9,10},{10,... | collective-permute-start | bytes 405512 | tf_op jit(solution)/shard_map/ppermute | solution.py:36
  41.0 3.3 %collective-permute-done.4.cols_ref = f32[256,128]{1,0:T(8,128)S(1)} collective-permute-done((f32[256,128]{1,0:T(8,128)S(1)}, f32[256,128]{1,0:T(8,128)S(1)}, u32[]{:S(2)}, u32[]{:S(2)}) %collective-permute-start.4) | collective-permute-done | bytes 131104 | tf_op jit(solution)/shard_map/ppermute | solution.py:36
  44.9 2.0 %collective-permute-start.8 = (f32[264,128]{1,0:T(8,128)S(1)}, f32[264,128]{1,0:T(8,128)S(1)}, u32[]{:S(2)}, u32[]{:S(2)}) collective-permute-start(f32[264,128]{1,0:T(8,128)S(1)} %get-tuple-element.64), channel_id=1, source_target_pairs={{0,2},{1,3},{2,4},{3,5},{4,6},{5,7},{6,8},{7,9},{8,10},{9,11},{10,... | collective-permute-start | bytes 405512 | tf_op jit(solution)/shard_map/ppermute | solution.py:36
  47.5 2.7 %collective-permute-start.7 = (f32[264,128]{1,0:T(8,128)S(1)}, f32[264,128]{1,0:T(8,128)S(1)}, u32[]{:S(2)}, u32[]{:S(2)}) collective-permute-start(f32[264,128]{1,0:T(8,128)S(1)} %get-tuple-element.63), channel_id=1, source_target_pairs={{0,1},{1,4},{2,3},{3,6},{4,5},{5,8},{6,7},{7,10},{8,9},{9,12},{10,... | collective-permute-start | bytes 405512 | tf_op jit(solution)/shard_map/ppermute | solution.py:36
  50.2 0.7 vertex_0.1
  50.9 3.8 %collective-permute-done.8.refs_1_ = f32[264,128]{1,0:T(8,128)S(1)} collective-permute-done((f32[264,128]{1,0:T(8,128)S(1)}, f32[264,128]{1,0:T(8,128)S(1)}, u32[]{:S(2)}, u32[]{:S(2)}) %collective-permute-start.8) | collective-permute-done | bytes 135200 | tf_op jit(solution)/shard_map/ppermute | solution.py:36
  54.8 1.1 %collective-permute-done.7.refs_0_ = f32[264,128]{1,0:T(8,128)S(1)} collective-permute-done((f32[264,128]{1,0:T(8,128)S(1)}, f32[264,128]{1,0:T(8,128)S(1)}, u32[]{:S(2)}, u32[]{:S(2)}) %collective-permute-start.7) | collective-permute-done | bytes 135200 | tf_op jit(solution)/shard_map/ppermute | solution.py:36
  55.9 0.8 gather_context.1
  56.7 4.8 %collective-permute-start.12 = (f32[256,128]{1,0:T(8,128)S(1)}, f32[256,128]{1,0:T(8,128)S(1)}, u32[]{:S(2)}, u32[]{:S(2)}) collective-permute-start(f32[256,128]{1,0:T(8,128)S(1)} %get-tuple-element.74), channel_id=1, source_target_pairs={{0,3},{1,2},{2,5},{3,4},{4,7},{5,6},{6,9},{7,8},{8,11},{9,10},{10,... | collective-permute-start | bytes 393224 | tf_op jit(solution)/shard_map/ppermute | solution.py:36
  61.5 1.1 %returned_context.1 = (f32[256,128]{1,0:T(8,128)S(1)}, f32[1032,128]{1,0:T(8,128)S(1)}) custom-call(s32[4,32]{1,0:T(4,128)S(1)} %pad_add_fusion.near_ref, f32[1024,128]{1,0:T(8,128)S(1)} %get-tuple-element.77.ctx_ref, f32[256,128]{1,0:T(8,128)S(1)} %get-tuple-element.78.rows_ref, f32[256,128]{1,0:T(8,128)S(1)} %get-tuple-element.79.cols_ref, ...), custom_call_target="tpu_custom_call" | custom-call | flops 4000000000 | tf_op jit(solution)/shard_map/returned_context/pallas_call | solution.py:81
  62.7 6.4 %collective-permute-start.13 = (f32[1032,128]{1,0:T(8,128)S(1)}, f32[1032,128]{1,0:T(8,128)S(1)}, u32[]{:S(2)}, u32[]{:S(2)}) collective-permute-start(f32[1032,128]{1,0:T(8,128)S(1)} %get-tuple-element.82), channel_id=1, source_target_pairs={{4,0},{5,1},{6,2},{7,3},{8,4},{9,5},{10,6},{11,7},{12,8},{13,9},{1... | collective-permute-start | bytes 1585160 | tf_op jit(solution)/shard_map/ppermute | solution.py:41
  69.0 1.9 %collective-permute-start.11 = (f32[256,128]{1,0:T(8,128)S(1)}, f32[256,128]{1,0:T(8,128)S(1)}, u32[]{:S(2)}, u32[]{:S(2)}) collective-permute-start(f32[256,128]{1,0:T(8,128)S(1)} %get-tuple-element.70), channel_id=1, source_target_pairs={{0,2},{1,3},{2,4},{3,5},{4,6},{5,7},{6,8},{7,9},{8,10},{9,11},{10,... | collective-permute-start | bytes 393224 | tf_op jit(solution)/shard_map/ppermute | solution.py:36
  71.0 1.9 %collective-permute-start.10 = (f32[256,128]{1,0:T(8,128)S(1)}, f32[256,128]{1,0:T(8,128)S(1)}, u32[]{:S(2)}, u32[]{:S(2)}) collective-permute-start(f32[256,128]{1,0:T(8,128)S(1)} %get-tuple-element.66), channel_id=1, source_target_pairs={{0,1},{1,4},{2,3},{3,6},{4,5},{5,8},{6,7},{7,10},{8,9},{9,12},{10,... | collective-permute-start | bytes 393224 | tf_op jit(solution)/shard_map/ppermute | solution.py:36
  73.5 6.3 %collective-permute-start.16 = (f32[256,128]{1,0:T(8,128)S(1)}, f32[256,128]{1,0:T(8,128)S(1)}, u32[]{:S(2)}, u32[]{:S(2)}) collective-permute-start(f32[256,128]{1,0:T(8,128)S(1)} %get-tuple-element.85), channel_id=1, source_target_pairs={{7,0},{6,1},{9,2},{8,3},{11,4},{10,5},{13,6},{12,7},{15,8},{14,9},... | collective-permute-start | bytes 393224 | tf_op jit(solution)/shard_map/ppermute | solution.py:41
  79.8 0.6 terms_1_2.1
  80.4 1.9 %collective-permute-start.15 = (f32[256,128]{1,0:T(8,128)S(1)}, f32[256,128]{1,0:T(8,128)S(1)}, u32[]{:S(2)}, u32[]{:S(2)}) collective-permute-start(f32[256,128]{1,0:T(8,128)S(1)} %get-tuple-element.84), channel_id=1, source_target_pairs={{6,0},{7,1},{8,2},{9,3},{10,4},{11,5},{12,6},{13,7},{14,8},{15,9},... | collective-permute-start | bytes 393224 | tf_op jit(solution)/shard_map/ppermute | solution.py:41
  82.9 4.0 %collective-permute-start.14 = (f32[256,128]{1,0:T(8,128)S(1)}, f32[256,128]{1,0:T(8,128)S(1)}, u32[]{:S(2)}, u32[]{:S(2)}) collective-permute-start(f32[256,128]{1,0:T(8,128)S(1)} %get-tuple-element.83), channel_id=1, source_target_pairs={{5,0},{8,1},{7,2},{10,3},{9,4},{12,5},{11,6},{14,7},{13,8},{16,9},... | collective-permute-start | bytes 393224 | tf_op jit(solution)/shard_map/ppermute | solution.py:41
  86.9 1.4 %vertex_1.1 = f32[1024,128]{1,0:T(8,128)} custom-call(s32[32]{0:T(128)S(1)} %pad_add_fusion.1.meta_ref, f32[1024,128]{1,0:T(8,128)S(1)} %get-tuple-element.60.vert_ref, f32[256,128]{1,0:T(8,128)S(1)} %get-tuple-element.68.refs_0_, f32[256,128]{1,0:T(8,128)S(1)} %get-tuple-element.72.refs_1_, f32[256,128]{1,0:T(8,128)S(1)} %get-tuple-element.76.refs_2_, ...), custom_call_target="tpu_custom_call" | custom-call | flops 1000000000 | tf_op jit(solution)/shard_map/vertex_1/pallas_call | solution.py:81
  88.5 4.7 %collective-permute-done.15.refs_1_ = f32[256,128]{1,0:T(8,128)S(1)} collective-permute-done((f32[256,128]{1,0:T(8,128)S(1)}, f32[256,128]{1,0:T(8,128)S(1)}, u32[]{:S(2)}, u32[]{:S(2)}) %collective-permute-start.15) | collective-permute-done | bytes 131104 | tf_op jit(solution)/shard_map/ppermute | solution.py:41
  93.1 3.8 %collective-permute-done.14.refs_0_ = f32[256,128]{1,0:T(8,128)S(1)} collective-permute-done((f32[256,128]{1,0:T(8,128)S(1)}, f32[256,128]{1,0:T(8,128)S(1)}, u32[]{:S(2)}, u32[]{:S(2)}) %collective-permute-start.14) | collective-permute-done | bytes 131104 | tf_op jit(solution)/shard_map/ppermute | solution.py:41
  97.0 1.4 %last_context.1 = f32[1024,128]{1,0:T(8,128)} custom-call(s32[8]{0:T(128)S(1)} %fusion.notes_ref, f32[1032,128]{1,0:T(8,128)S(1)} %collective-permute-done.13.ctx_ref, f32[256,128]{1,0:T(8,128)S(1)} %collective-permute-done.14.refs_0_, f32[256,128]{1,0:T(8,128)S(1)} %collective-permute-done.15.refs_1_, f32[256,128]{1,0:T(8,128)S(1)} %collective-permute-done.16.refs_2_), custom_call_target="tpu_custom_call" | custom-call | flops 1000000000 | tf_op jit(solution)/shard_map/last_context/pallas_call | solution.py:81
  (32 shorter events, 4.9 us)
Async XLA Ops:
  0.6 0.7 copy-start.3
  1.4 18.8 %copy-start.2 = (s32[1,8]{1,0:T(1,128)S(1)}, s32[1,8]{1,0:T(1,128)}, u32[]{:S(2)}) copy-start(s32[1,8]{1,0:T(1,128)} %live_ref.1) | copy-start | bytes 100
  1.5 21.1 %copy-start = (f32[1024,128]{1,0:T(8,128)S(1)}, f32[1024,128]{1,0:T(8,128)}, u32[]{:S(2)}) copy-start(f32[1024,128]{1,0:T(8,128)} %ctx_ref.9) | copy-start | bytes 1572868
  1.5 25.7 %collective-permute-start = (s32[32]{0:T(128)S(1)}, s32[32]{0:T(128)S(1)}, u32[]{:S(2)}, u32[]{:S(2)}) collective-permute-start(s32[32]{0:T(128)S(1)} %pad_add_fusion.1.meta_ref), channel_id=1, source_target_pairs={{1,0},{4,1},{3,2},{6,3},{5,4},{8,5},{7,6},{10,7},{9,8},{12,9},{11,... | collective-permute-start | bytes 392 | tf_op jit(solution)/shard_map/ppermute | solution.py:41
  4.9 22.3 %collective-permute-start.1 = (s32[32]{0:T(128)S(1)}, s32[32]{0:T(128)S(1)}, u32[]{:S(2)}, u32[]{:S(2)}) collective-permute-start(s32[32]{0:T(128)S(1)} %pad_add_fusion.1.meta_ref), channel_id=1, source_target_pairs={{2,0},{3,1},{4,2},{5,3},{6,4},{7,5},{8,6},{9,7},{10,8},{11,9},{12,... | collective-permute-start | bytes 392 | tf_op jit(solution)/shard_map/ppermute | solution.py:41
  8.9 18.3 %collective-permute-start.2 = (s32[32]{0:T(128)S(1)}, s32[32]{0:T(128)S(1)}, u32[]{:S(2)}, u32[]{:S(2)}) collective-permute-start(s32[32]{0:T(128)S(1)} %pad_add_fusion.1.meta_ref), channel_id=1, source_target_pairs={{3,0},{2,1},{5,2},{4,3},{7,4},{6,5},{9,6},{8,7},{11,8},{10,9},{13,... | collective-permute-start | bytes 392 | tf_op jit(solution)/shard_map/ppermute | solution.py:41
  23.7 32.2 %collective-permute-start.6 = (f32[1024,128]{1,0:T(8,128)S(1)}, f32[1024,128]{1,0:T(8,128)S(1)}, u32[]{:S(2)}, u32[]{:S(2)}) collective-permute-start(f32[1024,128]{1,0:T(8,128)S(1)} %get-tuple-element.62), channel_id=1, source_target_pairs={{0,4},{1,5},{2,6},{3,7},{4,8},{5,9},{6,10},{7,11},{8,12},{9,13},{1... | collective-permute-start | bytes 1572872 | tf_op jit(solution)/shard_map/ppermute | solution.py:36
  27.8 9.9 %collective-permute-start.5 = (f32[256,128]{1,0:T(8,128)S(1)}, f32[256,128]{1,0:T(8,128)S(1)}, u32[]{:S(2)}, u32[]{:S(2)}) collective-permute-start(f32[256,128]{1,0:T(8,128)S(1)} %select_1.1), channel_id=1, source_target_pairs={{0,3},{1,2},{2,5},{3,4},{4,7},{5,6},{6,9},{7,8},{8,11},{9,10},{10,... | collective-permute-start | bytes 393224 | tf_op jit(solution)/shard_map/ppermute | solution.py:36
  30.2 14.1 %collective-permute-start.4 = (f32[256,128]{1,0:T(8,128)S(1)}, f32[256,128]{1,0:T(8,128)S(1)}, u32[]{:S(2)}, u32[]{:S(2)}) collective-permute-start(f32[256,128]{1,0:T(8,128)S(1)} %select_2.1), channel_id=1, source_target_pairs={{0,2},{1,3},{2,4},{3,5},{4,6},{5,7},{6,8},{7,9},{8,10},{9,11},{10,... | collective-permute-start | bytes 393224 | tf_op jit(solution)/shard_map/ppermute | solution.py:36
  33.4 13.5 %collective-permute-start.3 = (f32[256,128]{1,0:T(8,128)S(1)}, f32[256,128]{1,0:T(8,128)S(1)}, u32[]{:S(2)}, u32[]{:S(2)}) collective-permute-start(f32[256,128]{1,0:T(8,128)S(1)} %select_3.1), channel_id=1, source_target_pairs={{0,1},{1,4},{2,3},{3,6},{4,5},{5,8},{6,7},{7,10},{8,9},{9,12},{10,... | collective-permute-start | bytes 393224 | tf_op jit(solution)/shard_map/ppermute | solution.py:36
  38.3 12.7 %collective-permute-start.9 = (f32[264,128]{1,0:T(8,128)S(1)}, f32[264,128]{1,0:T(8,128)S(1)}, u32[]{:S(2)}, u32[]{:S(2)}) collective-permute-start(f32[264,128]{1,0:T(8,128)S(1)} %get-tuple-element.65), channel_id=1, source_target_pairs={{0,3},{1,2},{2,5},{3,4},{4,7},{5,6},{6,9},{7,8},{8,11},{9,10},{10,... | collective-permute-start | bytes 405512 | tf_op jit(solution)/shard_map/ppermute | solution.py:36
  44.9 9.9 %collective-permute-start.8 = (f32[264,128]{1,0:T(8,128)S(1)}, f32[264,128]{1,0:T(8,128)S(1)}, u32[]{:S(2)}, u32[]{:S(2)}) collective-permute-start(f32[264,128]{1,0:T(8,128)S(1)} %get-tuple-element.64), channel_id=1, source_target_pairs={{0,2},{1,3},{2,4},{3,5},{4,6},{5,7},{6,8},{7,9},{8,10},{9,11},{10,... | collective-permute-start | bytes 405512 | tf_op jit(solution)/shard_map/ppermute | solution.py:36
  46.9 3.3 %copy-start.1 = (f32[1024,128]{1,0:T(8,128)S(1)}, f32[1024,128]{1,0:T(8,128)}, u32[]{:S(2)}) copy-start(f32[1024,128]{1,0:T(8,128)} %vert_ref.3) | copy-start | bytes 1572868
  47.5 8.4 %collective-permute-start.7 = (f32[264,128]{1,0:T(8,128)S(1)}, f32[264,128]{1,0:T(8,128)S(1)}, u32[]{:S(2)}, u32[]{:S(2)}) collective-permute-start(f32[264,128]{1,0:T(8,128)S(1)} %get-tuple-element.63), channel_id=1, source_target_pairs={{0,1},{1,4},{2,3},{3,6},{4,5},{5,8},{6,7},{7,10},{8,9},{9,12},{10,... | collective-permute-start | bytes 405512 | tf_op jit(solution)/shard_map/ppermute | solution.py:36
  56.7 16.2 %collective-permute-start.12 = (f32[256,128]{1,0:T(8,128)S(1)}, f32[256,128]{1,0:T(8,128)S(1)}, u32[]{:S(2)}, u32[]{:S(2)}) collective-permute-start(f32[256,128]{1,0:T(8,128)S(1)} %get-tuple-element.74), channel_id=1, source_target_pairs={{0,3},{1,2},{2,5},{3,4},{4,7},{5,6},{6,9},{7,8},{8,11},{9,10},{10,... | collective-permute-start | bytes 393224 | tf_op jit(solution)/shard_map/ppermute | solution.py:36
  62.7 25.7 %collective-permute-start.13 = (f32[1032,128]{1,0:T(8,128)S(1)}, f32[1032,128]{1,0:T(8,128)S(1)}, u32[]{:S(2)}, u32[]{:S(2)}) collective-permute-start(f32[1032,128]{1,0:T(8,128)S(1)} %get-tuple-element.82), channel_id=1, source_target_pairs={{4,0},{5,1},{6,2},{7,3},{8,4},{9,5},{10,6},{11,7},{12,8},{13,9},{1... | collective-permute-start | bytes 1585160 | tf_op jit(solution)/shard_map/ppermute | solution.py:41
  69.0 10.8 %collective-permute-start.11 = (f32[256,128]{1,0:T(8,128)S(1)}, f32[256,128]{1,0:T(8,128)S(1)}, u32[]{:S(2)}, u32[]{:S(2)}) collective-permute-start(f32[256,128]{1,0:T(8,128)S(1)} %get-tuple-element.70), channel_id=1, source_target_pairs={{0,2},{1,3},{2,4},{3,5},{4,6},{5,7},{6,8},{7,9},{8,10},{9,11},{10,... | collective-permute-start | bytes 393224 | tf_op jit(solution)/shard_map/ppermute | solution.py:36
  71.0 11.4 %collective-permute-start.10 = (f32[256,128]{1,0:T(8,128)S(1)}, f32[256,128]{1,0:T(8,128)S(1)}, u32[]{:S(2)}, u32[]{:S(2)}) collective-permute-start(f32[256,128]{1,0:T(8,128)S(1)} %get-tuple-element.66), channel_id=1, source_target_pairs={{0,1},{1,4},{2,3},{3,6},{4,5},{5,8},{6,7},{7,10},{8,9},{9,12},{10,... | collective-permute-start | bytes 393224 | tf_op jit(solution)/shard_map/ppermute | solution.py:36
  73.5 15.0 %collective-permute-start.16 = (f32[256,128]{1,0:T(8,128)S(1)}, f32[256,128]{1,0:T(8,128)S(1)}, u32[]{:S(2)}, u32[]{:S(2)}) collective-permute-start(f32[256,128]{1,0:T(8,128)S(1)} %get-tuple-element.85), channel_id=1, source_target_pairs={{7,0},{6,1},{9,2},{8,3},{11,4},{10,5},{13,6},{12,7},{15,8},{14,9},... | collective-permute-start | bytes 393224 | tf_op jit(solution)/shard_map/ppermute | solution.py:41
  80.4 12.7 %collective-permute-start.15 = (f32[256,128]{1,0:T(8,128)S(1)}, f32[256,128]{1,0:T(8,128)S(1)}, u32[]{:S(2)}, u32[]{:S(2)}) collective-permute-start(f32[256,128]{1,0:T(8,128)S(1)} %get-tuple-element.84), channel_id=1, source_target_pairs={{6,0},{7,1},{8,2},{9,3},{10,4},{11,5},{12,6},{13,7},{14,8},{15,9},... | collective-permute-start | bytes 393224 | tf_op jit(solution)/shard_map/ppermute | solution.py:41
  82.9 14.0 %collective-permute-start.14 = (f32[256,128]{1,0:T(8,128)S(1)}, f32[256,128]{1,0:T(8,128)S(1)}, u32[]{:S(2)}, u32[]{:S(2)}) collective-permute-start(f32[256,128]{1,0:T(8,128)S(1)} %get-tuple-element.83), channel_id=1, source_target_pairs={{5,0},{8,1},{7,2},{10,3},{9,4},{12,5},{11,6},{14,7},{13,8},{16,9},... | collective-permute-start | bytes 393224 | tf_op jit(solution)/shard_map/ppermute | solution.py:41
